TPU v7x, 512 devices: a whole 4x8x8 slice. The times are simulated.
512 devices in a mesh: grp: 16 (over z, core), ep: 32 (over y, x).
Axes of the slice: x: 4, y: 8, z: 8, core: 2. Of those that a mesh axis runs over, the one named last changes fastest.
Arguments:
- tokens: bfloat16 [65536, 2048], P(('grp', 'ep')), may hold values from -6 to 6
- out_grad: bfloat16 [65536, 2048], P(('grp', 'ep')), may hold values from -1.5 to 1.5
- routes: int32 [65536, 2], P(('grp', 'ep')), may hold values from 0 to 15, as said below
- gates: bfloat16 [65536, 2], P(('grp', 'ep')), may hold values from 0.099609375 to 1
- w_gate_up: bfloat16 [32, 2048, 1024], P('ep', 'grp'), may hold values from -0.125 to 0.125
- w_down: bfloat16 [32, 2048, 512], P('ep', 'grp'), may hold values from -0.25 to 0.25
- plan: int32 [32], replicated, may hold values from 0 to 15, as said below
- failed: int32 [16, 32], replicated, may hold values from 0 to 1, as said below
Outputs:
- token_grad: bfloat16 [65536, 2048], P(('grp', 'ep'))
- gate_grad: bfloat16 [65536, 2], P(('grp', 'ep'))
- weight_grad: float32 [16, 2048, 1536], P(None, ('grp', 'ep'))
Inputs may be any that keep to these rules, and one draw needn't show every extreme that they name: `plan`: each expert is hosted by one or three slots. Each group has one to 4 failed slots, and every expert keeps a live replica in every group. A token names 2 different experts. Under the replica rule the routes of one device reach any slot at most 10 times, and in every group some slot receives exactly 10 routes from every device of the group.
All inputs are finite; a program needn't handle non-finite values.
Results may differ from a plain program's by a relative error of at most 0.0058.
Values may be sent and summed in bfloat16 or wider, within the bound.
No kernel may reach another device: no remote copies, remote signals or barrier semaphores. Data moves between devices by JAX's collectives and lax.ppermute only.
A program may use at most 128 MiB of HBM per device.

v0:
```python
import jax
import jax.numpy as jnp
from jax import lax
from jax.sharding import PartitionSpec as P


def assign(route_ids, hosting, in_service, capacity, experts):
    route_count = route_ids.shape[0] * route_ids.shape[1]
    slot_count = hosting.shape[0]
    flat_routes = route_ids.reshape(route_count)
    expert_ids = jnp.arange(experts, dtype=jnp.int32)
    hosted = ((hosting[None, :] == expert_ids[:, None]) & (in_service[None, :] > 0)).astype(
        jnp.int32
    )
    replicas = jnp.sum(hosted, axis=1)
    ordinal = jnp.sum(hosted * (jnp.cumsum(hosted, axis=1) - 1), axis=0)
    expert_hot = (flat_routes[:, None] == expert_ids[None, :]).astype(jnp.int32)
    expert_rank = jnp.sum(expert_hot * (jnp.cumsum(expert_hot, axis=0) - 1), axis=1)
    route_replicas = jnp.sum(expert_hot * replicas[None, :], axis=1)
    replica_pick = expert_rank % route_replicas
    slot_hot = (
        (hosting[None, :] == flat_routes[:, None])
        & (in_service[None, :] > 0)
        & (ordinal[None, :] == replica_pick[:, None])
    ).astype(jnp.int32)
    slot_rank = jnp.sum(slot_hot * (jnp.cumsum(slot_hot, axis=0) - 1), axis=1)
    slot_index = jnp.sum(slot_hot * jnp.arange(slot_count, dtype=jnp.int32)[None, :], axis=1)
    return slot_index * capacity + slot_rank


def expert_rows(rows_x, rows_dy, rows_gate, full_gu, full_dn):
    hidden_width = full_dn.shape[1]
    projected = jnp.dot(rows_x, full_gu, preferred_element_type=jnp.float32)
    gate_pre = projected[:, :hidden_width]
    up_pre = projected[:, hidden_width:]
    sigmoid_a = jax.nn.sigmoid(gate_pre)
    silu_a = gate_pre * sigmoid_a
    hidden = (silu_a * up_pre).astype(jnp.bfloat16)
    upstream = jnp.dot(rows_dy, full_dn, preferred_element_type=jnp.float32)
    rebuilt = lax.dot_general(
        hidden, full_dn, (((1,), (1,)), ((), ())), preferred_element_type=jnp.float32
    )
    gate_grad = jnp.sum(rows_dy.astype(jnp.float32) * rebuilt, axis=1).astype(jnp.bfloat16)
    gate_value = rows_gate.astype(jnp.float32)[:, None]
    hidden_grad = gate_value * upstream
    gate_delta = hidden_grad * up_pre * sigmoid_a * (1.0 + gate_pre * (1.0 - sigmoid_a))
    up_delta = hidden_grad * silu_a
    pre_grad = jnp.concatenate([gate_delta, up_delta], axis=1).astype(jnp.bfloat16)
    row_grad = lax.dot_general(
        pre_grad, full_gu, (((1,), (1,)), ((), ())), preferred_element_type=jnp.float32
    ).astype(jnp.bfloat16)
    gated_hidden = (gate_value * hidden.astype(jnp.float32)).astype(jnp.bfloat16)
    grad_gu = lax.dot_general(
        rows_x, pre_grad, (((0,), (0,)), ((), ())), preferred_element_type=jnp.float32
    )
    grad_dn = lax.dot_general(
        rows_dy, gated_hidden, (((0,), (0,)), ((), ())), preferred_element_type=jnp.float32
    )
    return (row_grad, gate_grad, grad_gu, grad_dn)


def local(tokens, out_grad, routes, gates, w_gate_up, w_down, plan, failed):
    groups = lax.axis_size("grp")
    slot_count = lax.axis_size("ep")
    my_group = lax.axis_index("grp")
    tok_count, model_width = tokens.shape
    topk_count = routes.shape[1]
    experts = slot_count // 2
    capacity = tok_count * topk_count * 5 // (4 * slot_count)
    route_count = tok_count * topk_count
    buffer_rows = slot_count * capacity
    in_service = 1 - lax.dynamic_index_in_dim(failed, my_group, 0, keepdims=False)
    positions = assign(routes, plan, in_service, capacity, experts)
    source = (
        jnp.full((buffer_rows,), route_count, jnp.int32)
        .at[positions]
        .set(jnp.arange(route_count, dtype=jnp.int32))
    )
    token_of = source // topk_count
    zero_row = jnp.zeros((1, model_width), jnp.bfloat16)
    send_x = jnp.concatenate([tokens, zero_row], axis=0)[token_of].reshape(
        slot_count, capacity, model_width
    )
    send_dy = jnp.concatenate([out_grad, zero_row], axis=0)[token_of].reshape(
        slot_count, capacity, model_width
    )
    send_gate = jnp.concatenate([gates.reshape(route_count), jnp.zeros((1,), jnp.bfloat16)])[source]
    send_gate = send_gate.reshape(slot_count, capacity)
    recv_x, recv_dy, recv_gate = (
        lax.all_to_all(send_x, "ep", split_axis=0, concat_axis=0, tiled=True),
        lax.all_to_all(send_dy, "ep", split_axis=0, concat_axis=0, tiled=True),
        lax.all_to_all(send_gate, "ep", split_axis=0, concat_axis=0, tiled=True),
    )
    full_gu, full_dn = (
        lax.all_gather(w_gate_up, "grp", axis=1, tiled=True),
        lax.all_gather(w_down, "grp", axis=1, tiled=True),
    )
    full_gu = full_gu[0]
    full_dn = full_dn[0]
    hidden_width = full_dn.shape[1]
    flat_x = recv_x.reshape(buffer_rows, model_width)
    flat_dy = recv_dy.reshape(buffer_rows, model_width)
    flat_gate = recv_gate.reshape(buffer_rows)
    row_grads, gate_rows, grad_gu, grad_dn = expert_rows(
        flat_x, flat_dy, flat_gate, full_gu, full_dn
    )
    back_x, back_gate = (
        lax.all_to_all(
            row_grads.reshape(slot_count, capacity, model_width),
            "ep",
            split_axis=0,
            concat_axis=0,
            tiled=True,
        ),
        lax.all_to_all(
            gate_rows.reshape(slot_count, capacity), "ep", split_axis=0, concat_axis=0, tiled=True
        ),
    )
    route_rows = back_x.reshape(buffer_rows, model_width)[positions]
    token_grad = jnp.sum(
        route_rows.reshape(tok_count, topk_count, model_width).astype(jnp.float32), axis=1
    ).astype(jnp.bfloat16)
    gate_grad = back_gate.reshape(buffer_rows)[positions].reshape(tok_count, topk_count)
    columns = 3 * hidden_width
    rows_each = model_width // (groups * slot_count)
    slot_grad = jnp.concatenate([grad_gu, grad_dn], axis=1).astype(jnp.bfloat16)
    slot_grad = slot_grad.reshape(groups, slot_count, rows_each, columns)
    expert_ids = jnp.arange(experts, dtype=jnp.int32)
    mixed = lax.all_to_all(
        lax.all_to_all(slot_grad, "grp", split_axis=0, concat_axis=0, tiled=True),
        "ep",
        split_axis=1,
        concat_axis=1,
        tiled=True,
    )
    hosted_all = (
        (plan[None, None, :] == expert_ids[None, :, None]) & (failed[:, None, :] == 0)
    ).astype(jnp.bfloat16)
    per_group = jnp.einsum("ges,gsrc->gerc", hosted_all, mixed, preferred_element_type=jnp.float32)
    weight_grad = jnp.sum(per_group, axis=0) / groups
    return (token_grad, gate_grad, weight_grad)


def solution(mesh):
    placed = (
        P(("grp", "ep"), None),
        P(("grp", "ep"), None),
        P(("grp", "ep"), None),
        P(("grp", "ep"), None),
        P("ep", "grp", None),
        P("ep", "grp", None),
        P(),
        P(),
    )
    return jax.shard_map(
        local,
        mesh=mesh,
        in_specs=placed,
        out_specs=(P(("grp", "ep"), None), P(("grp", "ep"), None), P(None, ("grp", "ep"), None)),
        check_vma=False,
    )
```

profile of v0, /device:TPU:94, one launch (start us, length us, event | category | flops | bytes accessed | tf_op | source)
XLA Modules:
  0.0 556.9 jit_solution(9209337866441861698)
XLA Ops:
  15.8 1.4 scatter_custom_fusion
  17.2 2.5 gather_fusion
  20.4 9.9 %all-to-all-start = ((bf16[32,1,10]{2,1,0:T(2,128)(2,1)}), bf16[32,1,10]{2,1,0:T(2,128)(2,1)S(1)}, u32[]{:S(2)}, u32[]{:S(2)}) async-start(bf16[32,1,10]{2,1,0:T(2,128)(2,1)} %all_to_all.33), calls=%async_computation | async-start | bytes 32768 | tf_op jit(solution)/shard_map/all_to_all | solution.py:92
  30.4 2.4 gather_fusion.1
  32.8 1.6 reshape.198
  35.6 8.7 %all-to-all-start.1 = ((bf16[32,10,2048]{2,1,0:T(8,128)(2,1)}), bf16[32,10,2048]{2,1,0:T(8,128)(2,1)S(1)}, u32[]{:S(2)}, u32[]{:S(2)}) async-start(bf16[32,10,2048]{2,1,0:T(8,128)(2,1)} %reshape.198), calls=%async_computation.1 | async-start | bytes 4194304 | tf_op jit(solution)/shard_map/all_to_all | solution.py:91
  45.1 3.0 gather_fusion.2
  48.1 3.3 reshape.200
  51.5 39.8 %all-to-all-done.1 = bf16[32,10,2048]{2,1,0:T(8,128)(2,1)S(1)} async-done(((bf16[32,10,2048]{2,1,0:T(8,128)(2,1)}), bf16[32,10,2048]{2,1,0:T(8,128)(2,1)S(1)}, u32[]{:S(2)}, u32[]{:S(2)}) %all-to-all-start.1) | async-done | bytes 1310752 | tf_op jit(solution)/shard_map/all_to_all | solution.py:91
  91.3 8.6 %all-to-all-start.2 = ((bf16[32,10,2048]{2,1,0:T(8,128)(2,1)}), bf16[32,10,2048]{2,1,0:T(8,128)(2,1)}, u32[]{:S(2)}, u32[]{:S(2)}) async-start(bf16[32,10,2048]{2,1,0:T(8,128)(2,1)} %reshape.200), calls=%async_computation.2 | async-start | bytes 4194304 | tf_op jit(solution)/shard_map/all_to_all | solution.py:90
  102.8 43.1 %all-to-all-done.2 = bf16[32,10,2048]{2,1,0:T(8,128)(2,1)} async-done(((bf16[32,10,2048]{2,1,0:T(8,128)(2,1)}), bf16[32,10,2048]{2,1,0:T(8,128)(2,1)}, u32[]{:S(2)}, u32[]{:S(2)}) %all-to-all-start.2) | async-done | bytes 1310752 | tf_op jit(solution)/shard_map/all_to_all | solution.py:90
  145.9 3.6 reshape.201
  149.6 1.8 copy.28
  152.8 4.1 fusion.4
  156.9 3.6 multiply_convert_fusion.3
  162.3 8.6 %all-to-all-start.4 = ((bf16[32,1,10]{2,1,0:T(2,128)(2,1)}), bf16[32,1,10]{2,1,0:T(2,128)(2,1)S(1)}, u32[]{:S(2)}, u32[]{:S(2)}) async-start(bf16[32,1,10]{2,1,0:T(2,128)(2,1)} %convert_element_type.71), calls=%async_computation.4 | async-start | bytes 32768 | tf_op jit(solution)/shard_map/all_to_all | solution.py:115
  171.0 2.9 convolution_convert_fusion.1
  173.9 4.3 convolution_convert_fusion
  178.2 3.0 pad_maximum_fusion
  181.2 3.1 copy.32
  184.3 10.0 %all-to-all-start.5 = ((bf16[16,32,4,1536]{3,1,2,0:T(8,128)(2,1)}), bf16[16,32,4,1536]{3,1,2,0:T(8,128)(2,1)}, u32[]{:S(2)}, u32[]{:S(2)}) async-start(bf16[16,32,4,1536]{3,1,2,0:T(8,128)(2,1)} %copy.32), calls=%async_computation.5 | async-start | bytes 12582912 | tf_op jit(solution)/shard_map/all_to_all | solution.py:130
  194.3 3.7 fusion.6
  198.0 1.6 reshape.202
  199.6 132.1 %all-to-all-done.5 = bf16[16,32,4,1536]{3,1,2,0:T(8,128)(2,1)} async-done(((bf16[16,32,4,1536]{3,1,2,0:T(8,128)(2,1)}), bf16[16,32,4,1536]{3,1,2,0:T(8,128)(2,1)}, u32[]{:S(2)}, u32[]{:S(2)}) %all-to-all-start.5) | async-done | bytes 6291488 | tf_op jit(solution)/shard_map/all_to_all | solution.py:130
  331.7 9.8 %all-to-all-start.3 = ((bf16[32,10,2048]{2,1,0:T(8,128)(2,1)}), bf16[32,10,2048]{2,1,0:T(8,128)(2,1)S(1)}, u32[]{:S(2)}, u32[]{:S(2)}) async-start(bf16[32,10,2048]{2,1,0:T(8,128)(2,1)} %reshape.202), calls=%async_computation.3 | async-start | bytes 4194304 | tf_op jit(solution)/shard_map/all_to_all | solution.py:108
  341.5 8.9 %copy.33 = bf16[16,32,4,1536]{3,0,2,1:T(8,128)(2,1)} copy(bf16[16,32,4,1536]{3,1,2,0:T(8,128)(2,1)} %all-to-all-done.5) | data formatting | bytes 12582912 | tf_op jit(solution)/shard_map/all_to_all | solution.py:130
  350.4 38.9 %all-to-all-done.3 = bf16[32,10,2048]{2,1,0:T(8,128)(2,1)S(1)} async-done(((bf16[32,10,2048]{2,1,0:T(8,128)(2,1)}), bf16[32,10,2048]{2,1,0:T(8,128)(2,1)S(1)}, u32[]{:S(2)}, u32[]{:S(2)}) %all-to-all-start.3) | async-done | bytes 1310752 | tf_op jit(solution)/shard_map/all_to_all | solution.py:108
  389.2 8.3 %all-to-all-start.6 = ((bf16[16,32,4,1536]{3,0,2,1:T(8,128)(2,1)}), bf16[16,32,4,1536]{3,0,2,1:T(8,128)(2,1)}, u32[]{:S(2)}, u32[]{:S(2)}) async-start(bf16[16,32,4,1536]{3,0,2,1:T(8,128)(2,1)} %copy.33), calls=%async_computation.6 | async-start | bytes 12582912 | tf_op jit(solution)/shard_map/all_to_all | solution.py:129
  397.7 1.9 gather_fusion.4
  403.0 3.6 reduce_sum.91
  406.6 136.2 %all-to-all-done.6 = bf16[16,32,4,1536]{3,0,2,1:T(8,128)(2,1)} async-done(((bf16[16,32,4,1536]{3,0,2,1:T(8,128)(2,1)}), bf16[16,32,4,1536]{3,0,2,1:T(8,128)(2,1)}, u32[]{:S(2)}, u32[]{:S(2)}) %all-to-all-start.6) | async-done | bytes 6291488 | tf_op jit(solution)/shard_map/all_to_all | solution.py:129
  542.9 6.2 %fusion.12 = f32[16,4,1536]{2,0,1:T(8,128)S(1)} fusion(bf16[16,32,4,1536]{3,0,2,1:T(8,128)(2,1)} %all-to-all-done.6, pred[16,32]{1,0:T(8,128)(4,1)S(1)} %broadcast_compare_fusion, pred[16,32]{1,0:T(8,128)(4,1)S(1)} %get-tuple-element.23), kind=kOutput, calls=%fused_computation.17 | convolution fusion | flops 100769792 | bytes 6685696 | tf_op jit(solution)/shard_map/ges,gsrc->gerc/dot_general | solution.py:139
  (74 shorter events, 21.9 us)
Async XLA Ops:
  7.2 23.1 %copy-start.1 = (bf16[128,2048]{1,0:T(8,128)(2,1)S(1)}, bf16[128,2048]{1,0:T(8,128)(2,1)}, u32[]{:S(2)}) copy-start(bf16[128,2048]{1,0:T(8,128)(2,1)} %param.9) | copy-start | bytes 1572868
  7.2 145.6 %all-gather.5.cloned.1.call-start = ((), (), s32[]{:S(2)}) async-start(), calls=%async_computation.8 | async-start | bytes 4456448 | tf_op jit(solution)/shard_map/all_gather | solution.py:95
  20.4 15.1 %all-to-all-start = ((bf16[32,1,10]{2,1,0:T(2,128)(2,1)}), bf16[32,1,10]{2,1,0:T(2,128)(2,1)S(1)}, u32[]{:S(2)}, u32[]{:S(2)}) async-start(bf16[32,1,10]{2,1,0:T(2,128)(2,1)} %all_to_all.33), calls=%async_computation | async-start | bytes 32768 | tf_op jit(solution)/shard_map/all_to_all | solution.py:92
  34.4 10.7 %copy-start.2 = (bf16[128,2048]{1,0:T(8,128)(2,1)S(1)}, bf16[128,2048]{1,0:T(8,128)(2,1)}, u32[]{:S(2)}) copy-start(bf16[128,2048]{1,0:T(8,128)(2,1)} %param.8) | copy-start | bytes 1572868
  35.6 55.8 %all-to-all-start.1 = ((bf16[32,10,2048]{2,1,0:T(8,128)(2,1)}), bf16[32,10,2048]{2,1,0:T(8,128)(2,1)S(1)}, u32[]{:S(2)}, u32[]{:S(2)}) async-start(bf16[32,10,2048]{2,1,0:T(8,128)(2,1)} %reshape.198), calls=%async_computation.1 | async-start | bytes 4194304 | tf_op jit(solution)/shard_map/all_to_all | solution.py:91
  44.3 112.6 %all-gather.3.cloned.1.call-start = ((), (), s32[]{:S(2)}) async-start(), calls=%async_computation.7 | async-start | bytes 2228224 | tf_op jit(solution)/shard_map/all_gather | solution.py:96
  91.3 54.6 %all-to-all-start.2 = ((bf16[32,10,2048]{2,1,0:T(8,128)(2,1)}), bf16[32,10,2048]{2,1,0:T(8,128)(2,1)}, u32[]{:S(2)}, u32[]{:S(2)}) async-start(bf16[32,10,2048]{2,1,0:T(8,128)(2,1)} %reshape.200), calls=%async_computation.2 | async-start | bytes 4194304 | tf_op jit(solution)/shard_map/all_to_all | solution.py:90
  156.9 3.6 copy-start.4
  160.6 1.0 copy-start.5
  162.3 22.0 %all-to-all-start.4 = ((bf16[32,1,10]{2,1,0:T(2,128)(2,1)}), bf16[32,1,10]{2,1,0:T(2,128)(2,1)S(1)}, u32[]{:S(2)}, u32[]{:S(2)}) async-start(bf16[32,1,10]{2,1,0:T(2,128)(2,1)} %convert_element_type.71), calls=%async_computation.4 | async-start | bytes 32768 | tf_op jit(solution)/shard_map/all_to_all | solution.py:115
  170.9 3.0 copy-start
  171.0 3.0 copy-start.6
  171.0 3.0 copy-start.7
  184.3 147.4 %all-to-all-start.5 = ((bf16[16,32,4,1536]{3,1,2,0:T(8,128)(2,1)}), bf16[16,32,4,1536]{3,1,2,0:T(8,128)(2,1)}, u32[]{:S(2)}, u32[]{:S(2)}) async-start(bf16[16,32,4,1536]{3,1,2,0:T(8,128)(2,1)} %copy.32), calls=%async_computation.5 | async-start | bytes 12582912 | tf_op jit(solution)/shard_map/all_to_all | solution.py:130
  331.7 57.6 %all-to-all-start.3 = ((bf16[32,10,2048]{2,1,0:T(8,128)(2,1)}), bf16[32,10,2048]{2,1,0:T(8,128)(2,1)S(1)}, u32[]{:S(2)}, u32[]{:S(2)}) async-start(bf16[32,10,2048]{2,1,0:T(8,128)(2,1)} %reshape.202), calls=%async_computation.3 | async-start | bytes 4194304 | tf_op jit(solution)/shard_map/all_to_all | solution.py:108
  350.4 47.2 %copy-start.3 = (s32[16,32]{1,0:T(8,128)S(1)}, s32[16,32]{1,0:T(8,128)}, u32[]{:S(2)}) copy-start(s32[16,32]{1,0:T(8,128)} %param.15) | copy-start | bytes 6148
  389.2 153.6 %all-to-all-start.6 = ((bf16[16,32,4,1536]{3,0,2,1:T(8,128)(2,1)}), bf16[16,32,4,1536]{3,0,2,1:T(8,128)(2,1)}, u32[]{:S(2)}, u32[]{:S(2)}) async-start(bf16[16,32,4,1536]{3,0,2,1:T(8,128)(2,1)} %copy.33), calls=%async_computation.6 | async-start | bytes 12582912 | tf_op jit(solution)/shard_map/all_to_all | solution.py:129
Sparse Core Ops, SparseCore 0:
  10.1 48.5 all-gather.4
  60.8 41.0 all-gather.2
where the time goes:
time: 558 us; the launch traced here: 557 us
  waiting for transfers between devices  393 us (70%)
  starting transfers between devices  63.9 us (11%)
  local copies, waits for them, and re-layouts  47.8 us (9%)
  matrix products  25.9 us (5%)
  between operations  14.4 us (3%)
  other arithmetic  12.2 us (2%)
    all_to_all x1, waiting for transfers between devices, local(): lax.all_to_all(lax.all_to_all(slot_grad, 'grp', split_axis=0, concat_axis...  136 us
    all_to_all x1, waiting for transfers between devices, local(): lax.all_to_all(slot_grad, 'grp', split_axis=0, concat_axis=0, tiled=True)  132 us
    all_to_all x1, waiting for transfers between devices, local(): lax.all_to_all(send_x, 'ep', split_axis=0, concat_axis=0, tiled=True)  43.1 us
    all_to_all x1, waiting for transfers between devices, local(): lax.all_to_all(send_dy, 'ep', split_axis=0, concat_axis=0, tiled=True)  39.8 us
    all_to_all x1, waiting for transfers between devices, local(): lax.all_to_all(row_grads.reshape(slot_count, capacity, model_width), 'ep'...  38.9 us
  transfers between devices with their start and end apart: 9, of which 6 were waited for; matrix products, arithmetic and copies ran while one was open for 13% of the time, Pallas kernels for 0%

commit v1 on v0

v1 whole, which is shorter than its diff:
```python
import functools

import jax
import jax.numpy as jnp
from jax import lax
from jax.experimental import pallas as pl
from jax.experimental.pallas import tpu as pltpu
from jax.sharding import PartitionSpec as P

BF = jnp.bfloat16
F32 = jnp.float32
LANES = 128
MAIN = 8
VMEM_BYTES = 56 * 2**20
TN = (((0,), (0,)), ((), ()))
NT = (((1,), (1,)), ((), ()))


def mm(a, b, dims=(((1,), (0,)), ((), ()))):
    return lax.dot_general(a, b, dims, preferred_element_type=F32)


def iota(shape, dim):
    return lax.broadcasted_iota(jnp.int32, shape, dim)


def one_hot(cond):
    return jnp.where(cond, 1.0, 0.0).astype(BF)


def call(kernel, outs, name, **kw):
    return pl.pallas_call(
        kernel,
        out_shape=outs,
        name=name,
        compiler_params=pltpu.CompilerParams(vmem_limit_bytes=VMEM_BYTES),
        **kw,
    )


def pack_kernel(group, routes, gates, plan, failed, tokens, grads, sent, places):
    tok_count, width = tokens.shape
    slots = plan.shape[1]
    half = width // 2
    rows = slots * MAIN
    in_group = iota(failed.shape, 0) == group[0]
    dead = jnp.sum(jnp.where(in_group, failed[...], 0), axis=0, keepdims=True)
    slot_ids = iota((tok_count, slots), 1).astype(F32)
    before_slot = one_hot(iota((slots, slots), 0) < iota((slots, slots), 1))
    before_tok = one_hot(iota((tok_count, tok_count), 1) < iota((tok_count, tok_count), 0))
    experts = iota((tok_count, LANES), 1)
    ids = [routes[:, k : k + 1] for k in range(2)]
    hot = [jnp.where(experts == i, 1.0, 0.0) for i in ids]
    prefix = mm(before_tok, (hot[0] + hot[1]).astype(BF))
    rank = [
        jnp.sum(hot[0] * prefix, axis=1, keepdims=True),
        jnp.sum(hot[1] * (prefix + hot[0]), axis=1, keepdims=True),
    ]
    chosen = []
    for k in range(2):
        cand = jnp.where((plan[...] == ids[k]) & (dead == 0), 1.0, 0.0)
        ordinal = mm(cand.astype(BF), before_slot)
        count = jnp.maximum(jnp.sum(cand, axis=1, keepdims=True), 1.0)
        pick = rank[k] - count * jnp.floor((rank[k] + 0.5) / count)
        chosen.append(jnp.where(ordinal == pick, cand, 0.0))
    prefix = mm(before_tok, (chosen[0] + chosen[1]).astype(BF))
    position = [
        jnp.sum(chosen[0] * prefix, axis=1, keepdims=True),
        jnp.sum(chosen[1] * (prefix + chosen[0]), axis=1, keepdims=True),
    ]
    row_ids = iota((tok_count, rows), 1)
    lane = iota((tok_count, LANES), 1)
    main, rest, noted = [], [], jnp.zeros((tok_count, LANES), jnp.int32)
    for k in range(2):
        slot = jnp.sum(chosen[k] * slot_ids, axis=1, keepdims=True).astype(jnp.int32)
        pos = position[k].astype(jnp.int32)
        main.append(jnp.where(pos < MAIN, slot * MAIN + pos, -64))
        rest.append(jnp.where(pos < MAIN, -64, slot * MAIN + pos - MAIN))
        noted = jnp.where(lane == k, main[k], noted)
        noted = jnp.where(lane == 2 + k, rest[k], noted)
    places[...] = noted

    def pick_rows(at, shift=0):
        return one_hot((at[0] + shift == row_ids) | (at[1] + shift == row_ids))

    whole = pick_rows(main)
    sent[:, :width] = mm(whole, tokens[...], TN).astype(BF)
    sent[:, width : 2 * width] = mm(whole, grads[...], TN).astype(BF)
    cut = mm(pick_rows(rest), tokens[:, :half], TN)
    cut += mm(pick_rows(rest, 4), tokens[:, half:], TN)
    cut += mm(pick_rows(rest, 2), grads[:, :half], TN)
    cut += mm(pick_rows(rest, 6), grads[:, half:], TN)
    sent[:, 2 * width : 2 * width + half] = cut.astype(BF)
    gate_rows = jnp.zeros((rows, LANES), F32)
    for k in range(2):
        gate = jnp.broadcast_to(gates[:, k : k + 1].astype(F32), (tok_count, LANES))
        first = jnp.where(lane == 0, gate, 0.0).astype(BF)
        second = jnp.where(lane == 1, gate, 0.0).astype(BF)
        gate_rows += mm(one_hot(main[k] == row_ids), first, TN)
        gate_rows += mm(one_hot(rest[k] == row_ids), second, TN)
    sent[:, 2 * width + half :] = gate_rows.astype(BF)


def slot_kernel(got, weights, slot_grad, pre_out, gate_out, x_all, dy_all):
    rows = got.shape[0]
    width = weights.shape[0]
    hidden_width = weights.shape[1] // 3
    half = width // 2
    extra = rows // MAIN * 2
    source = iota((extra, rows), 0)
    base = source // 2 * MAIN + source % 2
    column = iota((extra, rows), 1)
    cut = got[:, 2 * width : 2 * width + half]
    first = one_hot(column == base)
    x_all[:rows] = got[:, :width]
    dy_all[:rows] = got[:, width : 2 * width]
    x_all[rows:, :half] = mm(first, cut).astype(BF)
    x_all[rows:, half:] = mm(one_hot(column == base + 4), cut).astype(BF)
    dy_all[rows:, :half] = mm(one_hot(column == base + 2), cut).astype(BF)
    dy_all[rows:, half:] = mm(one_hot(column == base + 6), cut).astype(BF)
    gate_block = got[:, 2 * width + half :]
    gate = jnp.concatenate(
        [gate_block[:, 0:1].astype(F32), mm(first, gate_block)[:, 1:2]], axis=0
    )
    pre = mm(x_all[...], weights[:, : 2 * hidden_width])
    a = pre[:, :hidden_width]
    b = pre[:, hidden_width:]
    sig = jax.nn.sigmoid(a)
    silu = a * sig
    hidden = (silu * b).astype(BF)
    hidden32 = hidden.astype(F32)
    upstream = mm(dy_all[...], weights[:, 2 * hidden_width :])
    gate_grad = jnp.sum(upstream * hidden32, axis=1, keepdims=True)
    gate_out[...] = jnp.broadcast_to(gate_grad, gate_out.shape).astype(BF)
    hidden_grad = gate * upstream
    pre_out[:, :hidden_width] = (hidden_grad * b * sig * (1.0 + a * (1.0 - sig))).astype(BF)
    pre_out[:, hidden_width:] = (hidden_grad * silu).astype(BF)
    gated = (gate * hidden32).astype(BF)
    step = 256
    for d in range(0, width, step):
        grad = mm(x_all[:, d : d + step], pre_out[...], TN)
        slot_grad[d : d + step, : 2 * hidden_width] = grad.astype(BF)
        grad = mm(dy_all[:, d : d + step], gated, TN)
        slot_grad[d : d + step, 2 * hidden_width :] = grad.astype(BF)


def back_kernel(pre_grad, gate_grad, weights, back):
    total, columns = pre_grad.shape
    width = weights.shape[0]
    rows = back.shape[0]
    extra = total - rows
    quarter = width // 4
    row = iota((rows, extra), 0)
    column = iota((rows, extra), 1)
    target = row // MAIN * 2 + row % 2
    part = row % MAIN // 2
    cut = jnp.zeros((rows, quarter), F32)
    for h in range(4):
        cols = slice(h * quarter, (h + 1) * quarter)
        grad = mm(pre_grad[...], weights[cols, :columns], NT).astype(BF)
        back[:, cols] = grad[:rows]
        cut += mm(one_hot((column == target) & (part == h)), grad[rows:])
    back[:, width : width + quarter] = cut.astype(BF)
    lane = iota((rows, LANES), 1)
    spread = mm(one_hot((column == target) & (part == 0)), gate_grad[rows:])
    gate_rows = jnp.where(lane == 0, gate_grad[:rows].astype(F32), spread)
    back[:, width + quarter :] = jnp.where(lane < 2, gate_rows, 0.0).astype(BF)


def join_kernel(back, places, token_grad, gate_grad):
    tok_count, width = token_grad.shape
    rows = back.shape[0]
    quarter = width // 4
    row_ids = iota((tok_count, rows), 1)
    main = [places[:, k : k + 1] for k in range(2)]
    rest = [places[:, 2 + k : 3 + k] for k in range(2)]
    whole = one_hot((main[0] == row_ids) | (main[1] == row_ids))
    cut = back[:, width : width + quarter]
    for h in range(4):
        cols = slice(h * quarter, (h + 1) * quarter)
        here = one_hot((rest[0] + 2 * h == row_ids) | (rest[1] + 2 * h == row_ids))
        token_grad[:, cols] = (mm(whole, back[:, cols]) + mm(here, cut)).astype(BF)
    gate_rows = back[:, width + quarter :]
    for k in range(2):
        value = mm(one_hot(main[k] == row_ids), gate_rows)[:, 0:1]
        value += mm(one_hot(rest[k] == row_ids), gate_rows)[:, 1:2]
        gate_grad[:, k : k + 1] = value.astype(BF)


def expert_kernel(groups, plan, mixed, out):
    out[...] = jnp.zeros_like(out)
    for s in range(mixed.shape[0]):
        e = plan[s]
        out[e] += mixed[s].astype(F32)
    out[...] = out[...] * (1.0 / groups)


def local(tokens, out_grad, routes, gates, w_gate_up, w_down, plan, failed):
    groups = lax.axis_size("grp")
    slots = lax.axis_size("ep")
    tok_count, width = tokens.shape
    hidden_width = w_down.shape[2]
    experts = slots // 2
    rows = slots * MAIN
    total = slots * (MAIN + 2)
    smem = pl.BlockSpec(memory_space=pltpu.SMEM)
    vmem = pl.BlockSpec(memory_space=pltpu.VMEM)
    weights = jnp.concatenate([w_gate_up[0], w_down[0]], axis=1)
    weights = lax.all_gather(weights, "grp", axis=0, tiled=True)
    sent, places = call(
        pack_kernel,
        (
            jax.ShapeDtypeStruct((rows, 2 * width + width // 2 + LANES), BF),
            jax.ShapeDtypeStruct((tok_count, LANES), jnp.int32),
        ),
        "pack",
        in_specs=[smem] + [vmem] * 6,
    )(
        lax.axis_index("grp").reshape(1),
        routes,
        gates,
        plan.reshape(1, slots),
        failed,
        tokens,
        out_grad,
    )
    got = lax.all_to_all(sent, "ep", split_axis=0, concat_axis=0, tiled=True)
    slot_grad, pre_grad, gate_rows = call(
        slot_kernel,
        (
            jax.ShapeDtypeStruct((width, 3 * hidden_width), BF),
            jax.ShapeDtypeStruct((total, 2 * hidden_width), BF),
            jax.ShapeDtypeStruct((total, LANES), BF),
        ),
        "slot",
        scratch_shapes=[pltpu.VMEM((total, width), BF)] * 2,
    )(got, weights)
    owned = lax.psum_scatter(slot_grad, "grp", scatter_dimension=0, tiled=True)
    back = call(
        back_kernel,
        jax.ShapeDtypeStruct((rows, width + width // 4 + LANES), BF),
        "back",
    )(pre_grad, gate_rows, weights)
    back = lax.all_to_all(back, "ep", split_axis=0, concat_axis=0, tiled=True)
    token_grad, gate_grad = call(
        join_kernel,
        (
            jax.ShapeDtypeStruct((tok_count, width), BF),
            jax.ShapeDtypeStruct((tok_count, 2), BF),
        ),
        "join",
    )(back, places)
    each = owned.shape[0] // slots
    owned = owned.reshape(slots, each, 3 * hidden_width)
    mixed = lax.all_to_all(owned, "ep", split_axis=0, concat_axis=0, tiled=True)
    weight_grad = call(
        functools.partial(expert_kernel, groups),
        jax.ShapeDtypeStruct((experts, each, 3 * hidden_width), F32),
        "experts",
        in_specs=[smem, vmem],
    )(plan, mixed)
    return token_grad, gate_grad, weight_grad


def solution(mesh):
    placed = (
        P(("grp", "ep"), None),
        P(("grp", "ep"), None),
        P(("grp", "ep"), None),
        P(("grp", "ep"), None),
        P("ep", "grp", None),
        P("ep", "grp", None),
        P(),
        P(),
    )
    return jax.shard_map(
        local,
        mesh=mesh,
        in_specs=placed,
        out_specs=(P(("grp", "ep"), None), P(("grp", "ep"), None), P(None, ("grp", "ep"), None)),
        check_vma=False,
    )
```

time: 558 us -> 207 us (0.37)
  the two profiles are of different devices: /device:TPU:94 before, /device:TPU:8 now
where the time goes in v1:
time: 207 us
  blocking collectives  73.8 us (36%)
  waiting for transfers between devices  67.1 us (32%)
  Pallas kernels  28.3 us (14%)
  starting transfers between devices  15 us (7%)
  between operations  14.1 us (7%)
  local copies, waits for them, and re-layouts  6.72 us (3%)
    all_to_all x1, blocking collectives, local(): got = lax.all_to_all(sent, 'ep', split_axis=0, concat_axis=0, tiled=True)  73.8 us
    reduce_scatter x1, waiting for transfers between devices, local(): owned = lax.psum_scatter(slot_grad, 'grp', scatter_dimension=0, tiled=True)  59.1 us
    pallas_call x1, Pallas kernels, local(): call(slot_kernel, (jax.ShapeDtypeStruct((width, 3 * hidden_width), BF), j...  12.4 us
    all_to_all x1, starting transfers between devices, local(): mixed = lax.all_to_all(owned, 'ep', split_axis=0, concat_axis=0, tiled=True)  9.73 us
    all_to_all x1, waiting for transfers between devices, local(): mixed = lax.all_to_all(owned, 'ep', split_axis=0, concat_axis=0, tiled=True)  7.89 us
    pallas_call x1, Pallas kernels, local(): call(back_kernel, jax.ShapeDtypeStruct((rows, width + width // 4 + LANES)...  6.4 us
    all_to_all x1, starting transfers between devices, local(): back = lax.all_to_all(back, 'ep', split_axis=0, concat_axis=0, tiled=True)  5.23 us
    unnamed x7, local copies, waits for them, and re-layouts  4.88 us
  transfers between devices with their start and end apart: 4, of which 2 were waited for; matrix products, arithmetic and copies ran while one was open for 3% of the time, Pallas kernels for 7%

profile of v1, /device:TPU:8, one launch (start us, length us, event | category | flops | bytes accessed | tf_op | source)
XLA Modules:
  0.0 206.8 jit_solution(9409738255852469860)
XLA Ops:
  7.2 0.0 all-gather.2.cloned.1.call-start
  7.2 1.8 pad_maximum_fusion
  9.0 0.0 all-gather.2.cloned.1.call-update
  9.0 0.0 reduce-scatter.2.cloned.1.call-start
  9.1 1.4 copy.12.gates
  10.5 1.4 copy.11.routes
  11.9 4.9 %pack.1 = (bf16[256,5248]{1,0:T(8,128)(2,1)}, s32[128,128]{1,0:T(8,128)}) custom-call(s32[1]{0:T(128)} %bitcast.group, s32[128,2]{1,0:T(8,128)} %copy.11.routes, bf16[128,2]{1,0:T(8,128)(2,1)} %copy.12.gates, s32[1,32]{1,0:T(1,128)} %bitcast.14, s32[16,32]{1,0:T(8,128)} %failed.1, bf16[128,2048]{1,0:T(8,128)(2,1)} %tokens.1, bf16[128,2048]{1,0:T(8,128)(2,1)} %grads.1), custom_call_target="tpu_custom_call" | custom-call | tf_op jit(solution)/shard_map/pack/pallas_call | solution.py:210
  16.8 73.8 %all_to_all.27 = bf16[32,8,5248]{2,1,0:T(8,128)(2,1)} all-to-all(bf16[32,8,5248]{2,1,0:T(8,128)(2,1)} %bitcast.11), channel_id=1, replica_groups=mesh['grp'=16,'ep'=32] {'ep'}, dimensions={0} | all-to-all | bytes 5373952 | tf_op jit(solution)/shard_map/all_to_all | solution.py:227
  90.5 0.0 all-gather.2.cloned.1.call-done.weights
  90.5 12.4 %slot.1 = (bf16[2048,1536]{1,0:T(8,128)(2,1)}, bf16[320,1024]{1,0:T(8,128)(2,1)}, bf16[320,128]{1,0:T(8,128)(2,1)}) custom-call(bf16[256,5248]{1,0:T(8,128)(2,1)} %bitcast.8, bf16[2048,1536]{1,0:T(8,128)(2,1)} %all-gather.2.cloned.1.call-done.weights), custom_call_target="tpu_custom_call" | custom-call | tf_op jit(solution)/shard_map/slot/pallas_call | solution.py:228
  102.9 0.0 reduce-scatter.2.cloned.1.call-update
  103.0 6.4 %back.1 = bf16[256,2688]{1,0:T(8,128)(2,1)} custom-call(bf16[320,1024]{1,0:T(8,128)(2,1)} %get-tuple-element.11.pre_grad, bf16[320,128]{1,0:T(8,128)(2,1)} %get-tuple-element.12.gate_grad, bf16[2048,1536]{1,0:T(8,128)(2,1)} %all-gather.2.cloned.1.call-done.weights), custom_call_target="tpu_custom_call" | custom-call | tf_op jit(solution)/shard_map/back/pallas_call | solution.py:239
  109.4 5.2 %all-to-all-start.1 = ((bf16[32,8,2688]{2,1,0:T(8,128)(2,1)}), bf16[32,8,2688]{2,1,0:T(8,128)(2,1)S(1)}, u32[]{:S(2)}, u32[]{:S(2)}) async-start(bf16[32,8,2688]{2,1,0:T(8,128)(2,1)} %bitcast.10), calls=%async_computation.1 | async-start | bytes 2752512 | tf_op jit(solution)/shard_map/all_to_all | solution.py:244
  114.6 59.1 %reduce-scatter.2.cloned.1.call-done = bf16[128,1536]{1,0:T(8,128)(2,1)} async-done(((bf16[2048,1536]{1,0:T(8,128)(2,1)}), bf16[128,1536]{1,0:T(8,128)(2,1)}) %reduce-scatter.2.cloned.1.call-update) | async-done | bytes 393232 | tf_op jit(solution)/shard_map/reduce_scatter | solution.py:238
  173.7 1.8 reshape.21
  175.6 0.0 all-to-all-done.1
  175.6 0.0 copy-start
  175.6 9.7 %all-to-all-start.2 = ((bf16[32,4,1536]{2,1,0:T(4,128)(2,1)}), bf16[32,4,1536]{2,1,0:T(4,128)(2,1)S(1)}, u32[]{:S(2)}, u32[]{:S(2)}) async-start(bf16[32,4,1536]{2,1,0:T(4,128)(2,1)} %reshape.21), calls=%async_computation.3 | async-start | bytes 786432 | tf_op jit(solution)/shard_map/all_to_all | solution.py:255
  185.3 0.0 copy-done
  185.3 2.7 %join.1 = (bf16[128,2048]{1,0:T(8,128)(2,1)}, bf16[128,2]{1,0:T(8,128)(2,1)}) custom-call(bf16[256,2688]{1,0:T(8,128)(2,1)} %bitcast.9, s32[128,128]{1,0:T(8,128)} %get-tuple-element.13.places), custom_call_target="tpu_custom_call" | custom-call | tf_op jit(solution)/shard_map/join/pallas_call | solution.py:245
  188.0 1.3 copy.13
  189.4 7.9 %all-to-all-done.2.mixed = bf16[32,4,1536]{2,1,0:T(4,128)(2,1)S(1)} async-done(((bf16[32,4,1536]{2,1,0:T(4,128)(2,1)}), bf16[32,4,1536]{2,1,0:T(4,128)(2,1)S(1)}, u32[]{:S(2)}, u32[]{:S(2)}) %all-to-all-start.2) | async-done | bytes 393248 | tf_op jit(solution)/shard_map/all_to_all | solution.py:255
  197.3 0.0 copy-start.1
  197.3 0.7 copy-done.1
  198.0 1.9 experts.1
Async XLA Ops:
  7.2 83.4 %all-gather.2.cloned.1.call-start = ((), (), s32[]{:S(2)}) async-start(), calls=%async_computation.4 | async-start | bytes 6684672 | tf_op jit(solution)/shard_map/all_gather | solution.py:209
  9.0 164.7 %reduce-scatter.2.cloned.1.call-start = ((), (), s32[]{:S(2)}) async-start(), calls=%async_computation.5 | async-start | bytes 6684672 | tf_op jit(solution)/shard_map/reduce_scatter | solution.py:238
  109.4 66.2 %all-to-all-start.1 = ((bf16[32,8,2688]{2,1,0:T(8,128)(2,1)}), bf16[32,8,2688]{2,1,0:T(8,128)(2,1)S(1)}, u32[]{:S(2)}, u32[]{:S(2)}) async-start(bf16[32,8,2688]{2,1,0:T(8,128)(2,1)} %bitcast.10), calls=%async_computation.1 | async-start | bytes 2752512 | tf_op jit(solution)/shard_map/all_to_all | solution.py:244
  175.6 9.7 %copy-start = (bf16[32,8,2688]{2,1,0:T(8,128)(2,1)}, bf16[32,8,2688]{2,1,0:T(8,128)(2,1)S(1)}, u32[]{:S(2)}) copy-start(bf16[32,8,2688]{2,1,0:T(8,128)(2,1)S(1)} %all-to-all-done.1) | copy-start | bytes 4128772
  175.6 21.7 %all-to-all-start.2 = ((bf16[32,4,1536]{2,1,0:T(4,128)(2,1)}), bf16[32,4,1536]{2,1,0:T(4,128)(2,1)S(1)}, u32[]{:S(2)}, u32[]{:S(2)}) async-start(bf16[32,4,1536]{2,1,0:T(4,128)(2,1)} %reshape.21), calls=%async_computation.3 | async-start | bytes 786432 | tf_op jit(solution)/shard_map/all_to_all | solution.py:255
  197.3 0.7 copy-start.1
Sparse Core Ops, SparseCore 0:
  10.7 54.0 all-gather.1
  103.1 70.6 reduce-scatter.1

commit v2 on v1

v2 whole, which is shorter than its diff:
```python
import functools

import jax
import jax.numpy as jnp
from jax import lax
from jax.experimental import pallas as pl
from jax.experimental.pallas import tpu as pltpu
from jax.sharding import PartitionSpec as P

BF = jnp.bfloat16
F32 = jnp.float32
LANES = 128
MAIN = 8
TN = (((0,), (0,)), ((), ()))
NT = (((1,), (1,)), ((), ()))


def mm(a, b, dims=(((1,), (0,)), ((), ()))):
    return lax.dot_general(a, b, dims, preferred_element_type=F32)


def iota(shape, dim):
    return lax.broadcasted_iota(jnp.int32, shape, dim)


def one_hot(cond):
    return jnp.where(cond, 1.0, 0.0).astype(BF)


def call(kernel, outs, name, mib, **kw):
    return pl.pallas_call(
        kernel,
        out_shape=outs,
        name=name,
        compiler_params=pltpu.CompilerParams(vmem_limit_bytes=mib * 2**20),
        **kw,
    )


ORDER = (-4, -2, 3, -3, 2, -1, 1, 0)
FIRST = 3


def feature_blocks(place, chips):
    blocks = []
    for core in (place[1], 1 - place[1]):
        for shift in ORDER:
            chip = lax.rem(place[0] + (1 - 2 * core) * shift + chips, chips)
            blocks.append(pl.ds(pl.multiple_of((2 * chip + core) * LANES, LANES), LANES))
    return blocks


def pack_kernel(place, routes, gates, plan, failed, tokens_in, grads_in, sent, places, tokens, grads):
    tok_count, width = tokens.shape
    slots = plan.shape[1]
    half = width // 2
    rows = slots * MAIN
    for j, block in enumerate(feature_blocks(place, width // (2 * LANES))):
        cols = slice(j * LANES, (j + 1) * LANES)
        tokens[:, cols] = tokens_in[:, block]
        grads[:, cols] = grads_in[:, block]
    in_group = iota(failed.shape, 0) == 2 * place[0] + place[1]
    dead = jnp.sum(jnp.where(in_group, failed[...], 0), axis=0, keepdims=True)
    hosting = jnp.where(dead == 0, plan[...], -1)
    diagonal = iota((slots, slots), 0) == iota((slots, slots), 1)
    hosting = jnp.sum(jnp.where(diagonal, hosting, 0), axis=1, keepdims=True)
    slot_ids = iota((slots, tok_count), 0).astype(F32)
    before_slot = one_hot(iota((slots, slots), 1) < iota((slots, slots), 0))
    before_tok = one_hot(iota((tok_count, tok_count), 0) < iota((tok_count, tok_count), 1))
    experts = iota((slots, tok_count), 0)
    ids = [routes[k : k + 1, :] for k in range(2)]
    hot = [jnp.where(experts == i, 1.0, 0.0) for i in ids]
    prefix = mm((hot[0] + hot[1]).astype(BF), before_tok)
    rank = [
        jnp.sum(hot[0] * prefix, axis=0, keepdims=True),
        jnp.sum(hot[1] * (prefix + hot[0]), axis=0, keepdims=True),
    ]
    chosen = []
    for k in range(2):
        cand = jnp.where(hosting == ids[k], 1.0, 0.0)
        ordinal = mm(before_slot, cand.astype(BF))
        count = jnp.maximum(jnp.sum(cand, axis=0, keepdims=True), 1.0)
        pick = rank[k] - count * jnp.floor((rank[k] + 0.5) / count)
        chosen.append(jnp.where(ordinal == pick, cand, 0.0))
    prefix = mm((chosen[0] + chosen[1]).astype(BF), before_tok)
    position = [
        jnp.sum(chosen[0] * prefix, axis=0, keepdims=True),
        jnp.sum(chosen[1] * (prefix + chosen[0]), axis=0, keepdims=True),
    ]
    row_ids = iota((rows, tok_count), 0)
    main, rest = [], []
    for k in range(2):
        slot = jnp.sum(chosen[k] * slot_ids, axis=0, keepdims=True).astype(jnp.int32)
        pos = position[k].astype(jnp.int32)
        main.append(jnp.where(pos < MAIN, slot * MAIN + pos, -64))
        rest.append(jnp.where(pos < MAIN, -64, slot * MAIN + pos - MAIN))
    line = iota(places.shape, 0)
    noted = jnp.full(places.shape, -64, jnp.int32)
    for i, at in enumerate(main + rest):
        noted = jnp.where(line == i, at, noted)
    places[...] = noted

    def pick_rows(at, shift=0):
        return one_hot((at[0] + shift == row_ids) | (at[1] + shift == row_ids))

    whole = pick_rows(main)
    sent[:, :width] = mm(whole, tokens[...]).astype(BF)
    sent[:, width : 2 * width] = mm(whole, grads[...]).astype(BF)
    cut = mm(pick_rows(rest), tokens[:, :half])
    cut += mm(pick_rows(rest, 4), tokens[:, half:])
    cut += mm(pick_rows(rest, 2), grads[:, :half])
    cut += mm(pick_rows(rest, 6), grads[:, half:])
    sent[:, 2 * width : 2 * width + half] = cut.astype(BF)
    lane_ids = iota((LANES, tok_count), 0)
    gate_rows = jnp.zeros((rows, LANES), F32)
    for k in range(2):
        gate = gates[k : k + 1, :].astype(F32)
        first = jnp.where(lane_ids == 0, gate, 0.0).astype(BF)
        second = jnp.where(lane_ids == 1, gate, 0.0).astype(BF)
        gate_rows += mm(one_hot(main[k] == row_ids), first, NT)
        gate_rows += mm(one_hot(rest[k] == row_ids), second, NT)
    sent[:, 2 * width + half :] = gate_rows.astype(BF)


def stack_kernel(*refs):
    out = refs[-1]
    at = 0
    for ref in refs[:-1]:
        out[at : at + ref.shape[0]] = ref[...]
        at += ref.shape[0]


def stack(blocks):
    rows, columns = sum(b.shape[0] for b in blocks), blocks[0].shape[1]
    return call(
        stack_kernel,
        jax.ShapeDtypeStruct((rows, columns), BF),
        "stack",
        8,
        cost_estimate=pl.CostEstimate(flops=0, bytes_accessed=2 * rows * columns, transcendentals=0),
    )(*blocks)


def slot_kernel(got, w0, w1, w2, w3, mine, first, later, pre_out, gate_out, x_all, dy_all):
    rows = got.shape[0]
    hidden_width = w0.shape[1] // 3
    half = w0.shape[0] + w1.shape[0]
    width = 2 * half
    extra = rows // MAIN * 2
    source = iota((extra, rows), 0)
    base = source // 2 * MAIN + source % 2
    column = iota((extra, rows), 1)
    cut = got[:, 2 * width : 2 * width + half]
    head = one_hot(column == base)
    x_all[:rows] = got[:, :width]
    x_all[rows:, :half] = mm(head, cut).astype(BF)
    x_all[rows:, half:] = mm(one_hot(column == base + 4), cut).astype(BF)
    dy_all[:rows] = got[:, width : 2 * width]
    dy_all[rows:, :half] = mm(one_hot(column == base + 2), cut).astype(BF)
    dy_all[rows:, half:] = mm(one_hot(column == base + 6), cut).astype(BF)
    gate_block = got[:, 2 * width + half :]
    gate = jnp.concatenate(
        [gate_block[:, 0:1].astype(F32), mm(head, gate_block)[:, 1:2]], axis=0
    )
    wide = slice(0, 2 * hidden_width)
    down = slice(2 * hidden_width, 3 * hidden_width)
    pre, upstream, at = 0.0, 0.0, 0
    for w in (w0, w1, w2, w3):
        cols = slice(at, at + w.shape[0])
        pre += mm(x_all[:, cols], w[:, wide])
        upstream += mm(dy_all[:, cols], w[:, down])
        at += w.shape[0]
    a = pre[:, :hidden_width]
    b = pre[:, hidden_width:]
    sig = jax.nn.sigmoid(a)
    silu = a * sig
    hidden32 = (silu * b).astype(BF).astype(F32)
    gate_grad = jnp.sum(upstream * hidden32, axis=1, keepdims=True)
    gate_out[...] = jnp.broadcast_to(gate_grad, gate_out.shape).astype(BF)
    hidden_grad = gate * upstream
    pre_out[:, :hidden_width] = (hidden_grad * b * sig * (1.0 + a * (1.0 - sig))).astype(BF)
    pre_out[:, hidden_width:] = (hidden_grad * silu).astype(BF)
    gated = (gate * hidden32).astype(BF)
    at = half
    for out in (first, later, mine):
        at = 0 if out is mine else at
        for d in range(0, out.shape[0], LANES):
            cols = slice(at, at + LANES)
            out[d : d + LANES, wide] = mm(x_all[:, cols], pre_out[...], TN).astype(BF)
            out[d : d + LANES, down] = mm(dy_all[:, cols], gated, TN).astype(BF)
            at += LANES


def back_kernel(pre_grad, gate_grad, w0, w1, w2, w3, back, cut_rows):
    total, columns = pre_grad.shape
    width = 2 * (w0.shape[0] + w1.shape[0])
    rows = back.shape[0]
    extra = total - rows
    quarter = width // 4
    at = 0
    for w in (w0, w1, w2, w3):
        grad = mm(pre_grad[...], w[:, :columns], NT).astype(BF)
        back[:, at : at + w.shape[0]] = grad[:rows]
        cut_rows[:, at : at + w.shape[0]] = grad[rows:]
        at += w.shape[0]
    row = iota((rows, extra), 0)
    column = iota((rows, extra), 1)
    target = row // MAIN * 2 + row % 2
    part = row % MAIN // 2
    cut = jnp.zeros((rows, quarter), F32)
    for h in range(4):
        cols = slice(h * quarter, (h + 1) * quarter)
        cut += mm(one_hot((column == target) & (part == h)), cut_rows[:, cols])
    back[:, width : width + quarter] = cut.astype(BF)
    lane = iota((rows, LANES), 1)
    spread = mm(one_hot((column == target) & (part == 0)), gate_grad[rows:])
    gate_rows = jnp.where(lane == 0, gate_grad[:rows].astype(F32), spread)
    back[:, width + quarter :] = jnp.where(lane < 2, gate_rows, 0.0).astype(BF)


def join_kernel(place, back, places, token_grad, gate_grad):
    tok_count, width = token_grad.shape
    rows = back.shape[0]
    quarter = width // 4
    row_ids = iota((rows, tok_count), 0)
    main = [places[k : k + 1, :] for k in range(2)]
    rest = [places[2 + k : 3 + k, :] for k in range(2)]
    whole = one_hot((main[0] == row_ids) | (main[1] == row_ids))
    cut = back[:, width : width + quarter]
    blocks = feature_blocks(place, width // (2 * LANES))
    for h in range(4):
        cols = slice(h * quarter, (h + 1) * quarter)
        here = one_hot((rest[0] + 2 * h == row_ids) | (rest[1] + 2 * h == row_ids))
        total = mm(whole, back[:, cols], TN) + mm(here, cut, TN)
        for j in range(quarter // LANES):
            block = blocks[h * (quarter // LANES) + j]
            token_grad[:, block] = total[:, j * LANES : (j + 1) * LANES].astype(BF)
    gate_rows = back[:, width + quarter :]
    for k in range(2):
        value = mm(gate_rows, one_hot(main[k] == row_ids), TN)[0:1, :]
        value += mm(gate_rows, one_hot(rest[k] == row_ids), TN)[1:2, :]
        gate_grad[k : k + 1, :] = value.astype(BF)


def expert_kernel(groups, plan, mixed, out):
    out[...] = jnp.zeros_like(out)
    for s in range(mixed.shape[0]):
        e = plan[s]
        out[e] += mixed[s].astype(F32)
    out[...] = out[...] * (1.0 / groups)


def move(array, step):
    chips = lax.axis_size("z")
    pairs = []
    for z in range(chips):
        pairs.append((2 * z, 2 * ((z + step) % chips)))
        pairs.append((2 * z + 1, 2 * ((z - step) % chips) + 1))
    return lax.ppermute(array, ("z", "core"), pairs)


def swap(array):
    return lax.ppermute(array, "core", [(0, 1), (1, 0)])


def local(tokens, out_grad, routes, gates, w_gate_up, w_down, plan, failed):
    chips = lax.axis_size("z")
    groups = chips * 2
    slots = lax.axis_size("ep")
    tok_count, width = tokens.shape
    hidden_width = w_down.shape[2]
    columns = 3 * hidden_width
    experts = slots // 2
    rows = slots * MAIN
    total = slots * (MAIN + 2)
    each = width // (groups * slots)
    smem = pl.BlockSpec(memory_space=pltpu.SMEM)
    vmem = pl.BlockSpec(memory_space=pltpu.VMEM)
    place = jnp.stack([lax.axis_index("z"), lax.axis_index("core")])

    sent, places = call(
        pack_kernel,
        (
            jax.ShapeDtypeStruct((rows, 2 * width + width // 2 + LANES), BF),
            jax.ShapeDtypeStruct((8, tok_count), jnp.int32),
        ),
        "pack",
        56,
        in_specs=[smem] + [vmem] * 6,
        scratch_shapes=[pltpu.VMEM((tok_count, width), BF)] * 2,
    )(
        place,
        routes.T,
        gates.T,
        plan.reshape(1, slots),
        failed,
        tokens,
        out_grad,
    )
    sent, w_gate_up, w_down = lax.optimization_barrier((sent, w_gate_up, w_down))
    got = lax.all_to_all(sent, "ep", split_axis=0, concat_axis=0, tiled=True)
    own = jnp.concatenate([w_gate_up[0], w_down[0]], axis=1)
    below, above = move(own, 1), move(own, -1)
    third, above2 = move(below, 2), move(above, -1)
    last, above3 = move(stack([third, below]), 1), move(above2, -1)
    w_mine = [stack([last, above3]), stack([third, above2, below, above, own])]
    w_all = w_mine + [swap(w) for w in w_mine]

    part = width // groups
    mine, first, later, pre_grad, gate_rows = call(
        slot_kernel,
        (
            jax.ShapeDtypeStruct((width // 2, columns), BF),
            jax.ShapeDtypeStruct((FIRST * part, columns), BF),
            jax.ShapeDtypeStruct((width // 2 - FIRST * part, columns), BF),
            jax.ShapeDtypeStruct((total, 2 * hidden_width), BF),
            jax.ShapeDtypeStruct((total, LANES), BF),
        ),
        "slot",
        32,
        in_specs=[vmem] * 5,
        scratch_shapes=[pltpu.VMEM((total, width), BF)] * 2,
    )(got, *w_all)
    first, later = swap(first), swap(later)
    back = call(
        back_kernel,
        jax.ShapeDtypeStruct((rows, width + width // 4 + LANES), BF),
        "back",
        24,
        in_specs=[vmem] * 6,
        scratch_shapes=[pltpu.VMEM((total - rows, width), BF)],
    )(pre_grad, gate_rows, *w_all)

    def both(j, n=1):
        theirs, at = (first, j) if j < FIRST else (later, j - FIRST)
        return (
            mine[j * part : (j + n) * part].astype(F32)
            + theirs[at * part : (at + n) * part].astype(F32)
        )

    minus, plus = both(0, 2).astype(BF), both(2).astype(BF)
    minus, plus, back = lax.optimization_barrier((minus, plus, back))
    minus, plus = move(minus, -1), move(plus, 1)
    far_sum = (minus[:part].astype(F32) + both(3)).astype(BF)
    plus = (plus.astype(F32) + both(4)).astype(BF)
    far_sum, plus = move(far_sum, -2), move(plus, 1)
    minus = (far_sum.astype(F32) + minus[part:].astype(F32) + both(5)).astype(BF)
    plus = (plus.astype(F32) + both(6)).astype(BF)
    minus, plus = move(minus, -1), move(plus, 1)
    owned = (minus.astype(F32) + plus.astype(F32) + both(7)).astype(BF)

    back = lax.all_to_all(back, "ep", split_axis=0, concat_axis=0, tiled=True)
    owned, back = lax.optimization_barrier((owned, back))
    token_grad, gate_grad = call(
        join_kernel,
        (
            jax.ShapeDtypeStruct((tok_count, width), BF),
            jax.ShapeDtypeStruct((2, tok_count), BF),
        ),
        "join",
        16,
        in_specs=[smem, vmem, vmem],
    )(place, back, places)
    owned = owned.reshape(slots, each, columns)
    mixed = lax.all_to_all(owned, "ep", split_axis=0, concat_axis=0, tiled=True)
    weight_grad = call(
        functools.partial(expert_kernel, groups),
        jax.ShapeDtypeStruct((experts, each, columns), F32),
        "experts",
        8,
        in_specs=[smem, vmem],
    )(plan, mixed)
    return token_grad, gate_grad.T, weight_grad


def solution(mesh):
    devices = mesh.devices.reshape(mesh.shape["grp"] // 2, 2, mesh.shape["ep"])
    fine = jax.sharding.Mesh(devices, ("z", "core", "ep"))
    everywhere = P(("z", "core", "ep"), None)
    weight = P("ep", ("z", "core"), None)
    return jax.shard_map(
        local,
        mesh=fine,
        in_specs=(everywhere,) * 4 + (weight, weight, P(), P()),
        out_specs=(everywhere, everywhere, P(None, ("z", "core", "ep"), None)),
        check_vma=False,
    )
```

time: 207 us -> 184 us (0.89)
  starting transfers between devices: 15 us -> 91.6 us
  blocking collectives: 73.8 us -> 0 us
  between operations: 14.1 us -> 0.96 us
  Pallas kernels: 28.3 us -> 18.8 us
  waiting for transfers between devices: 67.1 us -> 59.5 us
  other arithmetic: 1.79 us -> 6.38 us
    all_to_all x1 -> x0, blocking collectives: 73.8 us -> none  [local(): got = lax.all_to_all(sent, 'ep', split_axis=0, concat_axis=0, tiled=True)]
    ppermute x0 -> x16, starting transfers between devices: none -> 68.4 us  [the longest x12 59.2 us: move(): return lax.ppermute(array, ('z', 'core'), pairs)]
    reduce_scatter x1 -> x0, waiting for transfers between devices: 59.1 us -> none  [local(): owned = lax.psum_scatter(slot_grad, 'grp', scatter_dimension=0, tiled=True)]
    ppermute x0 -> x16, waiting for transfers between devices: none -> 47.8 us  [the longest x12 45.4 us: move(): return lax.ppermute(array, ('z', 'core'), pairs)]
    all_to_all x0 -> x1, starting transfers between devices: none -> 10.4 us  [local(): got = lax.all_to_all(sent, 'ep', split_axis=0, concat_axis=0, tiled=True)]
    convert_element_type x0 -> x5, other arithmetic: none -> 5.8 us  [the longest x1 1.69 us: local(): (far_sum.astype(F32) + minus[part:].astype(F32) + both(5)).astype(BF)]
    pallas_call x1, Pallas kernels: 6.4 us -> 2.16 us  [local(): call(back_kernel, jax.ShapeDtypeStruct((rows, width + width // 4 + LANES)...]
    all_to_all x1, waiting for transfers between devices: 7.89 us -> 11.7 us  [local(): mixed = lax.all_to_all(owned, 'ep', split_axis=0, concat_axis=0, tiled=True)]
  transfers between devices with their start and end apart: 4 -> 19, of which waited for: 2 -> 12; matrix products, arithmetic and copies ran while one was open for 3% -> 3% of each run, Pallas kernels for 7% -> 2%
where the time goes in v2:
time: 184 us; the launch traced here: 183 us
  starting transfers between devices  91.6 us (50%)
  waiting for transfers between devices  59.5 us (32%)
  Pallas kernels  18.8 us (10%)
  other arithmetic  6.38 us (3%)
  local copies, waits for them, and re-layouts  6.08 us (3%)
    ppermute x12, starting transfers between devices, move(): return lax.ppermute(array, ('z', 'core'), pairs)  59.2 us
    ppermute x12, waiting for transfers between devices, move(): return lax.ppermute(array, ('z', 'core'), pairs)  45.4 us
    all_to_all x1, waiting for transfers between devices, local(): mixed = lax.all_to_all(owned, 'ep', split_axis=0, concat_axis=0, tiled=True)  11.7 us
    all_to_all x1, starting transfers between devices, local(): got = lax.all_to_all(sent, 'ep', split_axis=0, concat_axis=0, tiled=True)  10.4 us
    ppermute x4, starting transfers between devices, swap(): return lax.ppermute(array, 'core', [(0, 1), (1, 0)])  9.16 us
    pallas_call x1, Pallas kernels, local(): call(slot_kernel, (jax.ShapeDtypeStruct((width // 2, columns), BF), jax.S...  8.48 us
    all_to_all x1, starting transfers between devices, local(): back = lax.all_to_all(back, 'ep', split_axis=0, concat_axis=0, tiled=True)  6.47 us
    all_to_all x1, starting transfers between devices, local(): mixed = lax.all_to_all(owned, 'ep', split_axis=0, concat_axis=0, tiled=True)  6.35 us
  transfers between devices with their start and end apart: 19, of which 12 were waited for; matrix products, arithmetic and copies ran while one was open for 3% of the time, Pallas kernels for 2%

profile of v2, /device:TPU:8, one launch (start us, length us, event | category | flops | bytes accessed | tf_op | source)
XLA Modules:
  0.0 183.3 jit_solution(6017597289862647558)
XLA Ops:
  1.2 4.5 %pack.1 = (bf16[256,5248]{1,0:T(8,128)(2,1)}, s32[8,128]{1,0:T(8,128)}) custom-call(s32[2]{0:T(128)} %pad_add_fusion.place, s32[2,128]{1,0:T(2,128)} %bitcast.18, bf16[2,128]{1,0:T(2,128)(2,1)} %bitcast.19, s32[1,32]{1,0:T(1,128)} %bitcast.14, s32[16,32]{1,0:T(8,128)} %failed.1, bf16[128,2048]{1,0:T(8,128)(2,1)} %tokens_in.1, bf16[128,2048]{1,0:T(8,128)(2,1)} %grads_in.1), custom_call_target="tpu_custom_call" | custom-call | tf_op jit(solution)/shard_map/pack/pallas_call | solution.py:281
  5.7 10.4 %all-to-all-start = ((bf16[32,8,5248]{2,1,0:T(8,128)(2,1)}), bf16[32,8,5248]{2,1,0:T(8,128)(2,1)}, u32[]{:S(2)}, u32[]{:S(2)}) async-start(bf16[32,8,5248]{2,1,0:T(8,128)(2,1)} %bitcast.15), calls=%async_computation | async-start | bytes 5373952 | tf_op jit(solution)/shard_map/all_to_all | solution.py:301
  16.1 4.3 %collective-permute-start = (bf16[128,1536]{1,0:T(8,128)(2,1)S(1)}, bf16[128,1536]{1,0:T(8,128)(2,1)S(1)}, u32[]{:S(2)}, u32[]{:S(2)}) collective-permute-start(bf16[128,1536]{1,0:T(8,128)(2,1)S(1)} %pad_maximum_fusion.refs_4_), channel_id=1, source_target_pairs={{0,64},{32,480},{64,128},{96,32},{128,192},{160,96},{192,256},{224... | collective-permute-start | bytes 1179656 | tf_op jit(solution)/shard_map/ppermute | solution.py:259
  20.4 8.6 %collective-permute-start.3 = (bf16[128,1536]{1,0:T(8,128)(2,1)S(1)}, bf16[128,1536]{1,0:T(8,128)(2,1)S(1)}, u32[]{:S(2)}, u32[]{:S(2)}) collective-permute-start(bf16[128,1536]{1,0:T(8,128)(2,1)S(1)} %pad_maximum_fusion.refs_4_), channel_id=1, source_target_pairs={{0,448},{32,96},{64,0},{96,160},{128,64},{160,224},{192,128},{224,... | collective-permute-start | bytes 1179656 | tf_op jit(solution)/shard_map/ppermute | solution.py:259
  29.0 4.8 %collective-permute-done.refs_1_.refs_2_ = bf16[128,1536]{1,0:T(8,128)(2,1)S(1)} collective-permute-done((bf16[128,1536]{1,0:T(8,128)(2,1)S(1)}, bf16[128,1536]{1,0:T(8,128)(2,1)S(1)}, u32[]{:S(2)}, u32[]{:S(2)}) %collective-permute-start) | collective-permute-done | bytes 393248 | tf_op jit(solution)/shard_map/ppermute | solution.py:259
  33.8 2.0 %collective-permute-start.1 = (bf16[128,1536]{1,0:T(8,128)(2,1)S(1)}, bf16[128,1536]{1,0:T(8,128)(2,1)S(1)}, u32[]{:S(2)}, u32[]{:S(2)}) collective-permute-start(bf16[128,1536]{1,0:T(8,128)(2,1)S(1)} %collective-permute-done.refs_1_.refs_2_), channel_id=1, source_target_pairs={{0,128},{32,416},{64,192},{96,480},{128,256},{160,32},{192,320},{2... | collective-permute-start | bytes 1179656 | tf_op jit(solution)/shard_map/ppermute | solution.py:259
  35.8 6.7 %collective-permute-start.4 = (bf16[128,1536]{1,0:T(8,128)(2,1)S(1)}, bf16[128,1536]{1,0:T(8,128)(2,1)S(1)}, u32[]{:S(2)}, u32[]{:S(2)}) collective-permute-start(bf16[128,1536]{1,0:T(8,128)(2,1)S(1)} %collective-permute-done.3.refs_3_), channel_id=1, source_target_pairs={{0,448},{32,96},{64,0},{96,160},{128,64},{160,224},{192,128},{224,... | collective-permute-start | bytes 1179656 | tf_op jit(solution)/shard_map/ppermute | solution.py:259
  42.5 9.1 %collective-permute-done.1.refs_0_ = bf16[128,1536]{1,0:T(8,128)(2,1)S(1)} collective-permute-done((bf16[128,1536]{1,0:T(8,128)(2,1)S(1)}, bf16[128,1536]{1,0:T(8,128)(2,1)S(1)}, u32[]{:S(2)}, u32[]{:S(2)}) %collective-permute-start.1) | collective-permute-done | bytes 393248 | tf_op jit(solution)/shard_map/ppermute | solution.py:259
  51.6 6.4 %collective-permute-start.2 = (bf16[256,1536]{1,0:T(8,128)(2,1)S(1)}, bf16[256,1536]{1,0:T(8,128)(2,1)S(1)}, u32[]{:S(2)}, u32[]{:S(2)}) collective-permute-start(bf16[256,1536]{1,0:T(8,128)(2,1)S(1)} %stack.15), channel_id=1, source_target_pairs={{0,64},{32,480},{64,128},{96,32},{128,192},{160,96},{192,256},{224... | collective-permute-start | bytes 2359304 | tf_op jit(solution)/shard_map/ppermute | solution.py:259
  58.2 1.9 %collective-permute-start.7 = (bf16[640,1536]{1,0:T(8,128)(2,1)S(1)}, bf16[640,1536]{1,0:T(8,128)(2,1)S(1)}, u32[]{:S(2)}, u32[]{:S(2)}) collective-permute-start(bf16[640,1536]{1,0:T(8,128)(2,1)S(1)} %stack.17.w1), channel_id=1, source_target_pairs={{0,32},{32,0},{1,33},{33,1},{2,34},{34,2},{3,35},{35,3},{4,36},{36... | collective-permute-start | bytes 5898248 | tf_op jit(solution)/shard_map/ppermute | solution.py:263
  60.1 2.2 %collective-permute-start.5 = (bf16[128,1536]{1,0:T(8,128)(2,1)S(1)}, bf16[128,1536]{1,0:T(8,128)(2,1)S(1)}, u32[]{:S(2)}, u32[]{:S(2)}) collective-permute-start(bf16[128,1536]{1,0:T(8,128)(2,1)S(1)} %collective-permute-done.4.refs_1_), channel_id=1, source_target_pairs={{0,448},{32,96},{64,0},{96,160},{128,64},{160,224},{192,128},{224,... | collective-permute-start | bytes 1179656 | tf_op jit(solution)/shard_map/ppermute | solution.py:259
  62.3 7.4 %collective-permute-done.5.refs_1_ = bf16[128,1536]{1,0:T(8,128)(2,1)S(1)} collective-permute-done((bf16[128,1536]{1,0:T(8,128)(2,1)S(1)}, bf16[128,1536]{1,0:T(8,128)(2,1)S(1)}, u32[]{:S(2)}, u32[]{:S(2)}) %collective-permute-start.5) | collective-permute-done | bytes 393248 | tf_op jit(solution)/shard_map/ppermute | solution.py:259
  69.8 2.0 %collective-permute-done.2.refs_0_ = bf16[256,1536]{1,0:T(8,128)(2,1)S(1)} collective-permute-done((bf16[256,1536]{1,0:T(8,128)(2,1)S(1)}, bf16[256,1536]{1,0:T(8,128)(2,1)S(1)}, u32[]{:S(2)}, u32[]{:S(2)}) %collective-permute-start.2) | collective-permute-done | bytes 786464 | tf_op jit(solution)/shard_map/ppermute | solution.py:259
  71.8 2.9 %collective-permute-start.6 = (bf16[384,1536]{1,0:T(8,128)(2,1)S(1)}, bf16[384,1536]{1,0:T(8,128)(2,1)S(1)}, u32[]{:S(2)}, u32[]{:S(2)}) collective-permute-start(bf16[384,1536]{1,0:T(8,128)(2,1)S(1)} %stack.16.w0), channel_id=1, source_target_pairs={{0,32},{32,0},{1,33},{33,1},{2,34},{34,2},{3,35},{35,3},{4,36},{36... | collective-permute-start | bytes 3538952 | tf_op jit(solution)/shard_map/ppermute | solution.py:263
  74.7 2.5 %collective-permute-done.6.w2 = bf16[384,1536]{1,0:T(8,128)(2,1)S(1)} collective-permute-done((bf16[384,1536]{1,0:T(8,128)(2,1)S(1)}, bf16[384,1536]{1,0:T(8,128)(2,1)S(1)}, u32[]{:S(2)}, u32[]{:S(2)}) %collective-permute-start.6) | collective-permute-done | bytes 1179680 | tf_op jit(solution)/shard_map/ppermute | solution.py:263
  82.4 8.5 %slot.1 = (bf16[1024,1536]{1,0:T(8,128)(2,1)S(1)}, bf16[384,1536]{1,0:T(8,128)(2,1)S(1)}, bf16[640,1536]{1,0:T(8,128)(2,1)}, bf16[320,1024]{1,0:T(8,128)(2,1)S(1)}, bf16[320,128]{1,0:T(8,128)(2,1)S(1)}) custom-call(bf16[256,5248]{1,0:T(8,128)(2,1)} %bitcast.6.got, bf16[384,1536]{1,0:T(8,128)(2,1)S(1)} %stack.16.w0, bf16[640,1536]{1,0:T(8,128)(2,1)S(1)} %stack.17.w1, ...), custom_call_target="tpu_custom_call" | custom-call | tf_op jit(solution)/shard_map/slot/pallas_call | solution.py:310
  90.9 2.3 %collective-permute-start.8 = (bf16[384,1536]{1,0:T(8,128)(2,1)S(1)}, bf16[384,1536]{1,0:T(8,128)(2,1)S(1)}, u32[]{:S(2)}, u32[]{:S(2)}) collective-permute-start(bf16[384,1536]{1,0:T(8,128)(2,1)S(1)} %get-tuple-element.25), channel_id=1, source_target_pairs={{0,32},{32,0},{1,33},{33,1},{2,34},{34,2},{3,35},{35,3},{4,36},{36... | collective-permute-start | bytes 3538952 | tf_op jit(solution)/shard_map/ppermute | solution.py:263
  93.2 2.0 %collective-permute-start.10 = (bf16[640,1536]{1,0:T(8,128)(2,1)}, bf16[640,1536]{1,0:T(8,128)(2,1)}, u32[]{:S(2)}, u32[]{:S(2)}) collective-permute-start(bf16[640,1536]{1,0:T(8,128)(2,1)} %get-tuple-element.29), channel_id=1, source_target_pairs={{0,32},{32,0},{1,33},{33,1},{2,34},{34,2},{3,35},{35,3},{4,36},{36... | collective-permute-start | bytes 5898248 | tf_op jit(solution)/shard_map/ppermute | solution.py:263
  95.2 2.2 %back.1 = bf16[256,2688]{1,0:T(8,128)(2,1)S(1)} custom-call(bf16[320,1024]{1,0:T(8,128)(2,1)S(1)} %get-tuple-element.26.pre_grad, bf16[320,128]{1,0:T(8,128)(2,1)S(1)} %get-tuple-element.27.gate_grad, bf16[384,1536]{1,0:T(8,128)(2,1)S(1)} %stack.16.w0, bf16[640,1536]{1,0:T(8,128)(2,1)S(1)} %stack.17.w1, bf16[384,1536]{1,0:T(8,128)(2,1)S(1)} %copy-done.4, ...), custom_call_target="tpu_custom_call" | custom-call | tf_op jit(solution)/shard_map/back/pallas_call | solution.py:325
  98.6 10.0 %collective-permute-start.9 = (bf16[256,1536]{1,0:T(8,128)(2,1)S(1)}, bf16[256,1536]{1,0:T(8,128)(2,1)S(1)}, u32[]{:S(2)}, u32[]{:S(2)}) collective-permute-start(bf16[256,1536]{1,0:T(8,128)(2,1)S(1)} %add_convert_fusion), channel_id=1, source_target_pairs={{0,448},{32,96},{64,0},{96,160},{128,64},{160,224},{192,128},{224,... | collective-permute-start | bytes 2359304 | tf_op jit(solution)/shard_map/ppermute | solution.py:259
  108.5 1.9 %collective-permute-start.13 = (bf16[128,1536]{1,0:T(8,128)(2,1)}, bf16[128,1536]{1,0:T(8,128)(2,1)S(1)}, u32[]{:S(2)}, u32[]{:S(2)}) collective-permute-start(bf16[128,1536]{1,0:T(8,128)(2,1)} %add_convert_fusion.6), channel_id=1, source_target_pairs={{0,64},{32,480},{64,128},{96,32},{128,192},{160,96},{192,256},{224... | collective-permute-start | bytes 1179656 | tf_op jit(solution)/shard_map/ppermute | solution.py:259
  110.5 6.5 %all-to-all-start.1 = ((bf16[32,8,2688]{2,1,0:T(8,128)(2,1)}), bf16[32,8,2688]{2,1,0:T(8,128)(2,1)S(1)}, u32[]{:S(2)}, u32[]{:S(2)}) async-start(bf16[32,8,2688]{2,1,0:T(8,128)(2,1)} %bitcast.13), calls=%async_computation.1 | async-start | bytes 2752512 | tf_op jit(solution)/shard_map/all_to_all | solution.py:352
  117.0 4.9 %collective-permute-done.13 = bf16[128,1536]{1,0:T(8,128)(2,1)S(1)} collective-permute-done((bf16[128,1536]{1,0:T(8,128)(2,1)}, bf16[128,1536]{1,0:T(8,128)(2,1)S(1)}, u32[]{:S(2)}, u32[]{:S(2)}) %collective-permute-start.13) | collective-permute-done | bytes 393248 | tf_op jit(solution)/shard_map/ppermute | solution.py:259
  123.7 4.4 %collective-permute-start.11 = (bf16[128,1536]{1,0:T(8,128)(2,1)S(1)}, bf16[128,1536]{1,0:T(8,128)(2,1)S(1)}, u32[]{:S(2)}, u32[]{:S(2)}) collective-permute-start(bf16[128,1536]{1,0:T(8,128)(2,1)S(1)} %get-tuple-element.39), channel_id=1, source_target_pairs={{0,384},{32,160},{64,448},{96,224},{128,0},{160,288},{192,64},{224... | collective-permute-start | bytes 1179656 | tf_op jit(solution)/shard_map/ppermute | solution.py:259
  128.1 4.6 %collective-permute-start.14 = (bf16[128,1536]{1,0:T(8,128)(2,1)S(1)}, bf16[128,1536]{1,0:T(8,128)(2,1)S(1)}, u32[]{:S(2)}, u32[]{:S(2)}) collective-permute-start(bf16[128,1536]{1,0:T(8,128)(2,1)S(1)} %get-tuple-element.40), channel_id=1, source_target_pairs={{0,64},{32,480},{64,128},{96,32},{128,192},{160,96},{192,256},{224... | collective-permute-start | bytes 1179656 | tf_op jit(solution)/shard_map/ppermute | solution.py:259
  132.7 7.7 %collective-permute-done.11 = bf16[128,1536]{1,0:T(8,128)(2,1)S(1)} collective-permute-done((bf16[128,1536]{1,0:T(8,128)(2,1)S(1)}, bf16[128,1536]{1,0:T(8,128)(2,1)S(1)}, u32[]{:S(2)}, u32[]{:S(2)}) %collective-permute-start.11) | collective-permute-done | bytes 393248 | tf_op jit(solution)/shard_map/ppermute | solution.py:259
  142.4 6.3 %collective-permute-start.12 = (bf16[128,1536]{1,0:T(8,128)(2,1)S(1)}, bf16[128,1536]{1,0:T(8,128)(2,1)S(1)}, u32[]{:S(2)}, u32[]{:S(2)}) collective-permute-start(bf16[128,1536]{1,0:T(8,128)(2,1)S(1)} %get-tuple-element.37), channel_id=1, source_target_pairs={{0,448},{32,96},{64,0},{96,160},{128,64},{160,224},{192,128},{224,... | collective-permute-start | bytes 1179656 | tf_op jit(solution)/shard_map/ppermute | solution.py:259
  148.8 1.9 %collective-permute-start.15 = (bf16[128,1536]{1,0:T(8,128)(2,1)S(1)}, bf16[128,1536]{1,0:T(8,128)(2,1)S(1)}, u32[]{:S(2)}, u32[]{:S(2)}) collective-permute-start(bf16[128,1536]{1,0:T(8,128)(2,1)S(1)} %get-tuple-element.38), channel_id=1, source_target_pairs={{0,64},{32,480},{64,128},{96,32},{128,192},{160,96},{192,256},{224... | collective-permute-start | bytes 1179656 | tf_op jit(solution)/shard_map/ppermute | solution.py:259
  150.7 6.1 %collective-permute-done.12 = bf16[128,1536]{1,0:T(8,128)(2,1)S(1)} collective-permute-done((bf16[128,1536]{1,0:T(8,128)(2,1)S(1)}, bf16[128,1536]{1,0:T(8,128)(2,1)S(1)}, u32[]{:S(2)}, u32[]{:S(2)}) %collective-permute-start.12) | collective-permute-done | bytes 393248 | tf_op jit(solution)/shard_map/ppermute | solution.py:259
  156.8 2.9 %collective-permute-done.15 = bf16[128,1536]{1,0:T(8,128)(2,1)S(1)} collective-permute-done((bf16[128,1536]{1,0:T(8,128)(2,1)S(1)}, bf16[128,1536]{1,0:T(8,128)(2,1)S(1)}, u32[]{:S(2)}, u32[]{:S(2)}) %collective-permute-start.15) | collective-permute-done | bytes 393248 | tf_op jit(solution)/shard_map/ppermute | solution.py:259
  161.8 6.4 %all-to-all-start.2 = ((bf16[32,4,1536]{2,1,0:T(4,128)(2,1)}), bf16[32,4,1536]{2,1,0:T(4,128)(2,1)S(1)}, u32[]{:S(2)}, u32[]{:S(2)}) async-start(bf16[32,4,1536]{2,1,0:T(4,128)(2,1)} %reshape.17), calls=%async_computation.2 | async-start | bytes 786432 | tf_op jit(solution)/shard_map/all_to_all | solution.py:365
  170.1 11.7 %all-to-all-done.2.mixed = bf16[32,4,1536]{2,1,0:T(4,128)(2,1)S(1)} async-done(((bf16[32,4,1536]{2,1,0:T(4,128)(2,1)}), bf16[32,4,1536]{2,1,0:T(4,128)(2,1)S(1)}, u32[]{:S(2)}, u32[]{:S(2)}) %all-to-all-start.2) | async-done | bytes 393248 | tf_op jit(solution)/shard_map/all_to_all | solution.py:365
  (44 shorter events, 16.7 us)
Async XLA Ops:
  5.7 10.4 %copy-start.9 = (bf16[1,128,1024]{2,1,0:T(8,128)(2,1)S(1)}, bf16[1,128,1024]{2,1,0:T(8,128)(2,1)}, u32[]{:S(2)}) copy-start(bf16[1,128,1024]{2,1,0:T(8,128)(2,1)} %param.12) | copy-start | bytes 786436
  5.7 10.4 %copy-start.10 = (bf16[1,128,512]{2,1,0:T(8,128)(2,1)S(1)}, bf16[1,128,512]{2,1,0:T(8,128)(2,1)}, u32[]{:S(2)}) copy-start(bf16[1,128,512]{2,1,0:T(8,128)(2,1)} %param.13) | copy-start | bytes 393220
  5.7 73.9 %all-to-all-start = ((bf16[32,8,5248]{2,1,0:T(8,128)(2,1)}), bf16[32,8,5248]{2,1,0:T(8,128)(2,1)}, u32[]{:S(2)}, u32[]{:S(2)}) async-start(bf16[32,8,5248]{2,1,0:T(8,128)(2,1)} %bitcast.15), calls=%async_computation | async-start | bytes 5373952 | tf_op jit(solution)/shard_map/all_to_all | solution.py:301
  16.1 17.7 %collective-permute-start = (bf16[128,1536]{1,0:T(8,128)(2,1)S(1)}, bf16[128,1536]{1,0:T(8,128)(2,1)S(1)}, u32[]{:S(2)}, u32[]{:S(2)}) collective-permute-start(bf16[128,1536]{1,0:T(8,128)(2,1)S(1)} %pad_maximum_fusion.refs_4_), channel_id=1, source_target_pairs={{0,64},{32,480},{64,128},{96,32},{128,192},{160,96},{192,256},{224... | collective-permute-start | bytes 1179656 | tf_op jit(solution)/shard_map/ppermute | solution.py:259
  20.4 15.4 %collective-permute-start.3 = (bf16[128,1536]{1,0:T(8,128)(2,1)S(1)}, bf16[128,1536]{1,0:T(8,128)(2,1)S(1)}, u32[]{:S(2)}, u32[]{:S(2)}) collective-permute-start(bf16[128,1536]{1,0:T(8,128)(2,1)S(1)} %pad_maximum_fusion.refs_4_), channel_id=1, source_target_pairs={{0,448},{32,96},{64,0},{96,160},{128,64},{160,224},{192,128},{224,... | collective-permute-start | bytes 1179656 | tf_op jit(solution)/shard_map/ppermute | solution.py:259
  33.8 17.7 %collective-permute-start.1 = (bf16[128,1536]{1,0:T(8,128)(2,1)S(1)}, bf16[128,1536]{1,0:T(8,128)(2,1)S(1)}, u32[]{:S(2)}, u32[]{:S(2)}) collective-permute-start(bf16[128,1536]{1,0:T(8,128)(2,1)S(1)} %collective-permute-done.refs_1_.refs_2_), channel_id=1, source_target_pairs={{0,128},{32,416},{64,192},{96,480},{128,256},{160,32},{192,320},{2... | collective-permute-start | bytes 1179656 | tf_op jit(solution)/shard_map/ppermute | solution.py:259
  35.8 22.2 %collective-permute-start.4 = (bf16[128,1536]{1,0:T(8,128)(2,1)S(1)}, bf16[128,1536]{1,0:T(8,128)(2,1)S(1)}, u32[]{:S(2)}, u32[]{:S(2)}) collective-permute-start(bf16[128,1536]{1,0:T(8,128)(2,1)S(1)} %collective-permute-done.3.refs_3_), channel_id=1, source_target_pairs={{0,448},{32,96},{64,0},{96,160},{128,64},{160,224},{192,128},{224,... | collective-permute-start | bytes 1179656 | tf_op jit(solution)/shard_map/ppermute | solution.py:259
  51.6 20.1 %collective-permute-start.2 = (bf16[256,1536]{1,0:T(8,128)(2,1)S(1)}, bf16[256,1536]{1,0:T(8,128)(2,1)S(1)}, u32[]{:S(2)}, u32[]{:S(2)}) collective-permute-start(bf16[256,1536]{1,0:T(8,128)(2,1)S(1)} %stack.15), channel_id=1, source_target_pairs={{0,64},{32,480},{64,128},{96,32},{128,192},{160,96},{192,256},{224... | collective-permute-start | bytes 2359304 | tf_op jit(solution)/shard_map/ppermute | solution.py:259
  58.2 20.1 %collective-permute-start.7 = (bf16[640,1536]{1,0:T(8,128)(2,1)S(1)}, bf16[640,1536]{1,0:T(8,128)(2,1)S(1)}, u32[]{:S(2)}, u32[]{:S(2)}) collective-permute-start(bf16[640,1536]{1,0:T(8,128)(2,1)S(1)} %stack.17.w1), channel_id=1, source_target_pairs={{0,32},{32,0},{1,33},{33,1},{2,34},{34,2},{3,35},{35,3},{4,36},{36... | collective-permute-start | bytes 5898248 | tf_op jit(solution)/shard_map/ppermute | solution.py:263
  60.1 9.7 %collective-permute-start.5 = (bf16[128,1536]{1,0:T(8,128)(2,1)S(1)}, bf16[128,1536]{1,0:T(8,128)(2,1)S(1)}, u32[]{:S(2)}, u32[]{:S(2)}) collective-permute-start(bf16[128,1536]{1,0:T(8,128)(2,1)S(1)} %collective-permute-done.4.refs_1_), channel_id=1, source_target_pairs={{0,448},{32,96},{64,0},{96,160},{128,64},{160,224},{192,128},{224,... | collective-permute-start | bytes 1179656 | tf_op jit(solution)/shard_map/ppermute | solution.py:259
  71.8 5.4 %collective-permute-start.6 = (bf16[384,1536]{1,0:T(8,128)(2,1)S(1)}, bf16[384,1536]{1,0:T(8,128)(2,1)S(1)}, u32[]{:S(2)}, u32[]{:S(2)}) collective-permute-start(bf16[384,1536]{1,0:T(8,128)(2,1)S(1)} %stack.16.w0), channel_id=1, source_target_pairs={{0,32},{32,0},{1,33},{33,1},{2,34},{34,2},{3,35},{35,3},{4,36},{36... | collective-permute-start | bytes 3538952 | tf_op jit(solution)/shard_map/ppermute | solution.py:263
  77.2 1.1 copy-start.3
  78.3 1.3 copy-start
  79.6 1.5 copy-start.1
  81.1 1.3 copy-start.4
  90.9 7.5 %copy-start.5 = (bf16[1024,1536]{1,0:T(8,128)(2,1)}, bf16[1024,1536]{1,0:T(8,128)(2,1)S(1)}, u32[]{:S(2)}) copy-start(bf16[1024,1536]{1,0:T(8,128)(2,1)S(1)} %get-tuple-element.24) | copy-start | bytes 9437188
  90.9 6.5 %collective-permute-start.8 = (bf16[384,1536]{1,0:T(8,128)(2,1)S(1)}, bf16[384,1536]{1,0:T(8,128)(2,1)S(1)}, u32[]{:S(2)}, u32[]{:S(2)}) collective-permute-start(bf16[384,1536]{1,0:T(8,128)(2,1)S(1)} %get-tuple-element.25), channel_id=1, source_target_pairs={{0,32},{32,0},{1,33},{33,1},{2,34},{34,2},{3,35},{35,3},{4,36},{36... | collective-permute-start | bytes 3538952 | tf_op jit(solution)/shard_map/ppermute | solution.py:263
  93.2 28.9 %collective-permute-start.10 = (bf16[640,1536]{1,0:T(8,128)(2,1)}, bf16[640,1536]{1,0:T(8,128)(2,1)}, u32[]{:S(2)}, u32[]{:S(2)}) collective-permute-start(bf16[640,1536]{1,0:T(8,128)(2,1)} %get-tuple-element.29), channel_id=1, source_target_pairs={{0,32},{32,0},{1,33},{33,1},{2,34},{34,2},{3,35},{35,3},{4,36},{36... | collective-permute-start | bytes 5898248 | tf_op jit(solution)/shard_map/ppermute | solution.py:263
  97.4 13.1 %copy-start.2 = (bf16[256,2688]{1,0:T(8,128)(2,1)}, bf16[256,2688]{1,0:T(8,128)(2,1)S(1)}, u32[]{:S(2)}) copy-start(bf16[256,2688]{1,0:T(8,128)(2,1)S(1)} %back.1) | copy-start | bytes 4128772
  98.6 23.5 %collective-permute-start.9 = (bf16[256,1536]{1,0:T(8,128)(2,1)S(1)}, bf16[256,1536]{1,0:T(8,128)(2,1)S(1)}, u32[]{:S(2)}, u32[]{:S(2)}) collective-permute-start(bf16[256,1536]{1,0:T(8,128)(2,1)S(1)} %add_convert_fusion), channel_id=1, source_target_pairs={{0,448},{32,96},{64,0},{96,160},{128,64},{160,224},{192,128},{224,... | collective-permute-start | bytes 2359304 | tf_op jit(solution)/shard_map/ppermute | solution.py:259
  108.5 13.3 %collective-permute-start.13 = (bf16[128,1536]{1,0:T(8,128)(2,1)}, bf16[128,1536]{1,0:T(8,128)(2,1)S(1)}, u32[]{:S(2)}, u32[]{:S(2)}) collective-permute-start(bf16[128,1536]{1,0:T(8,128)(2,1)} %add_convert_fusion.6), channel_id=1, source_target_pairs={{0,64},{32,480},{64,128},{96,32},{128,192},{160,96},{192,256},{224... | collective-permute-start | bytes 1179656 | tf_op jit(solution)/shard_map/ppermute | solution.py:259
  110.5 50.5 %all-to-all-start.1 = ((bf16[32,8,2688]{2,1,0:T(8,128)(2,1)}), bf16[32,8,2688]{2,1,0:T(8,128)(2,1)S(1)}, u32[]{:S(2)}, u32[]{:S(2)}) async-start(bf16[32,8,2688]{2,1,0:T(8,128)(2,1)} %bitcast.13), calls=%async_computation.1 | async-start | bytes 2752512 | tf_op jit(solution)/shard_map/all_to_all | solution.py:352
  123.7 16.7 %collective-permute-start.11 = (bf16[128,1536]{1,0:T(8,128)(2,1)S(1)}, bf16[128,1536]{1,0:T(8,128)(2,1)S(1)}, u32[]{:S(2)}, u32[]{:S(2)}) collective-permute-start(bf16[128,1536]{1,0:T(8,128)(2,1)S(1)} %get-tuple-element.39), channel_id=1, source_target_pairs={{0,384},{32,160},{64,448},{96,224},{128,0},{160,288},{192,64},{224... | collective-permute-start | bytes 1179656 | tf_op jit(solution)/shard_map/ppermute | solution.py:259
  128.1 12.6 %collective-permute-start.14 = (bf16[128,1536]{1,0:T(8,128)(2,1)S(1)}, bf16[128,1536]{1,0:T(8,128)(2,1)S(1)}, u32[]{:S(2)}, u32[]{:S(2)}) collective-permute-start(bf16[128,1536]{1,0:T(8,128)(2,1)S(1)} %get-tuple-element.40), channel_id=1, source_target_pairs={{0,64},{32,480},{64,128},{96,32},{128,192},{160,96},{192,256},{224... | collective-permute-start | bytes 1179656 | tf_op jit(solution)/shard_map/ppermute | solution.py:259
  142.4 25.8 %copy-start.6 = (s32[8,128]{1,0:T(8,128)S(1)}, s32[8,128]{1,0:T(8,128)}, u32[]{:S(2)}) copy-start(s32[8,128]{1,0:T(8,128)} %get-tuple-element.33.places) | copy-start | bytes 12292
  142.4 25.8 %copy-start.7 = (s32[2]{0:T(128)S(1)}, s32[2]{0:T(128)}, u32[]{:S(2)}) copy-start(s32[2]{0:T(128)} %pad_add_fusion.place) | copy-start | bytes 28
  142.4 14.3 %collective-permute-start.12 = (bf16[128,1536]{1,0:T(8,128)(2,1)S(1)}, bf16[128,1536]{1,0:T(8,128)(2,1)S(1)}, u32[]{:S(2)}, u32[]{:S(2)}) collective-permute-start(bf16[128,1536]{1,0:T(8,128)(2,1)S(1)} %get-tuple-element.37), channel_id=1, source_target_pairs={{0,448},{32,96},{64,0},{96,160},{128,64},{160,224},{192,128},{224,... | collective-permute-start | bytes 1179656 | tf_op jit(solution)/shard_map/ppermute | solution.py:259
  148.8 10.9 %collective-permute-start.15 = (bf16[128,1536]{1,0:T(8,128)(2,1)S(1)}, bf16[128,1536]{1,0:T(8,128)(2,1)S(1)}, u32[]{:S(2)}, u32[]{:S(2)}) collective-permute-start(bf16[128,1536]{1,0:T(8,128)(2,1)S(1)} %get-tuple-element.38), channel_id=1, source_target_pairs={{0,64},{32,480},{64,128},{96,32},{128,192},{160,96},{192,256},{224... | collective-permute-start | bytes 1179656 | tf_op jit(solution)/shard_map/ppermute | solution.py:259
  161.0 20.8 %copy-start.8 = (s32[32]{0:T(128)S(1)}, s32[32]{0:T(128)}, u32[]{:S(2)}) copy-start(s32[32]{0:T(128)} %plan.1) | copy-start | bytes 388
  161.8 20.0 %all-to-all-start.2 = ((bf16[32,4,1536]{2,1,0:T(4,128)(2,1)}), bf16[32,4,1536]{2,1,0:T(4,128)(2,1)S(1)}, u32[]{:S(2)}, u32[]{:S(2)}) async-start(bf16[32,4,1536]{2,1,0:T(4,128)(2,1)} %reshape.17), calls=%async_computation.2 | async-start | bytes 786432 | tf_op jit(solution)/shard_map/all_to_all | solution.py:365

commit v3 on v2

--- a/solution.py
+++ b/solution.py
@@ -43,23 +43,27 @@
 
 def feature_blocks(place, chips):
     blocks = []
-    for core in (place[1], 1 - place[1]):
+    z, mine = place[0][0], place[1][0]
+    for core in (mine, 1 - mine):
         for shift in ORDER:
-            chip = lax.rem(place[0] + (1 - 2 * core) * shift + chips, chips)
+            chip = lax.rem(z + (1 - 2 * core) * shift + chips, chips)
             blocks.append(pl.ds(pl.multiple_of((2 * chip + core) * LANES, LANES), LANES))
     return blocks
 
 
-def pack_kernel(place, routes, gates, plan, failed, tokens_in, grads_in, sent, places, tokens, grads):
-    tok_count, width = tokens.shape
+def pack_kernel(
+    z, core, routes, gates, plan, failed, tokens_in, grads_in, sent, places, *scratch
+):
+    whole_in, whole, packed, in_sems, out_sems = scratch
+    tok_count, width = tokens_in.shape
     slots = plan.shape[1]
     half = width // 2
     rows = slots * MAIN
-    for j, block in enumerate(feature_blocks(place, width // (2 * LANES))):
-        cols = slice(j * LANES, (j + 1) * LANES)
-        tokens[:, cols] = tokens_in[:, block]
-        grads[:, cols] = grads_in[:, block]
-    in_group = iota(failed.shape, 0) == 2 * place[0] + place[1]
+    loads = []
+    for i, ref in enumerate((tokens_in, grads_in)):
+        loads.append(pltpu.make_async_copy(ref, whole_in.at[i], in_sems.at[i]))
+        loads[i].start()
+    in_group = iota(failed.shape, 0) == 2 * z[0] + core[0]
     dead = jnp.sum(jnp.where(in_group, failed[...], 0), axis=0, keepdims=True)
     hosting = jnp.where(dead == 0, plan[...], -1)
     diagonal = iota((slots, slots), 0) == iota((slots, slots), 1)
@@ -103,14 +107,26 @@
     def pick_rows(at, shift=0):
         return one_hot((at[0] + shift == row_ids) | (at[1] + shift == row_ids))
 
-    whole = pick_rows(main)
-    sent[:, :width] = mm(whole, tokens[...]).astype(BF)
-    sent[:, width : 2 * width] = mm(whole, grads[...]).astype(BF)
-    cut = mm(pick_rows(rest), tokens[:, :half])
-    cut += mm(pick_rows(rest, 4), tokens[:, half:])
-    cut += mm(pick_rows(rest, 2), grads[:, :half])
-    cut += mm(pick_rows(rest, 6), grads[:, half:])
-    sent[:, 2 * width : 2 * width + half] = cut.astype(BF)
+    stores = []
+
+    def store(i, at):
+        stores.append(pltpu.make_async_copy(packed.at[:, at], sent.at[:, at], out_sems.at[i]))
+        stores[i].start()
+
+    blocks = feature_blocks((z, core), width // (2 * LANES))
+    picked = pick_rows(main)
+    for i in range(2):
+        loads[i].wait()
+        for j, block in enumerate(blocks):
+            whole[i, :, j * LANES : (j + 1) * LANES] = whole_in[i, :, block]
+        at = slice(i * width, (i + 1) * width)
+        packed[:, at] = mm(picked, whole[i]).astype(BF)
+        store(i, at)
+    cut = mm(pick_rows(rest), whole[0, :, :half])
+    cut += mm(pick_rows(rest, 4), whole[0, :, half:])
+    cut += mm(pick_rows(rest, 2), whole[1, :, :half])
+    cut += mm(pick_rows(rest, 6), whole[1, :, half:])
+    packed[:, 2 * width : 2 * width + half] = cut.astype(BF)
     lane_ids = iota((LANES, tok_count), 0)
     gate_rows = jnp.zeros((rows, LANES), F32)
     for k in range(2):
@@ -119,7 +135,10 @@
         second = jnp.where(lane_ids == 1, gate, 0.0).astype(BF)
         gate_rows += mm(one_hot(main[k] == row_ids), first, NT)
         gate_rows += mm(one_hot(rest[k] == row_ids), second, NT)
-    sent[:, 2 * width + half :] = gate_rows.astype(BF)
+    packed[:, 2 * width + half :] = gate_rows.astype(BF)
+    store(2, slice(2 * width, packed.shape[1]))
+    for copy in stores:
+        copy.wait()
 
 
 def stack_kernel(*refs):
@@ -141,7 +160,8 @@
     )(*blocks)
 
 
-def slot_kernel(got, w0, w1, w2, w3, mine, first, later, pre_out, gate_out, x_all, dy_all):
+def slot_kernel(got_in, w0, w1, w2, w3, mine, first, later, pre_out, gate_out, *scratch):
+    x_all, dy_all, got, weights, sems = scratch
     rows = got.shape[0]
     hidden_width = w0.shape[1] // 3
     half = w0.shape[0] + w1.shape[0]
@@ -150,11 +170,24 @@
     source = iota((extra, rows), 0)
     base = source // 2 * MAIN + source % 2
     column = iota((extra, rows), 1)
+    loads = []
+    for at in (slice(2 * width, got.shape[1]), slice(0, width), slice(width, 2 * width)):
+        loads.append((got_in.at[:, at], got.at[:, at]))
+    at = 0
+    for w in (w0, w1, w2, w3):
+        loads.append((w, weights.at[at : at + w.shape[0]]))
+        at += w.shape[0]
+    loads = [pltpu.make_async_copy(a, b, sems.at[i]) for i, (a, b) in enumerate(loads)]
+    for load in loads:
+        load.start()
+    loads[0].wait()
     cut = got[:, 2 * width : 2 * width + half]
     head = one_hot(column == base)
-    x_all[:rows] = got[:, :width]
     x_all[rows:, :half] = mm(head, cut).astype(BF)
     x_all[rows:, half:] = mm(one_hot(column == base + 4), cut).astype(BF)
+    loads[1].wait()
+    x_all[:rows] = got[:, :width]
+    loads[2].wait()
     dy_all[:rows] = got[:, width : 2 * width]
     dy_all[rows:, :half] = mm(one_hot(column == base + 2), cut).astype(BF)
     dy_all[rows:, half:] = mm(one_hot(column == base + 6), cut).astype(BF)
@@ -164,12 +197,10 @@
     )
     wide = slice(0, 2 * hidden_width)
     down = slice(2 * hidden_width, 3 * hidden_width)
-    pre, upstream, at = 0.0, 0.0, 0
-    for w in (w0, w1, w2, w3):
-        cols = slice(at, at + w.shape[0])
-        pre += mm(x_all[:, cols], w[:, wide])
-        upstream += mm(dy_all[:, cols], w[:, down])
-        at += w.shape[0]
+    for load in loads[3:]:
+        load.wait()
+    pre = mm(x_all[...], weights[:, wide])
+    upstream = mm(dy_all[...], weights[:, down])
     a = pre[:, :hidden_width]
     b = pre[:, hidden_width:]
     sig = jax.nn.sigmoid(a)
@@ -218,7 +249,7 @@
     back[:, width + quarter :] = jnp.where(lane < 2, gate_rows, 0.0).astype(BF)
 
 
-def join_kernel(place, back, places, token_grad, gate_grad):
+def join_kernel(z, core, back, places, token_grad, gate_grad):
     tok_count, width = token_grad.shape
     rows = back.shape[0]
     quarter = width // 4
@@ -227,7 +258,7 @@
     rest = [places[2 + k : 3 + k, :] for k in range(2)]
     whole = one_hot((main[0] == row_ids) | (main[1] == row_ids))
     cut = back[:, width : width + quarter]
-    blocks = feature_blocks(place, width // (2 * LANES))
+    blocks = feature_blocks((z, core), width // (2 * LANES))
     for h in range(4):
         cols = slice(h * quarter, (h + 1) * quarter)
         here = one_hot((rest[0] + 2 * h == row_ids) | (rest[1] + 2 * h == row_ids))
@@ -276,7 +307,8 @@
     each = width // (groups * slots)
     smem = pl.BlockSpec(memory_space=pltpu.SMEM)
     vmem = pl.BlockSpec(memory_space=pltpu.VMEM)
-    place = jnp.stack([lax.axis_index("z"), lax.axis_index("core")])
+    anywhere = pl.BlockSpec(memory_space=pl.ANY)
+    place = [lax.axis_index(name).reshape(1) for name in ("z", "core")]
 
     sent, places = call(
         pack_kernel,
@@ -286,10 +318,17 @@
         ),
         "pack",
         56,
-        in_specs=[smem] + [vmem] * 6,
-        scratch_shapes=[pltpu.VMEM((tok_count, width), BF)] * 2,
+        in_specs=[smem] * 2 + [vmem] * 4 + [anywhere] * 2,
+        out_specs=(anywhere, vmem),
+        scratch_shapes=[
+            pltpu.VMEM((2, tok_count, width), BF),
+            pltpu.VMEM((2, tok_count, width), BF),
+            pltpu.VMEM((rows, 2 * width + width // 2 + LANES), BF),
+            pltpu.SemaphoreType.DMA((2,)),
+            pltpu.SemaphoreType.DMA((3,)),
+        ],
     )(
-        place,
+        *place,
         routes.T,
         gates.T,
         plan.reshape(1, slots),
@@ -318,10 +357,26 @@
         ),
         "slot",
         32,
-        in_specs=[vmem] * 5,
-        scratch_shapes=[pltpu.VMEM((total, width), BF)] * 2,
+        in_specs=[anywhere] * 5,
+        scratch_shapes=[
+            pltpu.VMEM((total, width), BF),
+            pltpu.VMEM((total, width), BF),
+            pltpu.VMEM(sent.shape, BF),
+            pltpu.VMEM((width, columns), BF),
+            pltpu.SemaphoreType.DMA((7,)),
+        ],
     )(got, *w_all)
     first, later = swap(first), swap(later)
+
+    def both(j, n=1):
+        theirs, at = (first, j) if j < FIRST else (later, j - FIRST)
+        return (
+            mine[j * part : (j + n) * part].astype(F32)
+            + theirs[at * part : (at + n) * part].astype(F32)
+        )
+
+    minus, plus = both(0, 2).astype(BF), both(2).astype(BF)
+    minus, plus, pre_grad = lax.optimization_barrier((minus, plus, pre_grad))
     back = call(
         back_kernel,
         jax.ShapeDtypeStruct((rows, width + width // 4 + LANES), BF),
@@ -330,16 +385,6 @@
         in_specs=[vmem] * 6,
         scratch_shapes=[pltpu.VMEM((total - rows, width), BF)],
     )(pre_grad, gate_rows, *w_all)
-
-    def both(j, n=1):
-        theirs, at = (first, j) if j < FIRST else (later, j - FIRST)
-        return (
-            mine[j * part : (j + n) * part].astype(F32)
-            + theirs[at * part : (at + n) * part].astype(F32)
-        )
-
-    minus, plus = both(0, 2).astype(BF), both(2).astype(BF)
-    minus, plus, back = lax.optimization_barrier((minus, plus, back))
     minus, plus = move(minus, -1), move(plus, 1)
     far_sum = (minus[:part].astype(F32) + both(3)).astype(BF)
     plus = (plus.astype(F32) + both(4)).astype(BF)
@@ -359,8 +404,8 @@
         ),
         "join",
         16,
-        in_specs=[smem, vmem, vmem],
-    )(place, back, places)
+        in_specs=[smem, smem, vmem, vmem],
+    )(*place, back, places)
     owned = owned.reshape(slots, each, columns)
     mixed = lax.all_to_all(owned, "ep", split_axis=0, concat_axis=0, tiled=True)
     weight_grad = call(

time: 184 us -> 184 us (level)
  waiting for transfers between devices: 59.5 us -> 57.6 us
    ppermute x12, waiting for transfers between devices: 45.4 us -> 42.5 us  [move(): return lax.ppermute(array, ('z', 'core'), pairs)]
    unnamed x22 -> x20, local copies, waits for them, and re-layouts: 5.23 us -> 6.42 us
  transfers between devices with their start and end apart: 19 -> 19, of which waited for: 12 -> 13; matrix products, arithmetic and copies ran while one was open for 3% -> 4% of each run, Pallas kernels for 2% -> 2%
where the time goes in v3:
time: 184 us; the launch traced here: 183 us
  starting transfers between devices  92.3 us (50%)
  waiting for transfers between devices  57.6 us (31%)
  Pallas kernels  18.3 us (10%)
  local copies, waits for them, and re-layouts  7.27 us (4%)
  other arithmetic  6.79 us (4%)
    ppermute x12, starting transfers between devices, move(): return lax.ppermute(array, ('z', 'core'), pairs)  58.9 us
    ppermute x12, waiting for transfers between devices, move(): return lax.ppermute(array, ('z', 'core'), pairs)  42.5 us
    all_to_all x1, waiting for transfers between devices, local(): mixed = lax.all_to_all(owned, 'ep', split_axis=0, concat_axis=0, tiled=True)  12.2 us
    all_to_all x1, starting transfers between devices, local(): got = lax.all_to_all(sent, 'ep', split_axis=0, concat_axis=0, tiled=True)  10.4 us
    ppermute x4, starting transfers between devices, swap(): return lax.ppermute(array, 'core', [(0, 1), (1, 0)])  9.17 us
    pallas_call x1, Pallas kernels, local(): call(slot_kernel, (jax.ShapeDtypeStruct((width // 2, columns), BF), jax.S...  8.1 us
    all_to_all x1, starting transfers between devices, local(): mixed = lax.all_to_all(owned, 'ep', split_axis=0, concat_axis=0, tiled=True)  7.4 us
    all_to_all x1, starting transfers between devices, local(): back = lax.all_to_all(back, 'ep', split_axis=0, concat_axis=0, tiled=True)  6.45 us
  transfers between devices with their start and end apart: 19, of which 13 were waited for; matrix products, arithmetic and copies ran while one was open for 4% of the time, Pallas kernels for 2%

profile of v3, /device:TPU:8, one launch (start us, length us, event | category | flops | bytes accessed | tf_op | source)
XLA Modules:
  0.0 183.2 jit_solution(15574226889760417069)
XLA Ops:
  0.6 4.9 %pack.1 = (bf16[256,5248]{1,0:T(8,128)(2,1)}, s32[8,128]{1,0:T(8,128)}) custom-call(s32[1]{0:T(128)} %bitcast.z, s32[1]{0:T(128)} %bitcast.1.core, s32[2,128]{1,0:T(2,128)} %bitcast.18, bf16[2,128]{1,0:T(2,128)(2,1)} %bitcast.19, s32[1,32]{1,0:T(1,128)} %bitcast.14, s32[16,32]{1,0:T(8,128)} %failed.1, bf16[128,2048]{1,0:T(8,128)(2,1)} %tokens_in.1, ...), custom_call_target="tpu_custom_call" | custom-call | tf_op jit(solution)/shard_map/pack/pallas_call | solution.py:313
  5.6 10.4 %all-to-all-start = ((bf16[32,8,5248]{2,1,0:T(8,128)(2,1)}), bf16[32,8,5248]{2,1,0:T(8,128)(2,1)}, u32[]{:S(2)}, u32[]{:S(2)}) async-start(bf16[32,8,5248]{2,1,0:T(8,128)(2,1)} %bitcast.15), calls=%async_computation | async-start | bytes 5373952 | tf_op jit(solution)/shard_map/all_to_all | solution.py:340
  16.0 4.2 %collective-permute-start = (bf16[128,1536]{1,0:T(8,128)(2,1)S(1)}, bf16[128,1536]{1,0:T(8,128)(2,1)S(1)}, u32[]{:S(2)}, u32[]{:S(2)}) collective-permute-start(bf16[128,1536]{1,0:T(8,128)(2,1)S(1)} %pad_maximum_fusion.refs_4_), channel_id=1, source_target_pairs={{0,64},{32,480},{64,128},{96,32},{128,192},{160,96},{192,256},{224... | collective-permute-start | bytes 1179656 | tf_op jit(solution)/shard_map/ppermute | solution.py:290
  20.3 8.6 %collective-permute-start.3 = (bf16[128,1536]{1,0:T(8,128)(2,1)S(1)}, bf16[128,1536]{1,0:T(8,128)(2,1)S(1)}, u32[]{:S(2)}, u32[]{:S(2)}) collective-permute-start(bf16[128,1536]{1,0:T(8,128)(2,1)S(1)} %pad_maximum_fusion.refs_4_), channel_id=1, source_target_pairs={{0,448},{32,96},{64,0},{96,160},{128,64},{160,224},{192,128},{224,... | collective-permute-start | bytes 1179656 | tf_op jit(solution)/shard_map/ppermute | solution.py:290
  28.9 4.8 %collective-permute-done.refs_1_.refs_2_ = bf16[128,1536]{1,0:T(8,128)(2,1)S(1)} collective-permute-done((bf16[128,1536]{1,0:T(8,128)(2,1)S(1)}, bf16[128,1536]{1,0:T(8,128)(2,1)S(1)}, u32[]{:S(2)}, u32[]{:S(2)}) %collective-permute-start) | collective-permute-done | bytes 393248 | tf_op jit(solution)/shard_map/ppermute | solution.py:290
  33.6 2.0 %collective-permute-start.1 = (bf16[128,1536]{1,0:T(8,128)(2,1)S(1)}, bf16[128,1536]{1,0:T(8,128)(2,1)S(1)}, u32[]{:S(2)}, u32[]{:S(2)}) collective-permute-start(bf16[128,1536]{1,0:T(8,128)(2,1)S(1)} %collective-permute-done.refs_1_.refs_2_), channel_id=1, source_target_pairs={{0,128},{32,416},{64,192},{96,480},{128,256},{160,32},{192,320},{2... | collective-permute-start | bytes 1179656 | tf_op jit(solution)/shard_map/ppermute | solution.py:290
  35.7 6.6 %collective-permute-start.4 = (bf16[128,1536]{1,0:T(8,128)(2,1)S(1)}, bf16[128,1536]{1,0:T(8,128)(2,1)S(1)}, u32[]{:S(2)}, u32[]{:S(2)}) collective-permute-start(bf16[128,1536]{1,0:T(8,128)(2,1)S(1)} %collective-permute-done.3.refs_3_), channel_id=1, source_target_pairs={{0,448},{32,96},{64,0},{96,160},{128,64},{160,224},{192,128},{224,... | collective-permute-start | bytes 1179656 | tf_op jit(solution)/shard_map/ppermute | solution.py:290
  42.3 9.1 %collective-permute-done.1.refs_0_ = bf16[128,1536]{1,0:T(8,128)(2,1)S(1)} collective-permute-done((bf16[128,1536]{1,0:T(8,128)(2,1)S(1)}, bf16[128,1536]{1,0:T(8,128)(2,1)S(1)}, u32[]{:S(2)}, u32[]{:S(2)}) %collective-permute-start.1) | collective-permute-done | bytes 393248 | tf_op jit(solution)/shard_map/ppermute | solution.py:290
  51.5 6.3 %collective-permute-start.2 = (bf16[256,1536]{1,0:T(8,128)(2,1)S(1)}, bf16[256,1536]{1,0:T(8,128)(2,1)S(1)}, u32[]{:S(2)}, u32[]{:S(2)}) collective-permute-start(bf16[256,1536]{1,0:T(8,128)(2,1)S(1)} %stack.3), channel_id=1, source_target_pairs={{0,64},{32,480},{64,128},{96,32},{128,192},{160,96},{192,256},{224... | collective-permute-start | bytes 2359304 | tf_op jit(solution)/shard_map/ppermute | solution.py:290
  58.0 1.9 %collective-permute-start.7 = (bf16[640,1536]{1,0:T(8,128)(2,1)S(1)}, bf16[640,1536]{1,0:T(8,128)(2,1)S(1)}, u32[]{:S(2)}, u32[]{:S(2)}) collective-permute-start(bf16[640,1536]{1,0:T(8,128)(2,1)S(1)} %stack.5.w1), channel_id=1, source_target_pairs={{0,32},{32,0},{1,33},{33,1},{2,34},{34,2},{3,35},{35,3},{4,36},{36... | collective-permute-start | bytes 5898248 | tf_op jit(solution)/shard_map/ppermute | solution.py:294
  59.9 2.2 %collective-permute-start.5 = (bf16[128,1536]{1,0:T(8,128)(2,1)S(1)}, bf16[128,1536]{1,0:T(8,128)(2,1)S(1)}, u32[]{:S(2)}, u32[]{:S(2)}) collective-permute-start(bf16[128,1536]{1,0:T(8,128)(2,1)S(1)} %collective-permute-done.4.refs_1_), channel_id=1, source_target_pairs={{0,448},{32,96},{64,0},{96,160},{128,64},{160,224},{192,128},{224,... | collective-permute-start | bytes 1179656 | tf_op jit(solution)/shard_map/ppermute | solution.py:290
  62.2 7.4 %collective-permute-done.5.refs_1_ = bf16[128,1536]{1,0:T(8,128)(2,1)S(1)} collective-permute-done((bf16[128,1536]{1,0:T(8,128)(2,1)S(1)}, bf16[128,1536]{1,0:T(8,128)(2,1)S(1)}, u32[]{:S(2)}, u32[]{:S(2)}) %collective-permute-start.5) | collective-permute-done | bytes 393248 | tf_op jit(solution)/shard_map/ppermute | solution.py:290
  69.6 2.0 %collective-permute-done.2.refs_0_ = bf16[256,1536]{1,0:T(8,128)(2,1)S(1)} collective-permute-done((bf16[256,1536]{1,0:T(8,128)(2,1)S(1)}, bf16[256,1536]{1,0:T(8,128)(2,1)S(1)}, u32[]{:S(2)}, u32[]{:S(2)}) %collective-permute-start.2) | collective-permute-done | bytes 786464 | tf_op jit(solution)/shard_map/ppermute | solution.py:290
  71.6 2.9 %collective-permute-start.6 = (bf16[384,1536]{1,0:T(8,128)(2,1)S(1)}, bf16[384,1536]{1,0:T(8,128)(2,1)S(1)}, u32[]{:S(2)}, u32[]{:S(2)}) collective-permute-start(bf16[384,1536]{1,0:T(8,128)(2,1)S(1)} %stack.4.w0), channel_id=1, source_target_pairs={{0,32},{32,0},{1,33},{33,1},{2,34},{34,2},{3,35},{35,3},{4,36},{36... | collective-permute-start | bytes 3538952 | tf_op jit(solution)/shard_map/ppermute | solution.py:294
  74.6 2.5 %collective-permute-done.6.w2 = bf16[384,1536]{1,0:T(8,128)(2,1)S(1)} collective-permute-done((bf16[384,1536]{1,0:T(8,128)(2,1)S(1)}, bf16[384,1536]{1,0:T(8,128)(2,1)S(1)}, u32[]{:S(2)}, u32[]{:S(2)}) %collective-permute-start.6) | collective-permute-done | bytes 1179680 | tf_op jit(solution)/shard_map/ppermute | solution.py:294
  82.3 8.1 %slot.1 = (bf16[1024,1536]{1,0:T(8,128)(2,1)S(1)}, bf16[384,1536]{1,0:T(8,128)(2,1)S(1)}, bf16[640,1536]{1,0:T(8,128)(2,1)}, bf16[320,1024]{1,0:T(8,128)(2,1)S(1)}, bf16[320,128]{1,0:T(8,128)(2,1)S(1)}) custom-call(bf16[256,5248]{1,0:T(8,128)(2,1)} %bitcast.6.got_in, bf16[384,1536]{1,0:T(8,128)(2,1)S(1)} %stack.4.w0, bf16[640,1536]{1,0:T(8,128)(2,1)S(1)} %stack.5.w1, ...), custom_call_target="tpu_custom_call" | custom-call | tf_op jit(solution)/shard_map/slot/pallas_call | solution.py:349
  90.4 2.3 %collective-permute-start.8 = (bf16[384,1536]{1,0:T(8,128)(2,1)S(1)}, bf16[384,1536]{1,0:T(8,128)(2,1)S(1)}, u32[]{:S(2)}, u32[]{:S(2)}) collective-permute-start(bf16[384,1536]{1,0:T(8,128)(2,1)S(1)} %get-tuple-element.25), channel_id=1, source_target_pairs={{0,32},{32,0},{1,33},{33,1},{2,34},{34,2},{3,35},{35,3},{4,36},{36... | collective-permute-start | bytes 3538952 | tf_op jit(solution)/shard_map/ppermute | solution.py:294
  92.7 2.0 %collective-permute-start.10 = (bf16[640,1536]{1,0:T(8,128)(2,1)}, bf16[640,1536]{1,0:T(8,128)(2,1)}, u32[]{:S(2)}, u32[]{:S(2)}) collective-permute-start(bf16[640,1536]{1,0:T(8,128)(2,1)} %get-tuple-element.28), channel_id=1, source_target_pairs={{0,32},{32,0},{1,33},{33,1},{2,34},{34,2},{3,35},{35,3},{4,36},{36... | collective-permute-start | bytes 5898248 | tf_op jit(solution)/shard_map/ppermute | solution.py:294
  97.0 9.8 %collective-permute-start.9 = (bf16[256,1536]{1,0:T(8,128)(2,1)}, bf16[256,1536]{1,0:T(8,128)(2,1)}, u32[]{:S(2)}, u32[]{:S(2)}) collective-permute-start(bf16[256,1536]{1,0:T(8,128)(2,1)} %add_convert_fusion), channel_id=1, source_target_pairs={{0,448},{32,96},{64,0},{96,160},{128,64},{160,224},{192,128},{224,... | collective-permute-start | bytes 2359304 | tf_op jit(solution)/shard_map/ppermute | solution.py:290
  106.8 2.1 %collective-permute-start.13 = (bf16[128,1536]{1,0:T(8,128)(2,1)}, bf16[128,1536]{1,0:T(8,128)(2,1)S(1)}, u32[]{:S(2)}, u32[]{:S(2)}) collective-permute-start(bf16[128,1536]{1,0:T(8,128)(2,1)} %add_convert_fusion.6), channel_id=1, source_target_pairs={{0,64},{32,480},{64,128},{96,32},{128,192},{160,96},{192,256},{224... | collective-permute-start | bytes 1179656 | tf_op jit(solution)/shard_map/ppermute | solution.py:290
  108.9 2.2 %back.1 = bf16[256,2688]{1,0:T(8,128)(2,1)S(1)} custom-call(bf16[320,1024]{1,0:T(8,128)(2,1)S(1)} %get-tuple-element.30.pre_grad, bf16[320,128]{1,0:T(8,128)(2,1)S(1)} %get-tuple-element.31.gate_grad, bf16[384,1536]{1,0:T(8,128)(2,1)S(1)} %stack.4.w0, bf16[640,1536]{1,0:T(8,128)(2,1)S(1)} %stack.5.w1, bf16[384,1536]{1,0:T(8,128)(2,1)S(1)} %copy-done.4, ...), custom_call_target="tpu_custom_call" | custom-call | tf_op jit(solution)/shard_map/back/pallas_call | solution.py:380
  112.3 6.5 %all-to-all-start.1 = ((bf16[32,8,2688]{2,1,0:T(8,128)(2,1)}), bf16[32,8,2688]{2,1,0:T(8,128)(2,1)S(1)}, u32[]{:S(2)}, u32[]{:S(2)}) async-start(bf16[32,8,2688]{2,1,0:T(8,128)(2,1)} %bitcast.13), calls=%async_computation.1 | async-start | bytes 2752512 | tf_op jit(solution)/shard_map/all_to_all | solution.py:397
  118.7 1.9 %collective-permute-done.13 = bf16[128,1536]{1,0:T(8,128)(2,1)S(1)} collective-permute-done((bf16[128,1536]{1,0:T(8,128)(2,1)}, bf16[128,1536]{1,0:T(8,128)(2,1)S(1)}, u32[]{:S(2)}, u32[]{:S(2)}) %collective-permute-start.13) | collective-permute-done | bytes 393248 | tf_op jit(solution)/shard_map/ppermute | solution.py:290
  122.6 4.4 %collective-permute-start.11 = (bf16[128,1536]{1,0:T(8,128)(2,1)S(1)}, bf16[128,1536]{1,0:T(8,128)(2,1)S(1)}, u32[]{:S(2)}, u32[]{:S(2)}) collective-permute-start(bf16[128,1536]{1,0:T(8,128)(2,1)S(1)} %get-tuple-element.39), channel_id=1, source_target_pairs={{0,384},{32,160},{64,448},{96,224},{128,0},{160,288},{192,64},{224... | collective-permute-start | bytes 1179656 | tf_op jit(solution)/shard_map/ppermute | solution.py:290
  126.9 4.6 %collective-permute-start.14 = (bf16[128,1536]{1,0:T(8,128)(2,1)S(1)}, bf16[128,1536]{1,0:T(8,128)(2,1)S(1)}, u32[]{:S(2)}, u32[]{:S(2)}) collective-permute-start(bf16[128,1536]{1,0:T(8,128)(2,1)S(1)} %get-tuple-element.40), channel_id=1, source_target_pairs={{0,64},{32,480},{64,128},{96,32},{128,192},{160,96},{192,256},{224... | collective-permute-start | bytes 1179656 | tf_op jit(solution)/shard_map/ppermute | solution.py:290
  131.5 7.5 %collective-permute-done.11 = bf16[128,1536]{1,0:T(8,128)(2,1)S(1)} collective-permute-done((bf16[128,1536]{1,0:T(8,128)(2,1)S(1)}, bf16[128,1536]{1,0:T(8,128)(2,1)S(1)}, u32[]{:S(2)}, u32[]{:S(2)}) %collective-permute-start.11) | collective-permute-done | bytes 393248 | tf_op jit(solution)/shard_map/ppermute | solution.py:290
  141.5 6.1 %collective-permute-start.12 = (bf16[128,1536]{1,0:T(8,128)(2,1)S(1)}, bf16[128,1536]{1,0:T(8,128)(2,1)S(1)}, u32[]{:S(2)}, u32[]{:S(2)}) collective-permute-start(bf16[128,1536]{1,0:T(8,128)(2,1)S(1)} %get-tuple-element.37), channel_id=1, source_target_pairs={{0,448},{32,96},{64,0},{96,160},{128,64},{160,224},{192,128},{224,... | collective-permute-start | bytes 1179656 | tf_op jit(solution)/shard_map/ppermute | solution.py:290
  147.7 1.9 %collective-permute-start.15 = (bf16[128,1536]{1,0:T(8,128)(2,1)S(1)}, bf16[128,1536]{1,0:T(8,128)(2,1)S(1)}, u32[]{:S(2)}, u32[]{:S(2)}) collective-permute-start(bf16[128,1536]{1,0:T(8,128)(2,1)S(1)} %get-tuple-element.38), channel_id=1, source_target_pairs={{0,64},{32,480},{64,128},{96,32},{128,192},{160,96},{192,256},{224... | collective-permute-start | bytes 1179656 | tf_op jit(solution)/shard_map/ppermute | solution.py:290
  149.6 6.0 %collective-permute-done.12 = bf16[128,1536]{1,0:T(8,128)(2,1)S(1)} collective-permute-done((bf16[128,1536]{1,0:T(8,128)(2,1)S(1)}, bf16[128,1536]{1,0:T(8,128)(2,1)S(1)}, u32[]{:S(2)}, u32[]{:S(2)}) %collective-permute-start.12) | collective-permute-done | bytes 393248 | tf_op jit(solution)/shard_map/ppermute | solution.py:290
  155.6 2.9 %collective-permute-done.15 = bf16[128,1536]{1,0:T(8,128)(2,1)S(1)} collective-permute-done((bf16[128,1536]{1,0:T(8,128)(2,1)S(1)}, bf16[128,1536]{1,0:T(8,128)(2,1)S(1)}, u32[]{:S(2)}, u32[]{:S(2)}) %collective-permute-start.15) | collective-permute-done | bytes 393248 | tf_op jit(solution)/shard_map/ppermute | solution.py:290
  160.7 7.4 %all-to-all-start.2 = ((bf16[32,4,1536]{2,1,0:T(4,128)(2,1)}), bf16[32,4,1536]{2,1,0:T(4,128)(2,1)S(1)}, u32[]{:S(2)}, u32[]{:S(2)}) async-start(bf16[32,4,1536]{2,1,0:T(4,128)(2,1)} %reshape.25), calls=%async_computation.2 | async-start | bytes 786432 | tf_op jit(solution)/shard_map/all_to_all | solution.py:410
  169.5 12.2 %all-to-all-done.2.mixed = bf16[32,4,1536]{2,1,0:T(4,128)(2,1)S(1)} async-done(((bf16[32,4,1536]{2,1,0:T(4,128)(2,1)}), bf16[32,4,1536]{2,1,0:T(4,128)(2,1)S(1)}, u32[]{:S(2)}, u32[]{:S(2)}) %all-to-all-start.2) | async-done | bytes 393248 | tf_op jit(solution)/shard_map/all_to_all | solution.py:410
  (41 shorter events, 18.5 us)
Async XLA Ops:
  5.5 10.4 %copy-start.8 = (bf16[1,128,1024]{2,1,0:T(8,128)(2,1)S(1)}, bf16[1,128,1024]{2,1,0:T(8,128)(2,1)}, u32[]{:S(2)}) copy-start(bf16[1,128,1024]{2,1,0:T(8,128)(2,1)} %param.12) | copy-start | bytes 786436
  5.5 10.4 %copy-start.9 = (bf16[1,128,512]{2,1,0:T(8,128)(2,1)S(1)}, bf16[1,128,512]{2,1,0:T(8,128)(2,1)}, u32[]{:S(2)}) copy-start(bf16[1,128,512]{2,1,0:T(8,128)(2,1)} %param.13) | copy-start | bytes 393220
  5.6 73.9 %all-to-all-start = ((bf16[32,8,5248]{2,1,0:T(8,128)(2,1)}), bf16[32,8,5248]{2,1,0:T(8,128)(2,1)}, u32[]{:S(2)}, u32[]{:S(2)}) async-start(bf16[32,8,5248]{2,1,0:T(8,128)(2,1)} %bitcast.15), calls=%async_computation | async-start | bytes 5373952 | tf_op jit(solution)/shard_map/all_to_all | solution.py:340
  16.0 17.6 %collective-permute-start = (bf16[128,1536]{1,0:T(8,128)(2,1)S(1)}, bf16[128,1536]{1,0:T(8,128)(2,1)S(1)}, u32[]{:S(2)}, u32[]{:S(2)}) collective-permute-start(bf16[128,1536]{1,0:T(8,128)(2,1)S(1)} %pad_maximum_fusion.refs_4_), channel_id=1, source_target_pairs={{0,64},{32,480},{64,128},{96,32},{128,192},{160,96},{192,256},{224... | collective-permute-start | bytes 1179656 | tf_op jit(solution)/shard_map/ppermute | solution.py:290
  20.3 15.4 %collective-permute-start.3 = (bf16[128,1536]{1,0:T(8,128)(2,1)S(1)}, bf16[128,1536]{1,0:T(8,128)(2,1)S(1)}, u32[]{:S(2)}, u32[]{:S(2)}) collective-permute-start(bf16[128,1536]{1,0:T(8,128)(2,1)S(1)} %pad_maximum_fusion.refs_4_), channel_id=1, source_target_pairs={{0,448},{32,96},{64,0},{96,160},{128,64},{160,224},{192,128},{224,... | collective-permute-start | bytes 1179656 | tf_op jit(solution)/shard_map/ppermute | solution.py:290
  33.6 17.8 %collective-permute-start.1 = (bf16[128,1536]{1,0:T(8,128)(2,1)S(1)}, bf16[128,1536]{1,0:T(8,128)(2,1)S(1)}, u32[]{:S(2)}, u32[]{:S(2)}) collective-permute-start(bf16[128,1536]{1,0:T(8,128)(2,1)S(1)} %collective-permute-done.refs_1_.refs_2_), channel_id=1, source_target_pairs={{0,128},{32,416},{64,192},{96,480},{128,256},{160,32},{192,320},{2... | collective-permute-start | bytes 1179656 | tf_op jit(solution)/shard_map/ppermute | solution.py:290
  35.7 22.2 %collective-permute-start.4 = (bf16[128,1536]{1,0:T(8,128)(2,1)S(1)}, bf16[128,1536]{1,0:T(8,128)(2,1)S(1)}, u32[]{:S(2)}, u32[]{:S(2)}) collective-permute-start(bf16[128,1536]{1,0:T(8,128)(2,1)S(1)} %collective-permute-done.3.refs_3_), channel_id=1, source_target_pairs={{0,448},{32,96},{64,0},{96,160},{128,64},{160,224},{192,128},{224,... | collective-permute-start | bytes 1179656 | tf_op jit(solution)/shard_map/ppermute | solution.py:290
  51.5 20.1 %collective-permute-start.2 = (bf16[256,1536]{1,0:T(8,128)(2,1)S(1)}, bf16[256,1536]{1,0:T(8,128)(2,1)S(1)}, u32[]{:S(2)}, u32[]{:S(2)}) collective-permute-start(bf16[256,1536]{1,0:T(8,128)(2,1)S(1)} %stack.3), channel_id=1, source_target_pairs={{0,64},{32,480},{64,128},{96,32},{128,192},{160,96},{192,256},{224... | collective-permute-start | bytes 2359304 | tf_op jit(solution)/shard_map/ppermute | solution.py:290
  58.0 20.1 %collective-permute-start.7 = (bf16[640,1536]{1,0:T(8,128)(2,1)S(1)}, bf16[640,1536]{1,0:T(8,128)(2,1)S(1)}, u32[]{:S(2)}, u32[]{:S(2)}) collective-permute-start(bf16[640,1536]{1,0:T(8,128)(2,1)S(1)} %stack.5.w1), channel_id=1, source_target_pairs={{0,32},{32,0},{1,33},{33,1},{2,34},{34,2},{3,35},{35,3},{4,36},{36... | collective-permute-start | bytes 5898248 | tf_op jit(solution)/shard_map/ppermute | solution.py:294
  59.9 9.7 %collective-permute-start.5 = (bf16[128,1536]{1,0:T(8,128)(2,1)S(1)}, bf16[128,1536]{1,0:T(8,128)(2,1)S(1)}, u32[]{:S(2)}, u32[]{:S(2)}) collective-permute-start(bf16[128,1536]{1,0:T(8,128)(2,1)S(1)} %collective-permute-done.4.refs_1_), channel_id=1, source_target_pairs={{0,448},{32,96},{64,0},{96,160},{128,64},{160,224},{192,128},{224,... | collective-permute-start | bytes 1179656 | tf_op jit(solution)/shard_map/ppermute | solution.py:290
  71.6 5.4 %collective-permute-start.6 = (bf16[384,1536]{1,0:T(8,128)(2,1)S(1)}, bf16[384,1536]{1,0:T(8,128)(2,1)S(1)}, u32[]{:S(2)}, u32[]{:S(2)}) collective-permute-start(bf16[384,1536]{1,0:T(8,128)(2,1)S(1)} %stack.4.w0), channel_id=1, source_target_pairs={{0,32},{32,0},{1,33},{33,1},{2,34},{34,2},{3,35},{35,3},{4,36},{36... | collective-permute-start | bytes 3538952 | tf_op jit(solution)/shard_map/ppermute | solution.py:294
  77.0 1.1 copy-start.3
  78.2 1.3 copy-start
  79.4 1.5 copy-start.1
  81.0 1.3 copy-start.4
  90.4 20.7 %copy-start.5 = (bf16[1024,1536]{1,0:T(8,128)(2,1)}, bf16[1024,1536]{1,0:T(8,128)(2,1)S(1)}, u32[]{:S(2)}) copy-start(bf16[1024,1536]{1,0:T(8,128)(2,1)S(1)} %get-tuple-element.24) | copy-start | bytes 9437188
  90.4 4.7 %collective-permute-start.8 = (bf16[384,1536]{1,0:T(8,128)(2,1)S(1)}, bf16[384,1536]{1,0:T(8,128)(2,1)S(1)}, u32[]{:S(2)}, u32[]{:S(2)}) collective-permute-start(bf16[384,1536]{1,0:T(8,128)(2,1)S(1)} %get-tuple-element.25), channel_id=1, source_target_pairs={{0,32},{32,0},{1,33},{33,1},{2,34},{34,2},{3,35},{35,3},{4,36},{36... | collective-permute-start | bytes 3538952 | tf_op jit(solution)/shard_map/ppermute | solution.py:294
  92.7 28.1 %collective-permute-start.10 = (bf16[640,1536]{1,0:T(8,128)(2,1)}, bf16[640,1536]{1,0:T(8,128)(2,1)}, u32[]{:S(2)}, u32[]{:S(2)}) collective-permute-start(bf16[640,1536]{1,0:T(8,128)(2,1)} %get-tuple-element.28), channel_id=1, source_target_pairs={{0,32},{32,0},{1,33},{33,1},{2,34},{34,2},{3,35},{35,3},{4,36},{36... | collective-permute-start | bytes 5898248 | tf_op jit(solution)/shard_map/ppermute | solution.py:294
  97.0 23.8 %collective-permute-start.9 = (bf16[256,1536]{1,0:T(8,128)(2,1)}, bf16[256,1536]{1,0:T(8,128)(2,1)}, u32[]{:S(2)}, u32[]{:S(2)}) collective-permute-start(bf16[256,1536]{1,0:T(8,128)(2,1)} %add_convert_fusion), channel_id=1, source_target_pairs={{0,448},{32,96},{64,0},{96,160},{128,64},{160,224},{192,128},{224,... | collective-permute-start | bytes 2359304 | tf_op jit(solution)/shard_map/ppermute | solution.py:290
  106.8 13.8 %collective-permute-start.13 = (bf16[128,1536]{1,0:T(8,128)(2,1)}, bf16[128,1536]{1,0:T(8,128)(2,1)S(1)}, u32[]{:S(2)}, u32[]{:S(2)}) collective-permute-start(bf16[128,1536]{1,0:T(8,128)(2,1)} %add_convert_fusion.6), channel_id=1, source_target_pairs={{0,64},{32,480},{64,128},{96,32},{128,192},{160,96},{192,256},{224... | collective-permute-start | bytes 1179656 | tf_op jit(solution)/shard_map/ppermute | solution.py:290
  111.1 1.2 copy-start.2
  112.3 47.6 %all-to-all-start.1 = ((bf16[32,8,2688]{2,1,0:T(8,128)(2,1)}), bf16[32,8,2688]{2,1,0:T(8,128)(2,1)S(1)}, u32[]{:S(2)}, u32[]{:S(2)}) async-start(bf16[32,8,2688]{2,1,0:T(8,128)(2,1)} %bitcast.13), calls=%async_computation.1 | async-start | bytes 2752512 | tf_op jit(solution)/shard_map/all_to_all | solution.py:397
  122.6 16.5 %collective-permute-start.11 = (bf16[128,1536]{1,0:T(8,128)(2,1)S(1)}, bf16[128,1536]{1,0:T(8,128)(2,1)S(1)}, u32[]{:S(2)}, u32[]{:S(2)}) collective-permute-start(bf16[128,1536]{1,0:T(8,128)(2,1)S(1)} %get-tuple-element.39), channel_id=1, source_target_pairs={{0,384},{32,160},{64,448},{96,224},{128,0},{160,288},{192,64},{224... | collective-permute-start | bytes 1179656 | tf_op jit(solution)/shard_map/ppermute | solution.py:290
  126.9 12.8 %collective-permute-start.14 = (bf16[128,1536]{1,0:T(8,128)(2,1)S(1)}, bf16[128,1536]{1,0:T(8,128)(2,1)S(1)}, u32[]{:S(2)}, u32[]{:S(2)}) collective-permute-start(bf16[128,1536]{1,0:T(8,128)(2,1)S(1)} %get-tuple-element.40), channel_id=1, source_target_pairs={{0,64},{32,480},{64,128},{96,32},{128,192},{160,96},{192,256},{224... | collective-permute-start | bytes 1179656 | tf_op jit(solution)/shard_map/ppermute | solution.py:290
  141.5 26.6 %copy-start.6 = (s32[8,128]{1,0:T(8,128)S(1)}, s32[8,128]{1,0:T(8,128)}, u32[]{:S(2)}) copy-start(s32[8,128]{1,0:T(8,128)} %get-tuple-element.33.places) | copy-start | bytes 12292
  141.5 14.1 %collective-permute-start.12 = (bf16[128,1536]{1,0:T(8,128)(2,1)S(1)}, bf16[128,1536]{1,0:T(8,128)(2,1)S(1)}, u32[]{:S(2)}, u32[]{:S(2)}) collective-permute-start(bf16[128,1536]{1,0:T(8,128)(2,1)S(1)} %get-tuple-element.37), channel_id=1, source_target_pairs={{0,448},{32,96},{64,0},{96,160},{128,64},{160,224},{192,128},{224,... | collective-permute-start | bytes 1179656 | tf_op jit(solution)/shard_map/ppermute | solution.py:290
  147.7 10.9 %collective-permute-start.15 = (bf16[128,1536]{1,0:T(8,128)(2,1)S(1)}, bf16[128,1536]{1,0:T(8,128)(2,1)S(1)}, u32[]{:S(2)}, u32[]{:S(2)}) collective-permute-start(bf16[128,1536]{1,0:T(8,128)(2,1)S(1)} %get-tuple-element.38), channel_id=1, source_target_pairs={{0,64},{32,480},{64,128},{96,32},{128,192},{160,96},{192,256},{224... | collective-permute-start | bytes 1179656 | tf_op jit(solution)/shard_map/ppermute | solution.py:290
  159.9 21.9 %copy-start.7 = (s32[32]{0:T(128)S(1)}, s32[32]{0:T(128)}, u32[]{:S(2)}) copy-start(s32[32]{0:T(128)} %plan.1) | copy-start | bytes 388
  160.7 21.0 %all-to-all-start.2 = ((bf16[32,4,1536]{2,1,0:T(4,128)(2,1)}), bf16[32,4,1536]{2,1,0:T(4,128)(2,1)S(1)}, u32[]{:S(2)}, u32[]{:S(2)}) async-start(bf16[32,4,1536]{2,1,0:T(4,128)(2,1)} %reshape.25), calls=%async_computation.2 | async-start | bytes 786432 | tf_op jit(solution)/shard_map/all_to_all | solution.py:410

commit v4 on v3

--- a/solution.py
+++ b/solution.py
@@ -160,34 +160,20 @@
     )(*blocks)
 
 
-def slot_kernel(got_in, w0, w1, w2, w3, mine, first, later, pre_out, gate_out, *scratch):
-    x_all, dy_all, got, weights, sems = scratch
+def slot_kernel(got, weights, mine, first, later, pre_out, gate_out, x_all, dy_all):
     rows = got.shape[0]
-    hidden_width = w0.shape[1] // 3
-    half = w0.shape[0] + w1.shape[0]
-    width = 2 * half
+    hidden_width = weights.shape[1] // 3
+    width = weights.shape[0]
+    half = width // 2
     extra = rows // MAIN * 2
     source = iota((extra, rows), 0)
     base = source // 2 * MAIN + source % 2
     column = iota((extra, rows), 1)
-    loads = []
-    for at in (slice(2 * width, got.shape[1]), slice(0, width), slice(width, 2 * width)):
-        loads.append((got_in.at[:, at], got.at[:, at]))
-    at = 0
-    for w in (w0, w1, w2, w3):
-        loads.append((w, weights.at[at : at + w.shape[0]]))
-        at += w.shape[0]
-    loads = [pltpu.make_async_copy(a, b, sems.at[i]) for i, (a, b) in enumerate(loads)]
-    for load in loads:
-        load.start()
-    loads[0].wait()
     cut = got[:, 2 * width : 2 * width + half]
     head = one_hot(column == base)
     x_all[rows:, :half] = mm(head, cut).astype(BF)
     x_all[rows:, half:] = mm(one_hot(column == base + 4), cut).astype(BF)
-    loads[1].wait()
     x_all[:rows] = got[:, :width]
-    loads[2].wait()
     dy_all[:rows] = got[:, width : 2 * width]
     dy_all[rows:, :half] = mm(one_hot(column == base + 2), cut).astype(BF)
     dy_all[rows:, half:] = mm(one_hot(column == base + 6), cut).astype(BF)
@@ -197,8 +183,6 @@
     )
     wide = slice(0, 2 * hidden_width)
     down = slice(2 * hidden_width, 3 * hidden_width)
-    for load in loads[3:]:
-        load.wait()
     pre = mm(x_all[...], weights[:, wide])
     upstream = mm(dy_all[...], weights[:, down])
     a = pre[:, :hidden_width]
@@ -222,18 +206,12 @@
             at += LANES
 
 
-def back_kernel(pre_grad, gate_grad, w0, w1, w2, w3, back, cut_rows):
+def back_kernel(pre_grad, gate_grad, weights, back):
     total, columns = pre_grad.shape
-    width = 2 * (w0.shape[0] + w1.shape[0])
+    width = weights.shape[0]
     rows = back.shape[0]
     extra = total - rows
     quarter = width // 4
-    at = 0
-    for w in (w0, w1, w2, w3):
-        grad = mm(pre_grad[...], w[:, :columns], NT).astype(BF)
-        back[:, at : at + w.shape[0]] = grad[:rows]
-        cut_rows[:, at : at + w.shape[0]] = grad[rows:]
-        at += w.shape[0]
     row = iota((rows, extra), 0)
     column = iota((rows, extra), 1)
     target = row // MAIN * 2 + row % 2
@@ -241,7 +219,9 @@
     cut = jnp.zeros((rows, quarter), F32)
     for h in range(4):
         cols = slice(h * quarter, (h + 1) * quarter)
-        cut += mm(one_hot((column == target) & (part == h)), cut_rows[:, cols])
+        grad = mm(pre_grad[...], weights[cols, :columns], NT).astype(BF)
+        back[:, cols] = grad[:rows]
+        cut += mm(one_hot((column == target) & (part == h)), grad[rows:])
     back[:, width : width + quarter] = cut.astype(BF)
     lane = iota((rows, LANES), 1)
     spread = mm(one_hot((column == target) & (part == 0)), gate_grad[rows:])
@@ -343,7 +323,7 @@
     third, above2 = move(below, 2), move(above, -1)
     last, above3 = move(stack([third, below]), 1), move(above2, -1)
     w_mine = [stack([last, above3]), stack([third, above2, below, above, own])]
-    w_all = w_mine + [swap(w) for w in w_mine]
+    w_all = stack(w_mine + [swap(w) for w in w_mine])
 
     part = width // groups
     mine, first, later, pre_grad, gate_rows = call(
@@ -356,16 +336,13 @@
             jax.ShapeDtypeStruct((total, LANES), BF),
         ),
         "slot",
-        32,
-        in_specs=[anywhere] * 5,
+        28,
+        in_specs=[vmem] * 2,
         scratch_shapes=[
             pltpu.VMEM((total, width), BF),
             pltpu.VMEM((total, width), BF),
-            pltpu.VMEM(sent.shape, BF),
-            pltpu.VMEM((width, columns), BF),
-            pltpu.SemaphoreType.DMA((7,)),
         ],
-    )(got, *w_all)
+    )(got, w_all)
     first, later = swap(first), swap(later)
 
     def both(j, n=1):
@@ -382,9 +359,8 @@
         jax.ShapeDtypeStruct((rows, width + width // 4 + LANES), BF),
         "back",
         24,
-        in_specs=[vmem] * 6,
-        scratch_shapes=[pltpu.VMEM((total - rows, width), BF)],
-    )(pre_grad, gate_rows, *w_all)
+        in_specs=[vmem] * 3,
+    )(pre_grad, gate_rows, w_all)
     minus, plus = move(minus, -1), move(plus, 1)
     far_sum = (minus[:part].astype(F32) + both(3)).astype(BF)
     plus = (plus.astype(F32) + both(4)).astype(BF)

time: 184 us -> 184 us (level)
    pallas_call x1, Pallas kernels: 8.1 us -> 6.24 us  [local(): call(slot_kernel, (jax.ShapeDtypeStruct((width // 2, columns), BF), jax.S...]
    unnamed x20 -> x16, local copies, waits for them, and re-layouts: 6.42 us -> 5.44 us
  transfers between devices with their start and end apart: 19 -> 19, of which waited for: 13 -> 13; matrix products, arithmetic and copies ran while one was open for 4% -> 4% of each run, Pallas kernels for 2% -> 3%
where the time goes in v4:
time: 184 us; the launch traced here: 183 us
  starting transfers between devices  91.3 us (50%)
  waiting for transfers between devices  57.9 us (31%)
  Pallas kernels  18 us (10%)
  local copies, waits for them, and re-layouts  7.28 us (4%)
  other arithmetic  7.15 us (4%)
    ppermute x12, starting transfers between devices, move(): return lax.ppermute(array, ('z', 'core'), pairs)  58.2 us
    ppermute x12, waiting for transfers between devices, move(): return lax.ppermute(array, ('z', 'core'), pairs)  42.8 us
    all_to_all x1, waiting for transfers between devices, local(): mixed = lax.all_to_all(owned, 'ep', split_axis=0, concat_axis=0, tiled=True)  12.2 us
    all_to_all x1, starting transfers between devices, local(): got = lax.all_to_all(sent, 'ep', split_axis=0, concat_axis=0, tiled=True)  10.3 us
    ppermute x4, starting transfers between devices, swap(): return lax.ppermute(array, 'core', [(0, 1), (1, 0)])  8.94 us
    all_to_all x1, starting transfers between devices, local(): mixed = lax.all_to_all(owned, 'ep', split_axis=0, concat_axis=0, tiled=True)  7.4 us
    all_to_all x1, starting transfers between devices, local(): back = lax.all_to_all(back, 'ep', split_axis=0, concat_axis=0, tiled=True)  6.46 us
    pallas_call x1, Pallas kernels, local(): call(slot_kernel, (jax.ShapeDtypeStruct((width // 2, columns), BF), jax.S...  6.24 us
  transfers between devices with their start and end apart: 19, of which 13 were waited for; matrix products, arithmetic and copies ran while one was open for 4% of the time, Pallas kernels for 3%

profile of v4, /device:TPU:8, one launch (start us, length us, event | category | flops | bytes accessed | tf_op | source)
XLA Modules:
  0.0 182.6 jit_solution(3731061272663653935)
XLA Ops:
  0.6 4.9 %pack.1 = (bf16[256,5248]{1,0:T(8,128)(2,1)}, s32[8,128]{1,0:T(8,128)}) custom-call(s32[1]{0:T(128)} %bitcast.z, s32[1]{0:T(128)} %bitcast.1.core, s32[2,128]{1,0:T(2,128)} %bitcast.18, bf16[2,128]{1,0:T(2,128)(2,1)} %bitcast.19, s32[1,32]{1,0:T(1,128)} %bitcast.14, s32[16,32]{1,0:T(8,128)} %failed.1, bf16[128,2048]{1,0:T(8,128)(2,1)} %tokens_in.1, ...), custom_call_target="tpu_custom_call" | custom-call | tf_op jit(solution)/shard_map/pack/pallas_call | solution.py:293
  5.6 10.3 %all-to-all-start = ((bf16[32,8,5248]{2,1,0:T(8,128)(2,1)}), bf16[32,8,5248]{2,1,0:T(8,128)(2,1)S(1)}, u32[]{:S(2)}, u32[]{:S(2)}) async-start(bf16[32,8,5248]{2,1,0:T(8,128)(2,1)} %bitcast.15), calls=%async_computation | async-start | bytes 5373952 | tf_op jit(solution)/shard_map/all_to_all | solution.py:320
  15.9 4.3 %collective-permute-start = (bf16[128,1536]{1,0:T(8,128)(2,1)S(1)}, bf16[128,1536]{1,0:T(8,128)(2,1)S(1)}, u32[]{:S(2)}, u32[]{:S(2)}) collective-permute-start(bf16[128,1536]{1,0:T(8,128)(2,1)S(1)} %pad_maximum_fusion.refs_4_), channel_id=1, source_target_pairs={{0,64},{32,480},{64,128},{96,32},{128,192},{160,96},{192,256},{224... | collective-permute-start | bytes 1179656 | tf_op jit(solution)/shard_map/ppermute | solution.py:270
  20.2 8.6 %collective-permute-start.3 = (bf16[128,1536]{1,0:T(8,128)(2,1)S(1)}, bf16[128,1536]{1,0:T(8,128)(2,1)S(1)}, u32[]{:S(2)}, u32[]{:S(2)}) collective-permute-start(bf16[128,1536]{1,0:T(8,128)(2,1)S(1)} %pad_maximum_fusion.refs_4_), channel_id=1, source_target_pairs={{0,448},{32,96},{64,0},{96,160},{128,64},{160,224},{192,128},{224,... | collective-permute-start | bytes 1179656 | tf_op jit(solution)/shard_map/ppermute | solution.py:270
  28.8 4.8 %collective-permute-done.refs_1_.refs_2_ = bf16[128,1536]{1,0:T(8,128)(2,1)S(1)} collective-permute-done((bf16[128,1536]{1,0:T(8,128)(2,1)S(1)}, bf16[128,1536]{1,0:T(8,128)(2,1)S(1)}, u32[]{:S(2)}, u32[]{:S(2)}) %collective-permute-start) | collective-permute-done | bytes 393248 | tf_op jit(solution)/shard_map/ppermute | solution.py:270
  33.6 2.0 %collective-permute-start.1 = (bf16[128,1536]{1,0:T(8,128)(2,1)S(1)}, bf16[128,1536]{1,0:T(8,128)(2,1)S(1)}, u32[]{:S(2)}, u32[]{:S(2)}) collective-permute-start(bf16[128,1536]{1,0:T(8,128)(2,1)S(1)} %collective-permute-done.refs_1_.refs_2_), channel_id=1, source_target_pairs={{0,128},{32,416},{64,192},{96,480},{128,256},{160,32},{192,320},{2... | collective-permute-start | bytes 1179656 | tf_op jit(solution)/shard_map/ppermute | solution.py:270
  35.7 6.6 %collective-permute-start.4 = (bf16[128,1536]{1,0:T(8,128)(2,1)S(1)}, bf16[128,1536]{1,0:T(8,128)(2,1)S(1)}, u32[]{:S(2)}, u32[]{:S(2)}) collective-permute-start(bf16[128,1536]{1,0:T(8,128)(2,1)S(1)} %collective-permute-done.3.refs_3_), channel_id=1, source_target_pairs={{0,448},{32,96},{64,0},{96,160},{128,64},{160,224},{192,128},{224,... | collective-permute-start | bytes 1179656 | tf_op jit(solution)/shard_map/ppermute | solution.py:270
  42.3 9.3 %collective-permute-done.1.refs_0_ = bf16[128,1536]{1,0:T(8,128)(2,1)S(1)} collective-permute-done((bf16[128,1536]{1,0:T(8,128)(2,1)S(1)}, bf16[128,1536]{1,0:T(8,128)(2,1)S(1)}, u32[]{:S(2)}, u32[]{:S(2)}) %collective-permute-start.1) | collective-permute-done | bytes 393248 | tf_op jit(solution)/shard_map/ppermute | solution.py:270
  51.6 6.2 %collective-permute-start.2 = (bf16[256,1536]{1,0:T(8,128)(2,1)S(1)}, bf16[256,1536]{1,0:T(8,128)(2,1)S(1)}, u32[]{:S(2)}, u32[]{:S(2)}) collective-permute-start(bf16[256,1536]{1,0:T(8,128)(2,1)S(1)} %stack.4), channel_id=1, source_target_pairs={{0,64},{32,480},{64,128},{96,32},{128,192},{160,96},{192,256},{224... | collective-permute-start | bytes 2359304 | tf_op jit(solution)/shard_map/ppermute | solution.py:270
  59.9 2.1 %collective-permute-start.5 = (bf16[128,1536]{1,0:T(8,128)(2,1)S(1)}, bf16[128,1536]{1,0:T(8,128)(2,1)S(1)}, u32[]{:S(2)}, u32[]{:S(2)}) collective-permute-start(bf16[128,1536]{1,0:T(8,128)(2,1)S(1)} %collective-permute-done.4.refs_1_), channel_id=1, source_target_pairs={{0,448},{32,96},{64,0},{96,160},{128,64},{160,224},{192,128},{224,... | collective-permute-start | bytes 1179656 | tf_op jit(solution)/shard_map/ppermute | solution.py:270
  62.0 7.5 %collective-permute-done.5.refs_1_ = bf16[128,1536]{1,0:T(8,128)(2,1)S(1)} collective-permute-done((bf16[128,1536]{1,0:T(8,128)(2,1)S(1)}, bf16[128,1536]{1,0:T(8,128)(2,1)S(1)}, u32[]{:S(2)}, u32[]{:S(2)}) %collective-permute-start.5) | collective-permute-done | bytes 393248 | tf_op jit(solution)/shard_map/ppermute | solution.py:270
  69.6 2.0 %collective-permute-done.2.refs_0_ = bf16[256,1536]{1,0:T(8,128)(2,1)S(1)} collective-permute-done((bf16[256,1536]{1,0:T(8,128)(2,1)S(1)}, bf16[256,1536]{1,0:T(8,128)(2,1)S(1)}, u32[]{:S(2)}, u32[]{:S(2)}) %collective-permute-start.2) | collective-permute-done | bytes 786464 | tf_op jit(solution)/shard_map/ppermute | solution.py:270
  71.6 2.7 %collective-permute-start.6 = (bf16[384,1536]{1,0:T(8,128)(2,1)S(1)}, bf16[384,1536]{1,0:T(8,128)(2,1)S(1)}, u32[]{:S(2)}, u32[]{:S(2)}) collective-permute-start(bf16[384,1536]{1,0:T(8,128)(2,1)S(1)} %stack.5.refs_0_), channel_id=1, source_target_pairs={{0,32},{32,0},{1,33},{33,1},{2,34},{34,2},{3,35},{35,3},{4,36},{36... | collective-permute-start | bytes 3538952 | tf_op jit(solution)/shard_map/ppermute | solution.py:274
  74.3 2.5 %collective-permute-done.6.refs_2_ = bf16[384,1536]{1,0:T(8,128)(2,1)S(1)} collective-permute-done((bf16[384,1536]{1,0:T(8,128)(2,1)S(1)}, bf16[384,1536]{1,0:T(8,128)(2,1)S(1)}, u32[]{:S(2)}, u32[]{:S(2)}) %collective-permute-start.6) | collective-permute-done | bytes 1179680 | tf_op jit(solution)/shard_map/ppermute | solution.py:274
  77.2 2.6 %copy-done = bf16[2048,1536]{1,0:T(8,128)(2,1)} copy-done((bf16[2048,1536]{1,0:T(8,128)(2,1)}, bf16[2048,1536]{1,0:T(8,128)(2,1)S(1)}, u32[]{:S(2)}) %copy-start) | copy-done | bytes 6291480
  79.8 2.8 %copy-done.1 = bf16[2048,1536]{1,0:T(8,128)(2,1)S(1)} copy-done((bf16[2048,1536]{1,0:T(8,128)(2,1)S(1)}, bf16[2048,1536]{1,0:T(8,128)(2,1)}, u32[]{:S(2)}) %copy-start.1) | copy-done | bytes 6291480
  82.6 6.2 %slot.1 = (bf16[1024,1536]{1,0:T(8,128)(2,1)S(1)}, bf16[384,1536]{1,0:T(8,128)(2,1)S(1)}, bf16[640,1536]{1,0:T(8,128)(2,1)}, bf16[320,1024]{1,0:T(8,128)(2,1)S(1)}, bf16[320,128]{1,0:T(8,128)(2,1)S(1)}) custom-call(bf16[256,5248]{1,0:T(8,128)(2,1)S(1)} %bitcast.12, bf16[2048,1536]{1,0:T(8,128)(2,1)S(1)} %copy-done.1), custom_call_target="tpu_custom_call" | custom-call | tf_op jit(solution)/shard_map/slot/pallas_call | solution.py:329
  88.9 2.3 %collective-permute-start.8 = (bf16[384,1536]{1,0:T(8,128)(2,1)S(1)}, bf16[384,1536]{1,0:T(8,128)(2,1)S(1)}, u32[]{:S(2)}, u32[]{:S(2)}) collective-permute-start(bf16[384,1536]{1,0:T(8,128)(2,1)S(1)} %get-tuple-element.25), channel_id=1, source_target_pairs={{0,32},{32,0},{1,33},{33,1},{2,34},{34,2},{3,35},{35,3},{4,36},{36... | collective-permute-start | bytes 3538952 | tf_op jit(solution)/shard_map/ppermute | solution.py:274
  91.1 2.0 %collective-permute-start.10 = (bf16[640,1536]{1,0:T(8,128)(2,1)}, bf16[640,1536]{1,0:T(8,128)(2,1)S(1)}, u32[]{:S(2)}, u32[]{:S(2)}) collective-permute-start(bf16[640,1536]{1,0:T(8,128)(2,1)} %get-tuple-element.28), channel_id=1, source_target_pairs={{0,32},{32,0},{1,33},{33,1},{2,34},{34,2},{3,35},{35,3},{4,36},{36... | collective-permute-start | bytes 5898248 | tf_op jit(solution)/shard_map/ppermute | solution.py:274
  95.6 9.3 %collective-permute-start.9 = (bf16[256,1536]{1,0:T(8,128)(2,1)}, bf16[256,1536]{1,0:T(8,128)(2,1)}, u32[]{:S(2)}, u32[]{:S(2)}) collective-permute-start(bf16[256,1536]{1,0:T(8,128)(2,1)} %add_convert_fusion), channel_id=1, source_target_pairs={{0,448},{32,96},{64,0},{96,160},{128,64},{160,224},{192,128},{224,... | collective-permute-start | bytes 2359304 | tf_op jit(solution)/shard_map/ppermute | solution.py:270
  104.8 2.1 %collective-permute-start.13 = (bf16[128,1536]{1,0:T(8,128)(2,1)}, bf16[128,1536]{1,0:T(8,128)(2,1)}, u32[]{:S(2)}, u32[]{:S(2)}) collective-permute-start(bf16[128,1536]{1,0:T(8,128)(2,1)} %add_convert_fusion.6), channel_id=1, source_target_pairs={{0,64},{32,480},{64,128},{96,32},{128,192},{160,96},{192,256},{224... | collective-permute-start | bytes 1179656 | tf_op jit(solution)/shard_map/ppermute | solution.py:270
  107.0 3.3 %back.1 = bf16[256,2688]{1,0:T(8,128)(2,1)} custom-call(bf16[320,1024]{1,0:T(8,128)(2,1)S(1)} %get-tuple-element.30.pre_grad, bf16[320,128]{1,0:T(8,128)(2,1)S(1)} %get-tuple-element.31.gate_grad, bf16[2048,1536]{1,0:T(8,128)(2,1)S(1)} %copy-done.2), custom_call_target="tpu_custom_call" | custom-call | tf_op jit(solution)/shard_map/back/pallas_call | solution.py:357
  110.3 6.5 %all-to-all-start.1 = ((bf16[32,8,2688]{2,1,0:T(8,128)(2,1)}), bf16[32,8,2688]{2,1,0:T(8,128)(2,1)S(1)}, u32[]{:S(2)}, u32[]{:S(2)}) async-start(bf16[32,8,2688]{2,1,0:T(8,128)(2,1)} %bitcast.9), calls=%async_computation.1 | async-start | bytes 2752512 | tf_op jit(solution)/shard_map/all_to_all | solution.py:373
  116.8 2.0 %collective-permute-done.13 = bf16[128,1536]{1,0:T(8,128)(2,1)} collective-permute-done((bf16[128,1536]{1,0:T(8,128)(2,1)}, bf16[128,1536]{1,0:T(8,128)(2,1)}, u32[]{:S(2)}, u32[]{:S(2)}) %collective-permute-start.13) | collective-permute-done | bytes 393248 | tf_op jit(solution)/shard_map/ppermute | solution.py:270
  120.5 4.4 %collective-permute-start.11 = (bf16[128,1536]{1,0:T(8,128)(2,1)S(1)}, bf16[128,1536]{1,0:T(8,128)(2,1)S(1)}, u32[]{:S(2)}, u32[]{:S(2)}) collective-permute-start(bf16[128,1536]{1,0:T(8,128)(2,1)S(1)} %get-tuple-element.39), channel_id=1, source_target_pairs={{0,384},{32,160},{64,448},{96,224},{128,0},{160,288},{192,64},{224... | collective-permute-start | bytes 1179656 | tf_op jit(solution)/shard_map/ppermute | solution.py:270
  124.9 4.6 %collective-permute-start.14 = (bf16[128,1536]{1,0:T(8,128)(2,1)S(1)}, bf16[128,1536]{1,0:T(8,128)(2,1)S(1)}, u32[]{:S(2)}, u32[]{:S(2)}) collective-permute-start(bf16[128,1536]{1,0:T(8,128)(2,1)S(1)} %get-tuple-element.40), channel_id=1, source_target_pairs={{0,64},{32,480},{64,128},{96,32},{128,192},{160,96},{192,256},{224... | collective-permute-start | bytes 1179656 | tf_op jit(solution)/shard_map/ppermute | solution.py:270
  129.5 7.5 %collective-permute-done.11 = bf16[128,1536]{1,0:T(8,128)(2,1)S(1)} collective-permute-done((bf16[128,1536]{1,0:T(8,128)(2,1)S(1)}, bf16[128,1536]{1,0:T(8,128)(2,1)S(1)}, u32[]{:S(2)}, u32[]{:S(2)}) %collective-permute-start.11) | collective-permute-done | bytes 393248 | tf_op jit(solution)/shard_map/ppermute | solution.py:270
  139.3 6.1 %collective-permute-start.12 = (bf16[128,1536]{1,0:T(8,128)(2,1)S(1)}, bf16[128,1536]{1,0:T(8,128)(2,1)S(1)}, u32[]{:S(2)}, u32[]{:S(2)}) collective-permute-start(bf16[128,1536]{1,0:T(8,128)(2,1)S(1)} %get-tuple-element.37), channel_id=1, source_target_pairs={{0,448},{32,96},{64,0},{96,160},{128,64},{160,224},{192,128},{224,... | collective-permute-start | bytes 1179656 | tf_op jit(solution)/shard_map/ppermute | solution.py:270
  147.3 6.0 %collective-permute-done.12 = bf16[128,1536]{1,0:T(8,128)(2,1)S(1)} collective-permute-done((bf16[128,1536]{1,0:T(8,128)(2,1)S(1)}, bf16[128,1536]{1,0:T(8,128)(2,1)S(1)}, u32[]{:S(2)}, u32[]{:S(2)}) %collective-permute-start.12) | collective-permute-done | bytes 393248 | tf_op jit(solution)/shard_map/ppermute | solution.py:270
  153.3 2.9 %collective-permute-done.15 = bf16[128,1536]{1,0:T(8,128)(2,1)S(1)} collective-permute-done((bf16[128,1536]{1,0:T(8,128)(2,1)S(1)}, bf16[128,1536]{1,0:T(8,128)(2,1)S(1)}, u32[]{:S(2)}, u32[]{:S(2)}) %collective-permute-start.15) | collective-permute-done | bytes 393248 | tf_op jit(solution)/shard_map/ppermute | solution.py:270
  160.1 7.4 %all-to-all-start.2 = ((bf16[32,4,1536]{2,1,0:T(4,128)(2,1)}), bf16[32,4,1536]{2,1,0:T(4,128)(2,1)S(1)}, u32[]{:S(2)}, u32[]{:S(2)}) async-start(bf16[32,4,1536]{2,1,0:T(4,128)(2,1)} %reshape.25), calls=%async_computation.2 | async-start | bytes 786432 | tf_op jit(solution)/shard_map/all_to_all | solution.py:386
  168.8 12.2 %all-to-all-done.2.mixed = bf16[32,4,1536]{2,1,0:T(4,128)(2,1)S(1)} async-done(((bf16[32,4,1536]{2,1,0:T(4,128)(2,1)}), bf16[32,4,1536]{2,1,0:T(4,128)(2,1)S(1)}, u32[]{:S(2)}, u32[]{:S(2)}) %all-to-all-start.2) | async-done | bytes 393248 | tf_op jit(solution)/shard_map/all_to_all | solution.py:386
  (38 shorter events, 17.6 us)
Async XLA Ops:
  5.5 10.3 %copy-start.6 = (bf16[1,128,1024]{2,1,0:T(8,128)(2,1)S(1)}, bf16[1,128,1024]{2,1,0:T(8,128)(2,1)}, u32[]{:S(2)}) copy-start(bf16[1,128,1024]{2,1,0:T(8,128)(2,1)} %param.12) | copy-start | bytes 786436
  5.5 10.3 %copy-start.7 = (bf16[1,128,512]{2,1,0:T(8,128)(2,1)S(1)}, bf16[1,128,512]{2,1,0:T(8,128)(2,1)}, u32[]{:S(2)}) copy-start(bf16[1,128,512]{2,1,0:T(8,128)(2,1)} %param.13) | copy-start | bytes 393220
  5.6 74.3 %all-to-all-start = ((bf16[32,8,5248]{2,1,0:T(8,128)(2,1)}), bf16[32,8,5248]{2,1,0:T(8,128)(2,1)S(1)}, u32[]{:S(2)}, u32[]{:S(2)}) async-start(bf16[32,8,5248]{2,1,0:T(8,128)(2,1)} %bitcast.15), calls=%async_computation | async-start | bytes 5373952 | tf_op jit(solution)/shard_map/all_to_all | solution.py:320
  15.9 17.7 %collective-permute-start = (bf16[128,1536]{1,0:T(8,128)(2,1)S(1)}, bf16[128,1536]{1,0:T(8,128)(2,1)S(1)}, u32[]{:S(2)}, u32[]{:S(2)}) collective-permute-start(bf16[128,1536]{1,0:T(8,128)(2,1)S(1)} %pad_maximum_fusion.refs_4_), channel_id=1, source_target_pairs={{0,64},{32,480},{64,128},{96,32},{128,192},{160,96},{192,256},{224... | collective-permute-start | bytes 1179656 | tf_op jit(solution)/shard_map/ppermute | solution.py:270
  20.2 15.4 %collective-permute-start.3 = (bf16[128,1536]{1,0:T(8,128)(2,1)S(1)}, bf16[128,1536]{1,0:T(8,128)(2,1)S(1)}, u32[]{:S(2)}, u32[]{:S(2)}) collective-permute-start(bf16[128,1536]{1,0:T(8,128)(2,1)S(1)} %pad_maximum_fusion.refs_4_), channel_id=1, source_target_pairs={{0,448},{32,96},{64,0},{96,160},{128,64},{160,224},{192,128},{224,... | collective-permute-start | bytes 1179656 | tf_op jit(solution)/shard_map/ppermute | solution.py:270
  33.6 18.0 %collective-permute-start.1 = (bf16[128,1536]{1,0:T(8,128)(2,1)S(1)}, bf16[128,1536]{1,0:T(8,128)(2,1)S(1)}, u32[]{:S(2)}, u32[]{:S(2)}) collective-permute-start(bf16[128,1536]{1,0:T(8,128)(2,1)S(1)} %collective-permute-done.refs_1_.refs_2_), channel_id=1, source_target_pairs={{0,128},{32,416},{64,192},{96,480},{128,256},{160,32},{192,320},{2... | collective-permute-start | bytes 1179656 | tf_op jit(solution)/shard_map/ppermute | solution.py:270
  35.7 22.2 %collective-permute-start.4 = (bf16[128,1536]{1,0:T(8,128)(2,1)S(1)}, bf16[128,1536]{1,0:T(8,128)(2,1)S(1)}, u32[]{:S(2)}, u32[]{:S(2)}) collective-permute-start(bf16[128,1536]{1,0:T(8,128)(2,1)S(1)} %collective-permute-done.3.refs_3_), channel_id=1, source_target_pairs={{0,448},{32,96},{64,0},{96,160},{128,64},{160,224},{192,128},{224,... | collective-permute-start | bytes 1179656 | tf_op jit(solution)/shard_map/ppermute | solution.py:270
  51.6 19.9 %collective-permute-start.2 = (bf16[256,1536]{1,0:T(8,128)(2,1)S(1)}, bf16[256,1536]{1,0:T(8,128)(2,1)S(1)}, u32[]{:S(2)}, u32[]{:S(2)}) collective-permute-start(bf16[256,1536]{1,0:T(8,128)(2,1)S(1)} %stack.4), channel_id=1, source_target_pairs={{0,64},{32,480},{64,128},{96,32},{128,192},{160,96},{192,256},{224... | collective-permute-start | bytes 2359304 | tf_op jit(solution)/shard_map/ppermute | solution.py:270
  58.0 18.8 %collective-permute-start.7 = (bf16[640,1536]{1,0:T(8,128)(2,1)S(1)}, bf16[640,1536]{1,0:T(8,128)(2,1)S(1)}, u32[]{:S(2)}, u32[]{:S(2)}) collective-permute-start(bf16[640,1536]{1,0:T(8,128)(2,1)S(1)} %stack.6.refs_1_), channel_id=1, source_target_pairs={{0,32},{32,0},{1,33},{33,1},{2,34},{34,2},{3,35},{35,3},{4,36},{36... | collective-permute-start | bytes 5898248 | tf_op jit(solution)/shard_map/ppermute | solution.py:274
  59.9 9.7 %collective-permute-start.5 = (bf16[128,1536]{1,0:T(8,128)(2,1)S(1)}, bf16[128,1536]{1,0:T(8,128)(2,1)S(1)}, u32[]{:S(2)}, u32[]{:S(2)}) collective-permute-start(bf16[128,1536]{1,0:T(8,128)(2,1)S(1)} %collective-permute-done.4.refs_1_), channel_id=1, source_target_pairs={{0,448},{32,96},{64,0},{96,160},{128,64},{160,224},{192,128},{224,... | collective-permute-start | bytes 1179656 | tf_op jit(solution)/shard_map/ppermute | solution.py:270
  71.6 5.2 %collective-permute-start.6 = (bf16[384,1536]{1,0:T(8,128)(2,1)S(1)}, bf16[384,1536]{1,0:T(8,128)(2,1)S(1)}, u32[]{:S(2)}, u32[]{:S(2)}) collective-permute-start(bf16[384,1536]{1,0:T(8,128)(2,1)S(1)} %stack.5.refs_0_), channel_id=1, source_target_pairs={{0,32},{32,0},{1,33},{33,1},{2,34},{34,2},{3,35},{35,3},{4,36},{36... | collective-permute-start | bytes 3538952 | tf_op jit(solution)/shard_map/ppermute | solution.py:274
  77.2 2.6 %copy-start = (bf16[2048,1536]{1,0:T(8,128)(2,1)}, bf16[2048,1536]{1,0:T(8,128)(2,1)S(1)}, u32[]{:S(2)}) copy-start(bf16[2048,1536]{1,0:T(8,128)(2,1)S(1)} %stack.7.weights) | copy-start | bytes 18874372
  79.8 2.8 %copy-start.1 = (bf16[2048,1536]{1,0:T(8,128)(2,1)S(1)}, bf16[2048,1536]{1,0:T(8,128)(2,1)}, u32[]{:S(2)}) copy-start(bf16[2048,1536]{1,0:T(8,128)(2,1)} %copy-done) | copy-start | bytes 18874372
  82.6 24.4 %copy-start.2 = (bf16[2048,1536]{1,0:T(8,128)(2,1)S(1)}, bf16[2048,1536]{1,0:T(8,128)(2,1)}, u32[]{:S(2)}) copy-start(bf16[2048,1536]{1,0:T(8,128)(2,1)} %copy-done) | copy-start | bytes 18874372
  88.8 21.4 %copy-start.3 = (bf16[1024,1536]{1,0:T(8,128)(2,1)}, bf16[1024,1536]{1,0:T(8,128)(2,1)S(1)}, u32[]{:S(2)}) copy-start(bf16[1024,1536]{1,0:T(8,128)(2,1)S(1)} %get-tuple-element.24) | copy-start | bytes 9437188
  88.9 4.7 %collective-permute-start.8 = (bf16[384,1536]{1,0:T(8,128)(2,1)S(1)}, bf16[384,1536]{1,0:T(8,128)(2,1)S(1)}, u32[]{:S(2)}, u32[]{:S(2)}) collective-permute-start(bf16[384,1536]{1,0:T(8,128)(2,1)S(1)} %get-tuple-element.25), channel_id=1, source_target_pairs={{0,32},{32,0},{1,33},{33,1},{2,34},{34,2},{3,35},{35,3},{4,36},{36... | collective-permute-start | bytes 3538952 | tf_op jit(solution)/shard_map/ppermute | solution.py:274
  91.1 27.7 %collective-permute-start.10 = (bf16[640,1536]{1,0:T(8,128)(2,1)}, bf16[640,1536]{1,0:T(8,128)(2,1)S(1)}, u32[]{:S(2)}, u32[]{:S(2)}) collective-permute-start(bf16[640,1536]{1,0:T(8,128)(2,1)} %get-tuple-element.28), channel_id=1, source_target_pairs={{0,32},{32,0},{1,33},{33,1},{2,34},{34,2},{3,35},{35,3},{4,36},{36... | collective-permute-start | bytes 5898248 | tf_op jit(solution)/shard_map/ppermute | solution.py:274
  95.6 23.3 %collective-permute-start.9 = (bf16[256,1536]{1,0:T(8,128)(2,1)}, bf16[256,1536]{1,0:T(8,128)(2,1)}, u32[]{:S(2)}, u32[]{:S(2)}) collective-permute-start(bf16[256,1536]{1,0:T(8,128)(2,1)} %add_convert_fusion), channel_id=1, source_target_pairs={{0,448},{32,96},{64,0},{96,160},{128,64},{160,224},{192,128},{224,... | collective-permute-start | bytes 2359304 | tf_op jit(solution)/shard_map/ppermute | solution.py:270
  104.8 13.9 %collective-permute-start.13 = (bf16[128,1536]{1,0:T(8,128)(2,1)}, bf16[128,1536]{1,0:T(8,128)(2,1)}, u32[]{:S(2)}, u32[]{:S(2)}) collective-permute-start(bf16[128,1536]{1,0:T(8,128)(2,1)} %add_convert_fusion.6), channel_id=1, source_target_pairs={{0,64},{32,480},{64,128},{96,32},{128,192},{160,96},{192,256},{224... | collective-permute-start | bytes 1179656 | tf_op jit(solution)/shard_map/ppermute | solution.py:270
  110.3 47.9 %all-to-all-start.1 = ((bf16[32,8,2688]{2,1,0:T(8,128)(2,1)}), bf16[32,8,2688]{2,1,0:T(8,128)(2,1)S(1)}, u32[]{:S(2)}, u32[]{:S(2)}) async-start(bf16[32,8,2688]{2,1,0:T(8,128)(2,1)} %bitcast.9), calls=%async_computation.1 | async-start | bytes 2752512 | tf_op jit(solution)/shard_map/all_to_all | solution.py:373
  120.5 16.5 %collective-permute-start.11 = (bf16[128,1536]{1,0:T(8,128)(2,1)S(1)}, bf16[128,1536]{1,0:T(8,128)(2,1)S(1)}, u32[]{:S(2)}, u32[]{:S(2)}) collective-permute-start(bf16[128,1536]{1,0:T(8,128)(2,1)S(1)} %get-tuple-element.39), channel_id=1, source_target_pairs={{0,384},{32,160},{64,448},{96,224},{128,0},{160,288},{192,64},{224... | collective-permute-start | bytes 1179656 | tf_op jit(solution)/shard_map/ppermute | solution.py:270
  124.9 12.8 %collective-permute-start.14 = (bf16[128,1536]{1,0:T(8,128)(2,1)S(1)}, bf16[128,1536]{1,0:T(8,128)(2,1)S(1)}, u32[]{:S(2)}, u32[]{:S(2)}) collective-permute-start(bf16[128,1536]{1,0:T(8,128)(2,1)S(1)} %get-tuple-element.40), channel_id=1, source_target_pairs={{0,64},{32,480},{64,128},{96,32},{128,192},{160,96},{192,256},{224... | collective-permute-start | bytes 1179656 | tf_op jit(solution)/shard_map/ppermute | solution.py:270
  139.2 28.2 %copy-start.4 = (s32[8,128]{1,0:T(8,128)S(1)}, s32[8,128]{1,0:T(8,128)}, u32[]{:S(2)}) copy-start(s32[8,128]{1,0:T(8,128)} %get-tuple-element.33.places) | copy-start | bytes 12292
  139.3 14.1 %collective-permute-start.12 = (bf16[128,1536]{1,0:T(8,128)(2,1)S(1)}, bf16[128,1536]{1,0:T(8,128)(2,1)S(1)}, u32[]{:S(2)}, u32[]{:S(2)}) collective-permute-start(bf16[128,1536]{1,0:T(8,128)(2,1)S(1)} %get-tuple-element.37), channel_id=1, source_target_pairs={{0,448},{32,96},{64,0},{96,160},{128,64},{160,224},{192,128},{224,... | collective-permute-start | bytes 1179656 | tf_op jit(solution)/shard_map/ppermute | solution.py:270
  145.4 10.9 %collective-permute-start.15 = (bf16[128,1536]{1,0:T(8,128)(2,1)S(1)}, bf16[128,1536]{1,0:T(8,128)(2,1)S(1)}, u32[]{:S(2)}, u32[]{:S(2)}) collective-permute-start(bf16[128,1536]{1,0:T(8,128)(2,1)S(1)} %get-tuple-element.38), channel_id=1, source_target_pairs={{0,64},{32,480},{64,128},{96,32},{128,192},{160,96},{192,256},{224... | collective-permute-start | bytes 1179656 | tf_op jit(solution)/shard_map/ppermute | solution.py:270
  158.2 22.9 %copy-start.5 = (s32[32]{0:T(128)S(1)}, s32[32]{0:T(128)}, u32[]{:S(2)}) copy-start(s32[32]{0:T(128)} %plan.1) | copy-start | bytes 388
  160.1 21.0 %all-to-all-start.2 = ((bf16[32,4,1536]{2,1,0:T(4,128)(2,1)}), bf16[32,4,1536]{2,1,0:T(4,128)(2,1)S(1)}, u32[]{:S(2)}, u32[]{:S(2)}) async-start(bf16[32,4,1536]{2,1,0:T(4,128)(2,1)} %reshape.25), calls=%async_computation.2 | async-start | bytes 786432 | tf_op jit(solution)/shard_map/all_to_all | solution.py:386

commit v5 on v3

--- a/solution.py
+++ b/solution.py
@@ -365,6 +365,9 @@
             pltpu.VMEM((width, columns), BF),
             pltpu.SemaphoreType.DMA((7,)),
         ],
+        cost_estimate=pl.CostEstimate(
+            flops=int(6e9), bytes_accessed=4 * width * columns, transcendentals=0
+        ),
     )(got, *w_all)
     first, later = swap(first), swap(later)
 

time: 184 us -> 184 us (level)
    unnamed x20 -> x18, local copies, waits for them, and re-layouts: 6.42 us -> 5.25 us
  transfers between devices with their start and end apart: 19 -> 19, of which waited for: 13 -> 13; matrix products, arithmetic and copies ran while one was open for 4% -> 4% of each run, Pallas kernels for 2% -> 3%
where the time goes in v5:
time: 184 us; the launch traced here: 183 us
  starting transfers between devices  92.3 us (50%)
  waiting for transfers between devices  57.6 us (31%)
  Pallas kernels  19.5 us (11%)
  other arithmetic  6.8 us (4%)
  local copies, waits for them, and re-layouts  6.09 us (3%)
    ppermute x12, starting transfers between devices, move(): return lax.ppermute(array, ('z', 'core'), pairs)  58.9 us
    ppermute x12, waiting for transfers between devices, move(): return lax.ppermute(array, ('z', 'core'), pairs)  42.5 us
    all_to_all x1, waiting for transfers between devices, local(): mixed = lax.all_to_all(owned, 'ep', split_axis=0, concat_axis=0, tiled=True)  12.2 us
    all_to_all x1, starting transfers between devices, local(): got = lax.all_to_all(sent, 'ep', split_axis=0, concat_axis=0, tiled=True)  10.4 us
    ppermute x4, starting transfers between devices, swap(): return lax.ppermute(array, 'core', [(0, 1), (1, 0)])  9.17 us
    pallas_call x1, Pallas kernels, local(): call(slot_kernel, (jax.ShapeDtypeStruct((width // 2, columns), BF), jax.S...  8.11 us
    all_to_all x1, starting transfers between devices, local(): mixed = lax.all_to_all(owned, 'ep', split_axis=0, concat_axis=0, tiled=True)  7.39 us
    all_to_all x1, starting transfers between devices, local(): back = lax.all_to_all(back, 'ep', split_axis=0, concat_axis=0, tiled=True)  6.46 us
  transfers between devices with their start and end apart: 19, of which 13 were waited for; matrix products, arithmetic and copies ran while one was open for 4% of the time, Pallas kernels for 3%

profile of v5, /device:TPU:8, one launch (start us, length us, event | category | flops | bytes accessed | tf_op | source)
XLA Modules:
  0.0 183.2 jit_solution(6559777560237371070)
XLA Ops:
  0.6 4.9 %pack.1 = (bf16[256,5248]{1,0:T(8,128)(2,1)}, s32[8,128]{1,0:T(8,128)}) custom-call(s32[1]{0:T(128)} %bitcast.z, s32[1]{0:T(128)} %bitcast.1.core, s32[2,128]{1,0:T(2,128)} %bitcast.17, bf16[2,128]{1,0:T(2,128)(2,1)} %bitcast.18, s32[1,32]{1,0:T(1,128)} %bitcast.13, s32[16,32]{1,0:T(8,128)} %failed.1, bf16[128,2048]{1,0:T(8,128)(2,1)} %tokens_in.1, ...), custom_call_target="tpu_custom_call" | custom-call | tf_op jit(solution)/shard_map/pack/pallas_call | solution.py:313
  5.6 10.4 %all-to-all-start = ((bf16[32,8,5248]{2,1,0:T(8,128)(2,1)}), bf16[32,8,5248]{2,1,0:T(8,128)(2,1)}, u32[]{:S(2)}, u32[]{:S(2)}) async-start(bf16[32,8,5248]{2,1,0:T(8,128)(2,1)} %bitcast.14), calls=%async_computation | async-start | bytes 5373952 | tf_op jit(solution)/shard_map/all_to_all | solution.py:340
  16.0 4.2 %collective-permute-start = (bf16[128,1536]{1,0:T(8,128)(2,1)S(1)}, bf16[128,1536]{1,0:T(8,128)(2,1)S(1)}, u32[]{:S(2)}, u32[]{:S(2)}) collective-permute-start(bf16[128,1536]{1,0:T(8,128)(2,1)S(1)} %pad_maximum_fusion.refs_4_), channel_id=1, source_target_pairs={{0,64},{32,480},{64,128},{96,32},{128,192},{160,96},{192,256},{224... | collective-permute-start | bytes 1179656 | tf_op jit(solution)/shard_map/ppermute | solution.py:290
  20.3 8.6 %collective-permute-start.3 = (bf16[128,1536]{1,0:T(8,128)(2,1)S(1)}, bf16[128,1536]{1,0:T(8,128)(2,1)S(1)}, u32[]{:S(2)}, u32[]{:S(2)}) collective-permute-start(bf16[128,1536]{1,0:T(8,128)(2,1)S(1)} %pad_maximum_fusion.refs_4_), channel_id=1, source_target_pairs={{0,448},{32,96},{64,0},{96,160},{128,64},{160,224},{192,128},{224,... | collective-permute-start | bytes 1179656 | tf_op jit(solution)/shard_map/ppermute | solution.py:290
  28.9 4.8 %collective-permute-done.refs_1_.refs_2_ = bf16[128,1536]{1,0:T(8,128)(2,1)S(1)} collective-permute-done((bf16[128,1536]{1,0:T(8,128)(2,1)S(1)}, bf16[128,1536]{1,0:T(8,128)(2,1)S(1)}, u32[]{:S(2)}, u32[]{:S(2)}) %collective-permute-start) | collective-permute-done | bytes 393248 | tf_op jit(solution)/shard_map/ppermute | solution.py:290
  33.7 2.0 %collective-permute-start.1 = (bf16[128,1536]{1,0:T(8,128)(2,1)S(1)}, bf16[128,1536]{1,0:T(8,128)(2,1)S(1)}, u32[]{:S(2)}, u32[]{:S(2)}) collective-permute-start(bf16[128,1536]{1,0:T(8,128)(2,1)S(1)} %collective-permute-done.refs_1_.refs_2_), channel_id=1, source_target_pairs={{0,128},{32,416},{64,192},{96,480},{128,256},{160,32},{192,320},{2... | collective-permute-start | bytes 1179656 | tf_op jit(solution)/shard_map/ppermute | solution.py:290
  35.7 6.6 %collective-permute-start.4 = (bf16[128,1536]{1,0:T(8,128)(2,1)S(1)}, bf16[128,1536]{1,0:T(8,128)(2,1)S(1)}, u32[]{:S(2)}, u32[]{:S(2)}) collective-permute-start(bf16[128,1536]{1,0:T(8,128)(2,1)S(1)} %collective-permute-done.3.refs_3_), channel_id=1, source_target_pairs={{0,448},{32,96},{64,0},{96,160},{128,64},{160,224},{192,128},{224,... | collective-permute-start | bytes 1179656 | tf_op jit(solution)/shard_map/ppermute | solution.py:290
  42.3 9.1 %collective-permute-done.1.refs_0_ = bf16[128,1536]{1,0:T(8,128)(2,1)S(1)} collective-permute-done((bf16[128,1536]{1,0:T(8,128)(2,1)S(1)}, bf16[128,1536]{1,0:T(8,128)(2,1)S(1)}, u32[]{:S(2)}, u32[]{:S(2)}) %collective-permute-start.1) | collective-permute-done | bytes 393248 | tf_op jit(solution)/shard_map/ppermute | solution.py:290
  51.5 6.3 %collective-permute-start.2 = (bf16[256,1536]{1,0:T(8,128)(2,1)S(1)}, bf16[256,1536]{1,0:T(8,128)(2,1)S(1)}, u32[]{:S(2)}, u32[]{:S(2)}) collective-permute-start(bf16[256,1536]{1,0:T(8,128)(2,1)S(1)} %stack.3), channel_id=1, source_target_pairs={{0,64},{32,480},{64,128},{96,32},{128,192},{160,96},{192,256},{224... | collective-permute-start | bytes 2359304 | tf_op jit(solution)/shard_map/ppermute | solution.py:290
  58.0 1.9 %collective-permute-start.7 = (bf16[640,1536]{1,0:T(8,128)(2,1)S(1)}, bf16[640,1536]{1,0:T(8,128)(2,1)S(1)}, u32[]{:S(2)}, u32[]{:S(2)}) collective-permute-start(bf16[640,1536]{1,0:T(8,128)(2,1)S(1)} %stack.5.w1), channel_id=1, source_target_pairs={{0,32},{32,0},{1,33},{33,1},{2,34},{34,2},{3,35},{35,3},{4,36},{36... | collective-permute-start | bytes 5898248 | tf_op jit(solution)/shard_map/ppermute | solution.py:294
  60.0 2.2 %collective-permute-start.5 = (bf16[128,1536]{1,0:T(8,128)(2,1)S(1)}, bf16[128,1536]{1,0:T(8,128)(2,1)S(1)}, u32[]{:S(2)}, u32[]{:S(2)}) collective-permute-start(bf16[128,1536]{1,0:T(8,128)(2,1)S(1)} %collective-permute-done.4.refs_1_), channel_id=1, source_target_pairs={{0,448},{32,96},{64,0},{96,160},{128,64},{160,224},{192,128},{224,... | collective-permute-start | bytes 1179656 | tf_op jit(solution)/shard_map/ppermute | solution.py:290
  62.2 7.4 %collective-permute-done.5.refs_1_ = bf16[128,1536]{1,0:T(8,128)(2,1)S(1)} collective-permute-done((bf16[128,1536]{1,0:T(8,128)(2,1)S(1)}, bf16[128,1536]{1,0:T(8,128)(2,1)S(1)}, u32[]{:S(2)}, u32[]{:S(2)}) %collective-permute-start.5) | collective-permute-done | bytes 393248 | tf_op jit(solution)/shard_map/ppermute | solution.py:290
  69.6 2.0 %collective-permute-done.2.refs_0_ = bf16[256,1536]{1,0:T(8,128)(2,1)S(1)} collective-permute-done((bf16[256,1536]{1,0:T(8,128)(2,1)S(1)}, bf16[256,1536]{1,0:T(8,128)(2,1)S(1)}, u32[]{:S(2)}, u32[]{:S(2)}) %collective-permute-start.2) | collective-permute-done | bytes 786464 | tf_op jit(solution)/shard_map/ppermute | solution.py:290
  71.7 2.9 %collective-permute-start.6 = (bf16[384,1536]{1,0:T(8,128)(2,1)S(1)}, bf16[384,1536]{1,0:T(8,128)(2,1)S(1)}, u32[]{:S(2)}, u32[]{:S(2)}) collective-permute-start(bf16[384,1536]{1,0:T(8,128)(2,1)S(1)} %stack.4.w0), channel_id=1, source_target_pairs={{0,32},{32,0},{1,33},{33,1},{2,34},{34,2},{3,35},{35,3},{4,36},{36... | collective-permute-start | bytes 3538952 | tf_op jit(solution)/shard_map/ppermute | solution.py:294
  74.6 2.5 %collective-permute-done.6.w2 = bf16[384,1536]{1,0:T(8,128)(2,1)S(1)} collective-permute-done((bf16[384,1536]{1,0:T(8,128)(2,1)S(1)}, bf16[384,1536]{1,0:T(8,128)(2,1)S(1)}, u32[]{:S(2)}, u32[]{:S(2)}) %collective-permute-start.6) | collective-permute-done | bytes 1179680 | tf_op jit(solution)/shard_map/ppermute | solution.py:294
  82.3 8.1 %slot.1 = (bf16[1024,1536]{1,0:T(8,128)(2,1)S(1)}, bf16[384,1536]{1,0:T(8,128)(2,1)S(1)}, bf16[640,1536]{1,0:T(8,128)(2,1)}, bf16[320,1024]{1,0:T(8,128)(2,1)S(1)}, bf16[320,128]{1,0:T(8,128)(2,1)S(1)}) custom-call(bf16[256,5248]{1,0:T(8,128)(2,1)} %bitcast.6.got_in, bf16[384,1536]{1,0:T(8,128)(2,1)S(1)} %stack.4.w0, bf16[640,1536]{1,0:T(8,128)(2,1)S(1)} %stack.5.w1, ...), custom_call_target="tpu_custom_call" | custom-call | flops 6000000000 | bytes 12582912 | tf_op jit(solution)/shard_map/slot/pallas_call | solution.py:349
  90.4 2.3 %collective-permute-start.8 = (bf16[384,1536]{1,0:T(8,128)(2,1)S(1)}, bf16[384,1536]{1,0:T(8,128)(2,1)S(1)}, u32[]{:S(2)}, u32[]{:S(2)}) collective-permute-start(bf16[384,1536]{1,0:T(8,128)(2,1)S(1)} %get-tuple-element.25), channel_id=1, source_target_pairs={{0,32},{32,0},{1,33},{33,1},{2,34},{34,2},{3,35},{35,3},{4,36},{36... | collective-permute-start | bytes 3538952 | tf_op jit(solution)/shard_map/ppermute | solution.py:294
  92.7 2.0 %collective-permute-start.10 = (bf16[640,1536]{1,0:T(8,128)(2,1)}, bf16[640,1536]{1,0:T(8,128)(2,1)}, u32[]{:S(2)}, u32[]{:S(2)}) collective-permute-start(bf16[640,1536]{1,0:T(8,128)(2,1)} %get-tuple-element.28), channel_id=1, source_target_pairs={{0,32},{32,0},{1,33},{33,1},{2,34},{34,2},{3,35},{35,3},{4,36},{36... | collective-permute-start | bytes 5898248 | tf_op jit(solution)/shard_map/ppermute | solution.py:294
  97.0 9.8 %collective-permute-start.9 = (bf16[256,1536]{1,0:T(8,128)(2,1)}, bf16[256,1536]{1,0:T(8,128)(2,1)}, u32[]{:S(2)}, u32[]{:S(2)}) collective-permute-start(bf16[256,1536]{1,0:T(8,128)(2,1)} %add_convert_fusion), channel_id=1, source_target_pairs={{0,448},{32,96},{64,0},{96,160},{128,64},{160,224},{192,128},{224,... | collective-permute-start | bytes 2359304 | tf_op jit(solution)/shard_map/ppermute | solution.py:290
  106.8 2.1 %collective-permute-start.13 = (bf16[128,1536]{1,0:T(8,128)(2,1)}, bf16[128,1536]{1,0:T(8,128)(2,1)S(1)}, u32[]{:S(2)}, u32[]{:S(2)}) collective-permute-start(bf16[128,1536]{1,0:T(8,128)(2,1)} %add_convert_fusion.6), channel_id=1, source_target_pairs={{0,64},{32,480},{64,128},{96,32},{128,192},{160,96},{192,256},{224... | collective-permute-start | bytes 1179656 | tf_op jit(solution)/shard_map/ppermute | solution.py:290
  108.9 3.4 %back.1 = bf16[256,2688]{1,0:T(8,128)(2,1)} custom-call(bf16[320,1024]{1,0:T(8,128)(2,1)S(1)} %get-tuple-element.30.pre_grad, bf16[320,128]{1,0:T(8,128)(2,1)S(1)} %get-tuple-element.31.gate_grad, bf16[384,1536]{1,0:T(8,128)(2,1)S(1)} %stack.4.w0, bf16[640,1536]{1,0:T(8,128)(2,1)S(1)} %stack.5.w1, bf16[384,1536]{1,0:T(8,128)(2,1)S(1)} %copy-done.4, ...), custom_call_target="tpu_custom_call" | custom-call | tf_op jit(solution)/shard_map/back/pallas_call | solution.py:383
  112.3 6.5 %all-to-all-start.1 = ((bf16[32,8,2688]{2,1,0:T(8,128)(2,1)}), bf16[32,8,2688]{2,1,0:T(8,128)(2,1)S(1)}, u32[]{:S(2)}, u32[]{:S(2)}) async-start(bf16[32,8,2688]{2,1,0:T(8,128)(2,1)} %bitcast.9), calls=%async_computation.1 | async-start | bytes 2752512 | tf_op jit(solution)/shard_map/all_to_all | solution.py:400
  118.7 1.9 %collective-permute-done.13 = bf16[128,1536]{1,0:T(8,128)(2,1)S(1)} collective-permute-done((bf16[128,1536]{1,0:T(8,128)(2,1)}, bf16[128,1536]{1,0:T(8,128)(2,1)S(1)}, u32[]{:S(2)}, u32[]{:S(2)}) %collective-permute-start.13) | collective-permute-done | bytes 393248 | tf_op jit(solution)/shard_map/ppermute | solution.py:290
  122.6 4.4 %collective-permute-start.11 = (bf16[128,1536]{1,0:T(8,128)(2,1)S(1)}, bf16[128,1536]{1,0:T(8,128)(2,1)S(1)}, u32[]{:S(2)}, u32[]{:S(2)}) collective-permute-start(bf16[128,1536]{1,0:T(8,128)(2,1)S(1)} %get-tuple-element.39), channel_id=1, source_target_pairs={{0,384},{32,160},{64,448},{96,224},{128,0},{160,288},{192,64},{224... | collective-permute-start | bytes 1179656 | tf_op jit(solution)/shard_map/ppermute | solution.py:290
  127.0 4.6 %collective-permute-start.14 = (bf16[128,1536]{1,0:T(8,128)(2,1)S(1)}, bf16[128,1536]{1,0:T(8,128)(2,1)S(1)}, u32[]{:S(2)}, u32[]{:S(2)}) collective-permute-start(bf16[128,1536]{1,0:T(8,128)(2,1)S(1)} %get-tuple-element.40), channel_id=1, source_target_pairs={{0,64},{32,480},{64,128},{96,32},{128,192},{160,96},{192,256},{224... | collective-permute-start | bytes 1179656 | tf_op jit(solution)/shard_map/ppermute | solution.py:290
  131.6 7.5 %collective-permute-done.11 = bf16[128,1536]{1,0:T(8,128)(2,1)S(1)} collective-permute-done((bf16[128,1536]{1,0:T(8,128)(2,1)S(1)}, bf16[128,1536]{1,0:T(8,128)(2,1)S(1)}, u32[]{:S(2)}, u32[]{:S(2)}) %collective-permute-start.11) | collective-permute-done | bytes 393248 | tf_op jit(solution)/shard_map/ppermute | solution.py:290
  141.6 6.1 %collective-permute-start.12 = (bf16[128,1536]{1,0:T(8,128)(2,1)S(1)}, bf16[128,1536]{1,0:T(8,128)(2,1)S(1)}, u32[]{:S(2)}, u32[]{:S(2)}) collective-permute-start(bf16[128,1536]{1,0:T(8,128)(2,1)S(1)} %get-tuple-element.37), channel_id=1, source_target_pairs={{0,448},{32,96},{64,0},{96,160},{128,64},{160,224},{192,128},{224,... | collective-permute-start | bytes 1179656 | tf_op jit(solution)/shard_map/ppermute | solution.py:290
  147.7 1.9 %collective-permute-start.15 = (bf16[128,1536]{1,0:T(8,128)(2,1)S(1)}, bf16[128,1536]{1,0:T(8,128)(2,1)S(1)}, u32[]{:S(2)}, u32[]{:S(2)}) collective-permute-start(bf16[128,1536]{1,0:T(8,128)(2,1)S(1)} %get-tuple-element.38), channel_id=1, source_target_pairs={{0,64},{32,480},{64,128},{96,32},{128,192},{160,96},{192,256},{224... | collective-permute-start | bytes 1179656 | tf_op jit(solution)/shard_map/ppermute | solution.py:290
  149.6 6.0 %collective-permute-done.12 = bf16[128,1536]{1,0:T(8,128)(2,1)S(1)} collective-permute-done((bf16[128,1536]{1,0:T(8,128)(2,1)S(1)}, bf16[128,1536]{1,0:T(8,128)(2,1)S(1)}, u32[]{:S(2)}, u32[]{:S(2)}) %collective-permute-start.12) | collective-permute-done | bytes 393248 | tf_op jit(solution)/shard_map/ppermute | solution.py:290
  155.6 2.9 %collective-permute-done.15 = bf16[128,1536]{1,0:T(8,128)(2,1)S(1)} collective-permute-done((bf16[128,1536]{1,0:T(8,128)(2,1)S(1)}, bf16[128,1536]{1,0:T(8,128)(2,1)S(1)}, u32[]{:S(2)}, u32[]{:S(2)}) %collective-permute-start.15) | collective-permute-done | bytes 393248 | tf_op jit(solution)/shard_map/ppermute | solution.py:290
  160.7 7.4 %all-to-all-start.2 = ((bf16[32,4,1536]{2,1,0:T(4,128)(2,1)}), bf16[32,4,1536]{2,1,0:T(4,128)(2,1)S(1)}, u32[]{:S(2)}, u32[]{:S(2)}) async-start(bf16[32,4,1536]{2,1,0:T(4,128)(2,1)} %reshape.25), calls=%async_computation.2 | async-start | bytes 786432 | tf_op jit(solution)/shard_map/all_to_all | solution.py:413
  169.5 12.2 %all-to-all-done.2.mixed = bf16[32,4,1536]{2,1,0:T(4,128)(2,1)S(1)} async-done(((bf16[32,4,1536]{2,1,0:T(4,128)(2,1)}), bf16[32,4,1536]{2,1,0:T(4,128)(2,1)S(1)}, u32[]{:S(2)}, u32[]{:S(2)}) %all-to-all-start.2) | async-done | bytes 393248 | tf_op jit(solution)/shard_map/all_to_all | solution.py:413
  (39 shorter events, 17.3 us)
Async XLA Ops:
  5.5 10.4 %copy-start.7 = (bf16[1,128,1024]{2,1,0:T(8,128)(2,1)S(1)}, bf16[1,128,1024]{2,1,0:T(8,128)(2,1)}, u32[]{:S(2)}) copy-start(bf16[1,128,1024]{2,1,0:T(8,128)(2,1)} %param.12) | copy-start | bytes 786436
  5.6 10.4 %copy-start.8 = (bf16[1,128,512]{2,1,0:T(8,128)(2,1)S(1)}, bf16[1,128,512]{2,1,0:T(8,128)(2,1)}, u32[]{:S(2)}) copy-start(bf16[1,128,512]{2,1,0:T(8,128)(2,1)} %param.13) | copy-start | bytes 393220
  5.6 73.9 %all-to-all-start = ((bf16[32,8,5248]{2,1,0:T(8,128)(2,1)}), bf16[32,8,5248]{2,1,0:T(8,128)(2,1)}, u32[]{:S(2)}, u32[]{:S(2)}) async-start(bf16[32,8,5248]{2,1,0:T(8,128)(2,1)} %bitcast.14), calls=%async_computation | async-start | bytes 5373952 | tf_op jit(solution)/shard_map/all_to_all | solution.py:340
  16.0 17.6 %collective-permute-start = (bf16[128,1536]{1,0:T(8,128)(2,1)S(1)}, bf16[128,1536]{1,0:T(8,128)(2,1)S(1)}, u32[]{:S(2)}, u32[]{:S(2)}) collective-permute-start(bf16[128,1536]{1,0:T(8,128)(2,1)S(1)} %pad_maximum_fusion.refs_4_), channel_id=1, source_target_pairs={{0,64},{32,480},{64,128},{96,32},{128,192},{160,96},{192,256},{224... | collective-permute-start | bytes 1179656 | tf_op jit(solution)/shard_map/ppermute | solution.py:290
  20.3 15.4 %collective-permute-start.3 = (bf16[128,1536]{1,0:T(8,128)(2,1)S(1)}, bf16[128,1536]{1,0:T(8,128)(2,1)S(1)}, u32[]{:S(2)}, u32[]{:S(2)}) collective-permute-start(bf16[128,1536]{1,0:T(8,128)(2,1)S(1)} %pad_maximum_fusion.refs_4_), channel_id=1, source_target_pairs={{0,448},{32,96},{64,0},{96,160},{128,64},{160,224},{192,128},{224,... | collective-permute-start | bytes 1179656 | tf_op jit(solution)/shard_map/ppermute | solution.py:290
  33.7 17.8 %collective-permute-start.1 = (bf16[128,1536]{1,0:T(8,128)(2,1)S(1)}, bf16[128,1536]{1,0:T(8,128)(2,1)S(1)}, u32[]{:S(2)}, u32[]{:S(2)}) collective-permute-start(bf16[128,1536]{1,0:T(8,128)(2,1)S(1)} %collective-permute-done.refs_1_.refs_2_), channel_id=1, source_target_pairs={{0,128},{32,416},{64,192},{96,480},{128,256},{160,32},{192,320},{2... | collective-permute-start | bytes 1179656 | tf_op jit(solution)/shard_map/ppermute | solution.py:290
  35.7 22.2 %collective-permute-start.4 = (bf16[128,1536]{1,0:T(8,128)(2,1)S(1)}, bf16[128,1536]{1,0:T(8,128)(2,1)S(1)}, u32[]{:S(2)}, u32[]{:S(2)}) collective-permute-start(bf16[128,1536]{1,0:T(8,128)(2,1)S(1)} %collective-permute-done.3.refs_3_), channel_id=1, source_target_pairs={{0,448},{32,96},{64,0},{96,160},{128,64},{160,224},{192,128},{224,... | collective-permute-start | bytes 1179656 | tf_op jit(solution)/shard_map/ppermute | solution.py:290
  51.5 20.1 %collective-permute-start.2 = (bf16[256,1536]{1,0:T(8,128)(2,1)S(1)}, bf16[256,1536]{1,0:T(8,128)(2,1)S(1)}, u32[]{:S(2)}, u32[]{:S(2)}) collective-permute-start(bf16[256,1536]{1,0:T(8,128)(2,1)S(1)} %stack.3), channel_id=1, source_target_pairs={{0,64},{32,480},{64,128},{96,32},{128,192},{160,96},{192,256},{224... | collective-permute-start | bytes 2359304 | tf_op jit(solution)/shard_map/ppermute | solution.py:290
  58.0 20.1 %collective-permute-start.7 = (bf16[640,1536]{1,0:T(8,128)(2,1)S(1)}, bf16[640,1536]{1,0:T(8,128)(2,1)S(1)}, u32[]{:S(2)}, u32[]{:S(2)}) collective-permute-start(bf16[640,1536]{1,0:T(8,128)(2,1)S(1)} %stack.5.w1), channel_id=1, source_target_pairs={{0,32},{32,0},{1,33},{33,1},{2,34},{34,2},{3,35},{35,3},{4,36},{36... | collective-permute-start | bytes 5898248 | tf_op jit(solution)/shard_map/ppermute | solution.py:294
  60.0 9.7 %collective-permute-start.5 = (bf16[128,1536]{1,0:T(8,128)(2,1)S(1)}, bf16[128,1536]{1,0:T(8,128)(2,1)S(1)}, u32[]{:S(2)}, u32[]{:S(2)}) collective-permute-start(bf16[128,1536]{1,0:T(8,128)(2,1)S(1)} %collective-permute-done.4.refs_1_), channel_id=1, source_target_pairs={{0,448},{32,96},{64,0},{96,160},{128,64},{160,224},{192,128},{224,... | collective-permute-start | bytes 1179656 | tf_op jit(solution)/shard_map/ppermute | solution.py:290
  71.7 5.4 %collective-permute-start.6 = (bf16[384,1536]{1,0:T(8,128)(2,1)S(1)}, bf16[384,1536]{1,0:T(8,128)(2,1)S(1)}, u32[]{:S(2)}, u32[]{:S(2)}) collective-permute-start(bf16[384,1536]{1,0:T(8,128)(2,1)S(1)} %stack.4.w0), channel_id=1, source_target_pairs={{0,32},{32,0},{1,33},{33,1},{2,34},{34,2},{3,35},{35,3},{4,36},{36... | collective-permute-start | bytes 3538952 | tf_op jit(solution)/shard_map/ppermute | solution.py:294
  77.0 1.1 copy-start.3
  78.2 1.3 copy-start.1
  79.5 1.5 copy-start.2
  81.0 1.3 copy-start.4
  90.4 21.9 %copy-start = (bf16[1024,1536]{1,0:T(8,128)(2,1)}, bf16[1024,1536]{1,0:T(8,128)(2,1)S(1)}, u32[]{:S(2)}) copy-start(bf16[1024,1536]{1,0:T(8,128)(2,1)S(1)} %get-tuple-element.24) | copy-start | bytes 9437188
  90.4 4.7 %collective-permute-start.8 = (bf16[384,1536]{1,0:T(8,128)(2,1)S(1)}, bf16[384,1536]{1,0:T(8,128)(2,1)S(1)}, u32[]{:S(2)}, u32[]{:S(2)}) collective-permute-start(bf16[384,1536]{1,0:T(8,128)(2,1)S(1)} %get-tuple-element.25), channel_id=1, source_target_pairs={{0,32},{32,0},{1,33},{33,1},{2,34},{34,2},{3,35},{35,3},{4,36},{36... | collective-permute-start | bytes 3538952 | tf_op jit(solution)/shard_map/ppermute | solution.py:294
  92.7 28.1 %collective-permute-start.10 = (bf16[640,1536]{1,0:T(8,128)(2,1)}, bf16[640,1536]{1,0:T(8,128)(2,1)}, u32[]{:S(2)}, u32[]{:S(2)}) collective-permute-start(bf16[640,1536]{1,0:T(8,128)(2,1)} %get-tuple-element.28), channel_id=1, source_target_pairs={{0,32},{32,0},{1,33},{33,1},{2,34},{34,2},{3,35},{35,3},{4,36},{36... | collective-permute-start | bytes 5898248 | tf_op jit(solution)/shard_map/ppermute | solution.py:294
  97.0 23.8 %collective-permute-start.9 = (bf16[256,1536]{1,0:T(8,128)(2,1)}, bf16[256,1536]{1,0:T(8,128)(2,1)}, u32[]{:S(2)}, u32[]{:S(2)}) collective-permute-start(bf16[256,1536]{1,0:T(8,128)(2,1)} %add_convert_fusion), channel_id=1, source_target_pairs={{0,448},{32,96},{64,0},{96,160},{128,64},{160,224},{192,128},{224,... | collective-permute-start | bytes 2359304 | tf_op jit(solution)/shard_map/ppermute | solution.py:290
  106.8 13.8 %collective-permute-start.13 = (bf16[128,1536]{1,0:T(8,128)(2,1)}, bf16[128,1536]{1,0:T(8,128)(2,1)S(1)}, u32[]{:S(2)}, u32[]{:S(2)}) collective-permute-start(bf16[128,1536]{1,0:T(8,128)(2,1)} %add_convert_fusion.6), channel_id=1, source_target_pairs={{0,64},{32,480},{64,128},{96,32},{128,192},{160,96},{192,256},{224... | collective-permute-start | bytes 1179656 | tf_op jit(solution)/shard_map/ppermute | solution.py:290
  112.3 47.6 %all-to-all-start.1 = ((bf16[32,8,2688]{2,1,0:T(8,128)(2,1)}), bf16[32,8,2688]{2,1,0:T(8,128)(2,1)S(1)}, u32[]{:S(2)}, u32[]{:S(2)}) async-start(bf16[32,8,2688]{2,1,0:T(8,128)(2,1)} %bitcast.9), calls=%async_computation.1 | async-start | bytes 2752512 | tf_op jit(solution)/shard_map/all_to_all | solution.py:400
  122.6 16.5 %collective-permute-start.11 = (bf16[128,1536]{1,0:T(8,128)(2,1)S(1)}, bf16[128,1536]{1,0:T(8,128)(2,1)S(1)}, u32[]{:S(2)}, u32[]{:S(2)}) collective-permute-start(bf16[128,1536]{1,0:T(8,128)(2,1)S(1)} %get-tuple-element.39), channel_id=1, source_target_pairs={{0,384},{32,160},{64,448},{96,224},{128,0},{160,288},{192,64},{224... | collective-permute-start | bytes 1179656 | tf_op jit(solution)/shard_map/ppermute | solution.py:290
  127.0 12.8 %collective-permute-start.14 = (bf16[128,1536]{1,0:T(8,128)(2,1)S(1)}, bf16[128,1536]{1,0:T(8,128)(2,1)S(1)}, u32[]{:S(2)}, u32[]{:S(2)}) collective-permute-start(bf16[128,1536]{1,0:T(8,128)(2,1)S(1)} %get-tuple-element.40), channel_id=1, source_target_pairs={{0,64},{32,480},{64,128},{96,32},{128,192},{160,96},{192,256},{224... | collective-permute-start | bytes 1179656 | tf_op jit(solution)/shard_map/ppermute | solution.py:290
  141.5 26.6 %copy-start.5 = (s32[8,128]{1,0:T(8,128)S(1)}, s32[8,128]{1,0:T(8,128)}, u32[]{:S(2)}) copy-start(s32[8,128]{1,0:T(8,128)} %get-tuple-element.33.places) | copy-start | bytes 12292
  141.6 14.1 %collective-permute-start.12 = (bf16[128,1536]{1,0:T(8,128)(2,1)S(1)}, bf16[128,1536]{1,0:T(8,128)(2,1)S(1)}, u32[]{:S(2)}, u32[]{:S(2)}) collective-permute-start(bf16[128,1536]{1,0:T(8,128)(2,1)S(1)} %get-tuple-element.37), channel_id=1, source_target_pairs={{0,448},{32,96},{64,0},{96,160},{128,64},{160,224},{192,128},{224,... | collective-permute-start | bytes 1179656 | tf_op jit(solution)/shard_map/ppermute | solution.py:290
  147.7 10.9 %collective-permute-start.15 = (bf16[128,1536]{1,0:T(8,128)(2,1)S(1)}, bf16[128,1536]{1,0:T(8,128)(2,1)S(1)}, u32[]{:S(2)}, u32[]{:S(2)}) collective-permute-start(bf16[128,1536]{1,0:T(8,128)(2,1)S(1)} %get-tuple-element.38), channel_id=1, source_target_pairs={{0,64},{32,480},{64,128},{96,32},{128,192},{160,96},{192,256},{224... | collective-permute-start | bytes 1179656 | tf_op jit(solution)/shard_map/ppermute | solution.py:290
  159.9 21.9 %copy-start.6 = (s32[32]{0:T(128)S(1)}, s32[32]{0:T(128)}, u32[]{:S(2)}) copy-start(s32[32]{0:T(128)} %plan.1) | copy-start | bytes 388
  160.7 21.0 %all-to-all-start.2 = ((bf16[32,4,1536]{2,1,0:T(4,128)(2,1)}), bf16[32,4,1536]{2,1,0:T(4,128)(2,1)S(1)}, u32[]{:S(2)}, u32[]{:S(2)}) async-start(bf16[32,4,1536]{2,1,0:T(4,128)(2,1)} %reshape.25), calls=%async_computation.2 | async-start | bytes 786432 | tf_op jit(solution)/shard_map/all_to_all | solution.py:413
